TPU v7x, 128 devices: a whole 4x4x4 slice. The times are simulated.
128 devices in a mesh: dp: 8 (over x, y_lo), seq: 16 (over z, y_hi, core).
Axes of the slice: x: 4, y: 4 (y_hi: 2, y_lo: 2; y = y_hi * 2 + y_lo), z: 4, core: 2. Of those that a mesh axis runs over, the one named last changes fastest.
Arguments:
- section_input: bfloat16 [65536, 1536], P(('dp', 'seq')), parts along dimension 0, may hold values from -6 to 6
- conv_gain: float32 [1536], replicated, may hold values from 0.1 to 1.9
- conv_weight: bfloat16 [5, 1536, 1536], replicated, may hold values from -0.0625 to 0.0625
- conv_bias: float32 [1536], replicated, may hold values from -3 to 3
- attn_gain: float32 [1536], replicated, may hold values from 0.1 to 1.9
- q_weight: bfloat16 [1536, 1024], P('seq'), may hold values from -5 to 5
- kv_weight: bfloat16 [1536, 320], P('seq'), may hold values from -0.15625 to 0.15625
- o_weight: bfloat16 [1536, 1536], P('seq'), may hold values from -0.15625 to 0.15625
Outputs:
- skip: bfloat16 [32768, 1536], P(('dp', 'seq')), parts along dimension 0
- block_out: bfloat16 [32768, 1536], P(('dp', 'seq')), parts along dimension 0
There are 8 independent parts, one for each index of `dp`. A program takes and returns all parts, laid end to end along the dimension named above; an argument that names none is the same for every part. Nothing has to cross between parts.
All inputs are finite; a program needn't handle non-finite values.
Results may differ from a plain program's by a relative error of at most 0.008.
The roundings to bfloat16 on the way count: a program that leaves them out, or rounds other values in their place, can miss the bound.
Values may be sent and summed in bfloat16 or wider, within the bound.
No kernel may reach another device: no remote copies, remote signals or barrier semaphores. Data moves between devices by JAX's collectives and lax.ppermute only.
A program may use at most 192 MiB of HBM per device.

v0:
```python
import jax
import jax.numpy as jnp
from jax import lax
from jax.sharding import PartitionSpec as P

HEADS = 8
DK = 128


def padded_2(array, sides, width):
    for axis, dim in sides:
        count, length = (lax.axis_size(axis), array.shape[dim])
        up = [(i, (i + 1) % count) for i in range(count - 1)]
        down = [(j, i) for i, j in up]
        last = lax.slice_in_dim(array, length - width, length, axis=dim)
        initial = lax.slice_in_dim(array, 0, width, axis=dim)
        before = lax.ppermute(last, axis, up)
        after = lax.ppermute(initial, axis, down)
        array = jnp.concatenate([before, array, after], axis=dim)
    return array


def in_one_piece(arrays, axis, dim, along):
    ends, at = ([], 0)
    for a in arrays[:-1]:
        at += a.shape[along]
        ends.append(at)
    both = jnp.concatenate(arrays, axis=along)
    return tuple(jnp.split(lax.all_gather(both, axis, axis=dim, tiled=True), ends, axis=along))


def from_everyone(array, axis):
    count = lax.axis_size(axis)
    return lax.all_to_all(
        jnp.broadcast_to(array[None], (count, *array.shape)), axis, 0, 0, tiled=True
    )


def laid_out(parts, dim):
    parts = jnp.moveaxis(parts, 0, dim)
    lengths = parts.shape
    return parts.reshape(*lengths[:dim], lengths[dim] * lengths[dim + 1], *lengths[dim + 2 :])


def collect(array, axis, dim):
    parts = from_everyone(array, axis)
    return laid_out(parts, dim)


def rms_scale(rows, gain):
    values = rows.astype(jnp.float32)
    return values * lax.rsqrt(jnp.mean(values * values, axis=-1, keepdims=True) + 1e-06) * gain


def rotate(values, positions):
    half_size = values.shape[-1] // 2
    freqs = jnp.power(10000.0, -jnp.arange(half_size, dtype=jnp.float32) / half_size)
    angle = positions.astype(jnp.float32)[:, None] * freqs[None, :]
    if values.ndim == 3:
        angle = angle[:, None, :]
    cosine = jnp.cos(angle)
    sine = jnp.sin(angle)
    first = values[..., :half_size]
    second = values[..., half_size:]
    return jnp.concatenate(
        [first * cosine - second * sine, second * cosine + first * sine], axis=-1
    )


def activate(rows, gain):
    return jax.nn.gelu(rms_scale(rows, gain), approximate=True).astype(jnp.bfloat16)


def body(
    section_input, conv_gain, conv_weight, conv_bias, attn_gain, q_weight, kv_weight, o_weight
):
    pos_rows, width = section_input.shape
    tok_rows = pos_rows // 2
    taps = conv_weight.shape[0]
    reach = taps // 2
    key_size = kv_weight.shape[1] - o_weight.shape[0] // 1 * 0
    head_count = HEADS
    key_size = DK
    raw_padded = padded_2(section_input, (("seq", 0),), reach)
    padded = activate(raw_padded, conv_gain)
    conv = jnp.zeros((pos_rows, width), jnp.float32) + conv_bias
    for kernel_tap in range(taps):
        conv = conv + jnp.dot(
            padded[kernel_tap : kernel_tap + pos_rows],
            conv_weight[kernel_tap],
            preferred_element_type=jnp.float32,
        )
    summed = section_input.astype(jnp.float32) + conv
    skip = jnp.max(summed.reshape(tok_rows, 2, width), axis=1).astype(jnp.bfloat16)
    normed = rms_scale(skip, attn_gain).astype(jnp.bfloat16)
    slab_rows = in_one_piece((q_weight, kv_weight), "seq", 0, 1)
    columns = normed
    query_sums = jnp.dot(columns, slab_rows[0], preferred_element_type=jnp.float32)
    projected = jnp.dot(columns, slab_rows[1], preferred_element_type=jnp.float32)
    positions = lax.axis_index("seq") * tok_rows + jnp.arange(tok_rows, dtype=jnp.int32)
    queries = rotate(query_sums.reshape(tok_rows, head_count, key_size), positions).astype(
        jnp.bfloat16
    )
    keys = rotate(projected[:, :key_size], positions)
    key_values = jnp.concatenate([keys, projected[:, key_size:]], axis=1).astype(jnp.bfloat16)
    score_scale = key_size ** (-0.5)
    value_size = key_values.shape[1] - key_size
    slab_rows = collect(key_values, "seq", 0)
    peak_old = jnp.full((head_count, tok_rows), -1e30, jnp.float32)
    slab_keys = slab_rows[:, :key_size]
    slab_values = slab_rows[:, key_size:]
    scores = (
        jnp.einsum("thd,kd->htk", queries, slab_keys, preferred_element_type=jnp.float32)
        * score_scale
    )
    peak_new = jnp.maximum(peak_old, jnp.max(scores, axis=-1))
    weights = jnp.exp(scores - peak_new[..., None])
    total_new = jnp.sum(weights, axis=-1)
    summed_new = jnp.einsum(
        "htk,kv->htv", weights.astype(jnp.bfloat16), slab_values, preferred_element_type=jnp.float32
    )
    heads_out = summed_new / total_new[..., None]
    mixed = (
        jnp.transpose(heads_out, (1, 0, 2))
        .reshape(tok_rows, head_count * value_size)
        .astype(jnp.bfloat16)
    )
    columns = mixed
    attended = jnp.dot(
        columns,
        lax.all_gather(o_weight, "seq", axis=0, tiled=True),
        preferred_element_type=jnp.float32,
    )
    block_out = (skip.astype(jnp.float32) + attended).astype(jnp.bfloat16)
    return (skip, block_out)


def solution(mesh):
    in_specs = (
        P(("dp", "seq"), None),
        P(),
        P(),
        P(),
        P(),
        P("seq", None),
        P("seq", None),
        P("seq", None),
    )
    out_specs = (P(("dp", "seq"), None), P(("dp", "seq"), None))
    return jax.shard_map(body, mesh=mesh, in_specs=in_specs, out_specs=out_specs, check_vma=False)
```

profile of v0, /device:TPU:1, one launch (start us, length us, event | category | flops | bytes accessed | tf_op | source)
XLA Modules:
  0.0 175.9 jit_solution(2801278796043050510)
XLA Ops:
  7.2 0.0 copy-start
  7.2 0.0 all-gather.3.cloned.1.call-start
  7.2 1.8 %pad_maximum_fusion.1 = bf16[96,1344]{1,0:T(8,128)(2,1)} fusion(bf16[96,320]{1,0:T(8,128)(2,1)} %param.14, bf16[96,1024]{1,0:T(8,128)(2,1)} %param.13), kind=kLoop, calls=%fused_computation.68 | loop fusion | flops 516096 | bytes 516096 | tf_op jit(solution)/shard_map/concatenate | solution.py:28
  9.0 0.0 all-gather.3.cloned.1.call-update
  9.0 0.8 fusion.75
  9.8 6.2 %collective-permute-start = (bf16[2,1536]{1,0:T(2,128)(2,1)S(1)}, bf16[2,1536]{1,0:T(2,128)(2,1)S(1)}, u32[]{:S(2)}, u32[]{:S(2)}) collective-permute-start(bf16[2,1536]{1,0:T(2,128)(2,1)S(1)} %get-tuple-element.4), channel_id=1, source_target_pairs={{0,1},{1,2},{2,3},{3,4},{4,5},{5,6},{6,7},{7,8},{8,9},{9,10},{10,1... | collective-permute-start | bytes 18440 | tf_op jit(solution)/shard_map/ppermute | solution.py:17
  16.0 1.9 %collective-permute-start.1 = (bf16[2,1536]{1,0:T(2,128)(2,1)S(1)}, bf16[2,1536]{1,0:T(2,128)(2,1)S(1)}, u32[]{:S(2)}, u32[]{:S(2)}) collective-permute-start(bf16[2,1536]{1,0:T(2,128)(2,1)S(1)} %get-tuple-element.5), channel_id=1, source_target_pairs={{1,0},{2,1},{3,2},{4,3},{5,4},{6,5},{7,6},{8,7},{9,8},{10,9},{11,1... | collective-permute-start | bytes 18440 | tf_op jit(solution)/shard_map/ppermute | solution.py:18
  18.0 0.0 collective-permute-done
  18.0 4.5 %collective-permute-done.1 = bf16[2,1536]{1,0:T(2,128)(2,1)S(1)} collective-permute-done((bf16[2,1536]{1,0:T(2,128)(2,1)S(1)}, bf16[2,1536]{1,0:T(2,128)(2,1)S(1)}, u32[]{:S(2)}, u32[]{:S(2)}) %collective-permute-start.1) | collective-permute-done | bytes 6176 | tf_op jit(solution)/shard_map/ppermute | solution.py:18
  22.5 2.1 %fusion.38 = f32[516]{0:T(1024)S(1)} fusion(bf16[2,1536]{1,0:T(2,128)(2,1)S(1)} %collective-permute-done.1, bf16[512,1536]{1,0:T(8,128)(2,1)} %param.8, bf16[2,1536]{1,0:T(2,128)(2,1)S(1)} %collective-permute-done), kind=kLoop, calls=%fused_computation.30 | loop fusion | flops 6340092 | bytes 1587216 | tf_op jit(solution)/shard_map/reduce_sum | solution.py:52
  24.6 0.0 copy-done
  24.6 3.4 %fusion.42 = bf16[516,1536]{1,0:T(8,128)(2,1)S(1)} fusion(f32[1536]{0:T(1024)} %param.9, f32[516]{0:T(1024)S(1)} %add_rsqrt_fusion, bf16[2,1536]{1,0:T(2,128)(2,1)S(1)} %collective-permute-done.1, bf16[512,1536]{1,0:T(8,128)(2,1)S(1)} %copy-done, bf16[2,1536]{1,0:T(2,128)(2,1)S(1)} %collective-permute-done), kind=kLoop, calls=%fused_computation.34 | loop fusion | flops 13473792 | bytes 3178512 | tf_op jit(solution)/shard_map/convert_element_type | solution.py:71
  28.0 4.5 %fusion.11 = f32[512,1536]{1,0:T(8,128)S(1)} fusion(bf16[5,1536,1536]{2,1,0:T(8,128)(2,1)} %param.10, bf16[516,1536]{1,0:T(8,128)(2,1)S(1)} %fusion.42), kind=kOutput, calls=%fused_computation.13 | convolution fusion | flops 2415919104 | bytes 9437184 | tf_op jit(solution)/shard_map/dot_general | solution.py:88
  32.5 4.5 %fusion.9 = f32[512,1536]{1,0:T(8,128)S(1)} fusion(bf16[5,1536,1536]{2,1,0:T(8,128)(2,1)} %param.10, bf16[516,1536]{1,0:T(8,128)(2,1)S(1)} %fusion.42), kind=kOutput, calls=%fused_computation.11 | convolution fusion | flops 2415919104 | bytes 9437184 | tf_op jit(solution)/shard_map/dot_general | solution.py:88
  37.0 4.5 %fusion.7 = f32[512,1536]{1,0:T(8,128)S(1)} fusion(bf16[5,1536,1536]{2,1,0:T(8,128)(2,1)} %param.10, bf16[516,1536]{1,0:T(8,128)(2,1)S(1)} %fusion.42), kind=kOutput, calls=%fused_computation.9 | convolution fusion | flops 2415919104 | bytes 9437184 | tf_op jit(solution)/shard_map/dot_general | solution.py:88
  41.5 0.0 copy-start.4
  41.5 4.5 %fusion.5 = f32[512,1536]{1,0:T(8,128)S(1)} fusion(bf16[5,1536,1536]{2,1,0:T(8,128)(2,1)} %param.10, bf16[516,1536]{1,0:T(8,128)(2,1)S(1)} %fusion.42), kind=kOutput, calls=%fused_computation.7 | convolution fusion | flops 2415919104 | bytes 9437184 | tf_op jit(solution)/shard_map/dot_general | solution.py:88
  46.0 0.0 copy-done.4
  46.0 5.9 %fusion.35 = bf16[512,1536]{1,0:T(8,128)(2,1)S(1)} fusion(f32[512,1536]{1,0:T(8,128)S(1)} %fusion.5, f32[512,1536]{1,0:T(8,128)S(1)} %fusion.7, f32[512,1536]{1,0:T(8,128)S(1)} %fusion.9, f32[512,1536]{1,0:T(8,128)S(1)} %fusion.11, bf16[5,1536,1536]{2,1,0:T(8,128)(2,1)} %param.10, bf16[512,1536]{1,0:T(8,128)(2,1)S(1)} %copy-done, ...), kind=kOutput, calls=%fused_computation.29 | convolution fusion | flops 2422210560 | bytes 22028288 | tf_op jit(solution)/shard_map/dot_general | solution.py:88
  51.9 0.0 copy-start.5
  51.9 0.8 reshape.120
  52.8 4.3 %reduce_max.18 = bf16[256,1536]{1,0:T(8,128)(2,1)S(1)} reduce(bf16[256,2,1536]{2,1,0:T(2,128)(2,1)S(1)} %reshape.120, bf16[]{:T(256)} %constant.91), dimensions={1}, to_apply=%region_1.0 | reduce | flops 393216 | bytes 2359298 | tf_op jit(solution)/shard_map/reduce_max | solution.py:94
  57.1 0.0 copy-start.2
  57.1 0.2 fusion.51
  57.3 13.5 %all-gather.3.cloned.1.call-done = bf16[1536,1344]{1,0:T(8,128)(2,1)} async-done(((bf16[96,1344]{1,0:T(8,128)(2,1)}), bf16[1536,1344]{1,0:T(8,128)(2,1)}) %all-gather.3.cloned.1.call-update) | async-done | bytes 4128784 | tf_op jit(solution)/shard_map/all_gather | solution.py:29
  70.8 0.0 copy-done.5
  70.8 1.9 %fusion.65 = f32[256,320]{0,1:T(8,128)S(1)} fusion(bf16[1536,1344]{1,0:T(8,128)(2,1)} %all-gather.3.cloned.1.call-done, bf16[256,1536]{1,0:T(8,128)(2,1)S(1)} %reduce_max.18, f32[1536]{0:T(1024)S(1)} %copy-done.5, f32[256]{0:T(256)S(1)} %add_rsqrt_fusion.1), kind=kOutput, calls=%fused_computation.59 | convolution fusion | flops 253231104 | bytes 2300928 | tf_op jit(solution)/shard_map/dot_general | solution.py:99
  72.7 1.0 multiply_cosine_fusion
  73.7 1.8 %broadcast_in_dim.4 = bf16[16,256,320]{1,2,0:T(8,128)(2,1)} broadcast(bf16[256,320]{0,1:T(8,128)(2,1)S(1)} %pad_maximum_fusion.2), dimensions={1,2} | broadcast | bytes 2785280 | tf_op jit(solution)/shard_map/broadcast_in_dim | solution.py:35
  75.5 3.8 %all-to-all-start = ((bf16[16,256,320]{1,2,0:T(8,128)(2,1)}), bf16[16,256,320]{1,2,0:T(8,128)(2,1)S(1)}, u32[]{:S(2)}, u32[]{:S(2)}) async-start(bf16[16,256,320]{1,2,0:T(8,128)(2,1)} %broadcast_in_dim.4), calls=%async_computation | async-start | bytes 5242880 | tf_op jit(solution)/shard_map/all_to_all | solution.py:34
  79.3 0.0 all-gather.5.cloned.1.call-start
  79.3 0.7 all-gather.5.cloned.1.call-update
  80.0 2.9 %fusion.62 = f32[32,8,8,128]{3,1,2,0:T(8,128)S(1)} fusion(bf16[1536,1344]{1,0:T(8,128)(2,1)} %all-gather.3.cloned.1.call-done, bf16[256,1536]{1,0:T(8,128)(2,1)S(1)} %reduce_max.18, f32[1536]{0:T(1024)S(1)} %copy-done.5, f32[256]{0:T(256)S(1)} %add_rsqrt_fusion.1), kind=kOutput, calls=%fused_computation.58 | convolution fusion | flops 806879232 | bytes 4987904 | tf_op jit(solution)/shard_map/dot_general | solution.py:98
  82.9 1.2 copy.29
  84.1 0.9 copy.19
  85.0 1.6 copy.21
  86.6 1.9 %fusion.76 = (f32[256,8,64]{2,1,0:T(8,128)S(1)}, f32[256,8,64]{2,1,0:T(8,128)S(1)}) fusion(f32[256,8,128]{2,1,0:T(8,128)} %bitcast.61), kind=kLoop, calls=%fused_computation.83 | loop fusion | bytes 2097152 | tf_op jit(solution)/shard_map/slice | solution.py:63
  88.5 0.0 copy-done.3
  88.6 1.4 subtract_convert_fusion
  90.0 26.6 %all-to-all-done = bf16[16,256,320]{1,2,0:T(8,128)(2,1)S(1)} async-done(((bf16[16,256,320]{1,2,0:T(8,128)(2,1)}), bf16[16,256,320]{1,2,0:T(8,128)(2,1)S(1)}, u32[]{:S(2)}, u32[]{:S(2)}) %all-to-all-start) | async-done | bytes 2621472 | tf_op jit(solution)/shard_map/all_to_all | solution.py:34
  116.6 2.8 %copy.17 = bf16[16,256,320]{2,1,0:T(8,128)(2,1)} copy(bf16[16,256,320]{1,2,0:T(8,128)(2,1)S(1)} %all-to-all-done) | data formatting | bytes 5242880 | tf_op jit(solution)/shard_map/all_to_all | solution.py:34
  119.4 17.3 %bitcast_reduce_fusion = (f32[8,256]{1,0:T(8,128)S(1)}, f32[4096,256,8]{1,0,2:T(8,128)}) fusion(bf16[256,8,64]{2,0,1:T(8,128)(2,1)} %get-tuple-element.3, bf16[256,8,64]{2,0,1:T(8,128)(2,1)} %get-tuple-element.2, bf16[4096,320]{1,0:T(8,128)(2,1)} %bitcast.62), kind=kOutput, calls=%fused_computation.1 | convolution fusion | flops 2165307392 | bytes 35659776 | tf_op jit(solution)/shard_map/thd,kd->htk/dot_general | solution.py:113
  136.7 14.3 %fusion.1 = f32[8,256]{1,0:T(8,128)S(1)} fusion(f32[4096,256,8]{1,0,2:T(8,128)} %get-tuple-element.15, f32[8,256]{1,0:T(8,128)S(1)} %broadcast_maximum_fusion), kind=kLoop, calls=%fused_computation.3 | loop fusion | flops 25163776 | bytes 33570816 | tf_op jit(solution)/shard_map/reduce_sum | solution.py:118
  151.0 0.0 copy-done.1
  151.0 13.4 %fusion.59 = bf16[256,8,192]{0,2,1:T(8,128)(2,1)S(1)} fusion(bf16[4096,320]{1,0:T(8,128)(2,1)S(1)} %bitcast.63, f32[4096,256,8]{1,0,2:T(8,128)} %get-tuple-element.15, f32[8,256]{1,0:T(8,128)S(1)} %broadcast_maximum_fusion, f32[256,8]{0,1:T(8,128)S(1)} %bitcast.64), kind=kOutput, calls=%fused_computation.57 | convolution fusion | flops 3247177728 | bytes 36454400 | tf_op jit(solution)/shard_map/htk,kv->htv/dot_general | solution.py:119
  164.4 0.0 all-gather.5.cloned.1.call-done
  164.4 0.0 copy-done.2
  164.5 4.6 %fusion.50 = bf16[256,1536]{1,0:T(8,128)(2,1)} fusion(bf16[256,1536]{0,1:T(8,128)(2,1)S(1)} %bitcast.65, bf16[1536,1536]{1,0:T(8,128)(2,1)} %all-gather.5.cloned.1.call-done, bf16[256,1536]{1,0:T(8,128)(2,1)S(1)} %reduce_max.18), kind=kOutput, calls=%fused_computation.43 | convolution fusion | flops 1209139200 | bytes 7077888 | tf_op jit(solution)/shard_map/dot_general | solution.py:129
  (9 shorter events, 0.1 us)
Async XLA Ops:
  7.2 17.4 %copy-start = (bf16[512,1536]{1,0:T(8,128)(2,1)S(1)}, bf16[512,1536]{1,0:T(8,128)(2,1)}, u32[]{:S(2)}) copy-start(bf16[512,1536]{1,0:T(8,128)(2,1)} %param.8) | copy-start | bytes 4718596
  7.2 63.6 %all-gather.3.cloned.1.call-start = ((), (), s32[]{:S(2)}) async-start(), calls=%async_computation.1 | async-start | bytes 4595712 | tf_op jit(solution)/shard_map/all_gather | solution.py:29
  9.8 8.2 %collective-permute-start = (bf16[2,1536]{1,0:T(2,128)(2,1)S(1)}, bf16[2,1536]{1,0:T(2,128)(2,1)S(1)}, u32[]{:S(2)}, u32[]{:S(2)}) collective-permute-start(bf16[2,1536]{1,0:T(2,128)(2,1)S(1)} %get-tuple-element.4), channel_id=1, source_target_pairs={{0,1},{1,2},{2,3},{3,4},{4,5},{5,6},{6,7},{7,8},{8,9},{9,10},{10,1... | collective-permute-start | bytes 18440 | tf_op jit(solution)/shard_map/ppermute | solution.py:17
  16.0 6.5 %collective-permute-start.1 = (bf16[2,1536]{1,0:T(2,128)(2,1)S(1)}, bf16[2,1536]{1,0:T(2,128)(2,1)S(1)}, u32[]{:S(2)}, u32[]{:S(2)}) collective-permute-start(bf16[2,1536]{1,0:T(2,128)(2,1)S(1)} %get-tuple-element.5), channel_id=1, source_target_pairs={{1,0},{2,1},{3,2},{4,3},{5,4},{6,5},{7,6},{8,7},{9,8},{10,9},{11,1... | collective-permute-start | bytes 18440 | tf_op jit(solution)/shard_map/ppermute | solution.py:18
  41.5 4.5 %copy-start.4 = (f32[1536]{0:T(1024)S(1)}, f32[1536]{0:T(1024)}, u32[]{:S(2)}) copy-start(f32[1536]{0:T(1024)} %param.11) | copy-start | bytes 18436
  51.9 18.9 %copy-start.5 = (f32[1536]{0:T(1024)S(1)}, f32[1536]{0:T(1024)}, u32[]{:S(2)}) copy-start(f32[1536]{0:T(1024)} %param.12) | copy-start | bytes 18436
  57.1 107.4 %copy-start.2 = (bf16[256,1536]{1,0:T(8,128)(2,1)}, bf16[256,1536]{1,0:T(8,128)(2,1)S(1)}, u32[]{:S(2)}) copy-start(bf16[256,1536]{1,0:T(8,128)(2,1)S(1)} %reduce_max.18) | copy-start | bytes 2359300
  75.5 41.1 %all-to-all-start = ((bf16[16,256,320]{1,2,0:T(8,128)(2,1)}), bf16[16,256,320]{1,2,0:T(8,128)(2,1)S(1)}, u32[]{:S(2)}, u32[]{:S(2)}) async-start(bf16[16,256,320]{1,2,0:T(8,128)(2,1)} %broadcast_in_dim.4), calls=%async_computation | async-start | bytes 5242880 | tf_op jit(solution)/shard_map/all_to_all | solution.py:34
  79.3 85.2 %all-gather.5.cloned.1.call-start = ((), (), s32[]{:S(2)}) async-start(), calls=%async_computation.2 | async-start | bytes 5013504 | tf_op jit(solution)/shard_map/all_gather | solution.py:131
  86.6 1.9 %copy-start.3 = (f32[256,64]{1,0:T(8,128)S(1)}, f32[256,64]{1,0:T(8,128)}, u32[]{:S(2)}) copy-start(f32[256,64]{1,0:T(8,128)} %copy.21) | copy-start | bytes 196612
  136.7 14.3 %copy-start.1 = (bf16[16,256,320]{2,1,0:T(8,128)(2,1)S(1)}, bf16[16,256,320]{2,1,0:T(8,128)(2,1)}, u32[]{:S(2)}) copy-start(bf16[16,256,320]{2,1,0:T(8,128)(2,1)} %copy.17) | copy-start | bytes 7864324
Sparse Core Ops, SparseCore 0:
  11.0 59.6 all-gather.2
  82.6 68.0 all-gather.4
where the time goes:
time: 177 us; the launch traced here: 176 us
  matrix products  64 us (36%)
  waiting for transfers between devices  45.3 us (26%)
  other arithmetic  28.6 us (16%)
  between operations  14.3 us (8%)
  starting transfers between devices  12 us (7%)
  local copies, waits for them, and re-layouts  11.8 us (7%)
    all_to_all x1, waiting for transfers between devices, from_everyone(): lax.all_to_all(jnp.broadcast_to(array[None], (count, *array.shape)), axis...  26.6 us
    dot_general x5, matrix products, body(): jnp.dot(padded[kernel_tap:kernel_tap + pos_rows], conv_weight[kernel_tap]...  23.9 us
    dot_general x1, matrix products, body(): jnp.einsum('thd,kd->htk', queries, slab_keys, preferred_element_type=jnp....  17.3 us
    reduce_sum x1, other arithmetic, body(): total_new = jnp.sum(weights, axis=-1)  14.3 us
    all_gather x1, waiting for transfers between devices, in_one_piece(): lax.all_gather(both, axis, axis=dim, tiled=True)  13.5 us
    dot_general x1, matrix products, body(): jnp.einsum('htk,kv->htv', weights.astype(jnp.bfloat16), slab_values, pref...  13.4 us
    ppermute x1, starting transfers between devices, padded_2(): before = lax.ppermute(last, axis, up)  6.21 us
    dot_general x1, matrix products, body(): jnp.dot(columns, lax.all_gather(o_weight, 'seq', axis=0, tiled=True), pre...  4.62 us
  transfers between devices with their start and end apart: 5, of which 3 were waited for; matrix products, arithmetic and copies ran while one was open for 53% of the time, Pallas kernels for 0%

commit v1 on v0

v1 whole, which is shorter than its diff:
```python
import functools
import math

import jax
import jax.numpy as jnp
from jax import lax
from jax.experimental import pallas as pl
from jax.experimental.pallas import tpu as pltpu
from jax.sharding import PartitionSpec as P

HEADS = 8
DK = 128
DV = 192
EPS = 1e-06
BF = jnp.bfloat16
F32 = jnp.float32
AXES = ("dp", "seq")
VMEM_LIMIT = 60 * 1024 * 1024


def place(l):
    dp, s = divmod(l, 16)
    return dp // 2, dp % 2, s // 4, (s // 2) % 2, s % 2


def device(x, yl, z, yh, c):
    return ((x % 4) * 2 + yl) * 16 + (z % 4) * 4 + yh * 2 + c


def moves(f):
    return [(l, device(*f(*place(l)))) for l in range(128)]


def along_z(k):
    return moves(lambda x, yl, z, yh, c: (x, yl, z + k, yh, c))


def along_x(k):
    return moves(lambda x, yl, z, yh, c: (x + k, yl, z, yh, c))


OTHER_Y = moves(lambda x, yl, z, yh, c: (x, yl, z, 1 - yh, c))
NEAR_Y = moves(lambda x, yl, z, yh, c: (x, 1 - yl, z, 1 - yh, c))
OTHER_CORE = moves(lambda x, yl, z, yh, c: (x, yl, z, yh, 1 - c))


def send(array, pairs):
    return lax.ppermute(array, AXES, pairs)


def full(shape):
    return pl.BlockSpec(shape, lambda *_: (0,) * len(shape))


def gelu(v):
    return jax.nn.gelu(v, approximate=True)


def activate_kernel(x_ref, gain_ref, act_ref, raw_ref, act_s, raw_s):
    groups, rows, lanes = act_s.shape

    def step(i, _):
        at = pl.multiple_of(i * rows, rows)
        half = pl.ds(pl.multiple_of(i * (rows // 2), rows // 2), rows // 2)
        v = x_ref[pl.ds(at, rows), :].astype(F32)
        scale = lax.rsqrt(jnp.mean(v * v, axis=-1, keepdims=True) + EPS)
        g = gelu(v * scale * gain_ref[...])
        for k in range(groups):
            cols = slice(k * lanes, (k + 1) * lanes)
            raw_s[k] = v[:, cols]
            act_s[k] = g[:, cols]
            for j in range(2):
                act_ref[j, half, cols] = act_s[k, pl.ds(j, rows // 2, 2), :].astype(BF)
                raw_ref[j, half, cols] = raw_s[k, pl.ds(j, rows // 2, 2), :].astype(BF)
        return 0

    lax.fori_loop(0, x_ref.shape[0] // rows, step, 0)


def activate(x, gain):
    rows, width = x.shape
    out = jax.ShapeDtypeStruct((2, rows // 2, width), BF)
    return pl.pallas_call(
        activate_kernel,
        out_shape=(out, out),
        scratch_shapes=[pltpu.VMEM((width // 128, 64, 128), F32)] * 2,
        compiler_params=pltpu.CompilerParams(vmem_limit_bytes=VMEM_LIMIT),
        name="activate",
    )(x, gain[None])


def conv_kernel(
    taps, act_ref, raw_ref, before_ref, after_ref, cg_ref, b_ref, ag_ref, w_ref,
    skip_ref, norm_ref, lhs, wide,
):
    n = pl.program_id(0)
    rows, width = skip_ref.shape
    tile = w_ref.shape[2]

    @pl.when(n == 0)
    def _():
        def halo(ref):
            v = ref[...].astype(F32)
            return gelu(v * lax.rsqrt(jnp.mean(v * v, axis=-1, keepdims=True) + EPS) * cg_ref[...])

        before, after = halo(before_ref), halo(after_ref)
        for j in range(2):
            lhs[2 + j] = act_ref[j]
            wide[pl.ds(8, rows), :] = act_ref[j].astype(F32)
            wide[7:8, :] = before[j : j + 1]
            wide[rows + 8 : rows + 9, :] = after[j : j + 1]
            lhs[j] = wide[pl.ds(7, rows), :].astype(BF)
            lhs[4 + j] = wide[pl.ds(9, rows), :].astype(BF)

    acc = jnp.zeros((2 * rows, tile), F32)
    for t in range(taps):
        acc = acc + jnp.dot(
            lhs[t : t + 2].reshape(2 * rows, width), w_ref[t], preferred_element_type=F32
        )
    cols = pl.ds(pl.multiple_of(n * tile, tile), tile)
    bias = b_ref[:, cols]
    even = raw_ref[0, :, cols].astype(F32) + (acc[:rows] + bias)
    odd = raw_ref[1, :, cols].astype(F32) + (acc[rows:] + bias)
    skip_ref[:, cols] = jnp.maximum(even, odd).astype(BF)

    @pl.when(n == pl.num_programs(0) - 1)
    def _():
        v = skip_ref[...].astype(F32)
        scale = lax.rsqrt(jnp.mean(v * v, axis=-1, keepdims=True) + EPS)
        norm_ref[...] = (v * scale * ag_ref[...]).astype(BF)


def convolve(act, raw, before, after, conv_gain, conv_weight, conv_bias, attn_gain):
    _, rows, width = act.shape
    taps = conv_weight.shape[0]
    tile = 256
    out = jax.ShapeDtypeStruct((rows, width), BF)
    return pl.pallas_call(
        functools.partial(conv_kernel, taps),
        out_shape=(out, out),
        grid=(width // tile,),
        in_specs=[
            full((2, rows, width)),
            full((2, rows, width)),
            full((2, width)),
            full((2, width)),
            full((1, width)),
            full((1, width)),
            full((1, width)),
            pl.BlockSpec((taps, width, tile), lambda n: (0, 0, n)),
        ],
        out_specs=(full((rows, width)), full((rows, width))),
        scratch_shapes=[
            pltpu.VMEM((6, rows, width), BF),
            pltpu.VMEM((rows + 16, width), F32),
        ],
        compiler_params=pltpu.CompilerParams(vmem_limit_bytes=VMEM_LIMIT),
        name="conv",
    )(act, raw, before, after, conv_gain[None], conv_bias[None], attn_gain[None], conv_weight)


def gather_weight(shard, yh):
    other = send(shard, NEAR_Y)
    pair = jnp.where(
        yh == 0, jnp.concatenate([shard, other], 0), jnp.concatenate([other, shard], 0)
    )
    pieces = [pair, send(pair, along_z(1)), send(pair, along_z(-1)), send(pair, along_z(2))]
    return pieces + [send(p, OTHER_CORE) for p in pieces]


STEPS = (0, -1, 1, 2)


def weight_copies(where_ref, pieces, buf, sems):
    out = []
    each = pieces[0].shape[0] // 2
    for i, piece in enumerate(pieces):
        z = lax.rem(where_ref[0] + STEPS[i % 4] + 4, 4)
        core = where_ref[1] if i < 4 else 1 - where_ref[1]
        for yh in range(2):
            row = pl.multiple_of((z * 4 + yh * 2 + core) * each, each)
            out.append(
                pltpu.make_async_copy(
                    piece.at[pl.ds(yh * each, each), :],
                    buf.at[pl.ds(row, each), :],
                    sems.at[2 * i + yh],
                )
            )
    return out


def rotated(v, c, s):
    return v * c + pltpu.roll(v, DK // 2, 1) * s


def project_kernel(where_ref, norm_ref, cos_ref, sin_ref, *rest):
    pieces, (q_ref, kv_ref, buf, sems) = rest[:8], rest[8:]
    copies = weight_copies(where_ref, pieces, buf, sems)
    for c in copies:
        c.start()
    for c in copies:
        c.wait()
    x = norm_ref[...]
    rows = x.shape[0]
    kv = jnp.dot(x, buf[:, HEADS * DK :], preferred_element_type=F32)
    c, s = cos_ref[...], sin_ref[...]
    kv_ref[pl.ds(0, rows), :] = rotated(kv[:, :DK], c, s).astype(BF)
    kv_ref[pl.ds(rows, rows), :] = kv[:, DK : 2 * DK].astype(BF)
    tail = kv[:, 2 * DK :]
    kv_ref[pl.ds(2 * rows, rows // 2), :] = jnp.concatenate(
        [tail[: rows // 2], tail[rows // 2 :]], axis=1
    ).astype(BF)
    for h in range(HEADS):
        q = jnp.dot(x, buf[:, h * DK : (h + 1) * DK], preferred_element_type=F32)
        q_ref[h] = rotated(q, c, s).astype(BF)


def project(where, normed, cosine, sine, pieces):
    rows, width = normed.shape
    cols = pieces[0].shape[1]
    vm = pl.BlockSpec(memory_space=pltpu.VMEM)
    return pl.pallas_call(
        project_kernel,
        out_shape=(
            jax.ShapeDtypeStruct((HEADS, rows, DK), BF),
            jax.ShapeDtypeStruct((rows * 5 // 2, DK), BF),
        ),
        in_specs=[pl.BlockSpec(memory_space=pltpu.SMEM), vm, vm, vm]
        + [pl.BlockSpec(memory_space=pl.ANY)] * 8,
        scratch_shapes=[pltpu.VMEM((width, cols), BF), pltpu.SemaphoreType.DMA((16,))],
        compiler_params=pltpu.CompilerParams(vmem_limit_bytes=VMEM_LIMIT),
        name="project",
    )(where, normed, cosine, sine, *pieces)


def attention_kernel(counts, q_ref, *rest):
    parts = rest[: len(counts)]
    out_ref, kbuf, vbuf, tails, scores, peak, acc, sems = rest[len(counts) :]
    rows = q_ref.shape[1]
    copies = []
    p = 0
    for part, count in zip(parts, counts):
        for i in range(count):
            to = pl.ds(p * rows, rows)
            for j, (lo, size, dst) in enumerate(
                (
                    (0, rows, kbuf.at[to, :]),
                    (rows, rows, vbuf.at[to, pl.ds(0, DK)]),
                    (2 * rows, rows // 2, tails.at[p]),
                )
            ):
                copies.append(
                    pltpu.make_async_copy(part.at[i, pl.ds(lo, size), :], dst, sems.at[p, j])
                )
            p += 1
    for c in copies:
        c.start()
    for c in copies:
        c.wait()
    half = rows // 2
    lane = lax.broadcasted_iota(jnp.int32, (half, DK), 1)
    rest_lanes = jnp.where(lane == DK // 2, 1.0, 0.0)

    def unpack(i, _):
        t = tails[i].astype(F32)
        at = pl.multiple_of(i * rows, rows)
        vbuf[pl.ds(at, half), DK:] = jnp.where(lane < DK // 2, t, rest_lanes).astype(BF)
        vbuf[pl.ds(at + half, half), DK:] = jnp.where(
            lane < DK // 2, pltpu.roll(t, DK // 2, 1), rest_lanes
        ).astype(BF)
        return 0

    lax.fori_loop(0, p, unpack, 0)

    tokens = p * rows
    chunk = 512
    chunks = tokens // chunk
    per = 2
    block = per * rows
    scale = DK ** (-0.5) * math.log2(math.e)

    def keys_of(kc):
        return pl.ds(pl.multiple_of(kc * chunk, chunk), chunk)

    def make_scores(tile, kc, top):
        q = q_ref[pl.ds(tile * per, per)].reshape(block, DK)
        s = lax.dot_general(
            q, kbuf[keys_of(kc), :], (((1,), (1,)), ((), ())), preferred_element_type=F32
        )
        scores[tile % 2, kc] = s
        for j in range(chunk // DK):
            top = jnp.maximum(top, s[:, j * DK : (j + 1) * DK])
        return top

    def use_scores(tile, kc):
        m = peak[...]
        s = scores[tile % 2, kc]
        w = jnp.concatenate(
            [jnp.exp2((s[:, j * DK : (j + 1) * DK] - m) * scale) for j in range(chunk // DK)],
            axis=1,
        ).astype(BF)
        acc[...] += jnp.dot(w, vbuf[keys_of(kc), :], preferred_element_type=F32)

    def spread(top):
        peak[...] = jnp.broadcast_to(jnp.max(top, axis=-1, keepdims=True), (block, DK))

    lowest = jnp.full((block, DK), -jnp.inf, F32)
    tiles = HEADS // per
    spread(lax.fori_loop(0, chunks, lambda kc, top: make_scores(0, kc, top), lowest))
    for tile in range(tiles):
        acc[...] = jnp.zeros_like(acc)
        if tile + 1 < tiles:

            def both(kc, top, tile=tile):
                top = make_scores(tile + 1, kc, top)
                use_scores(tile, kc)
                return top

            top = lax.fori_loop(0, chunks, both, lowest)
        else:

            def last(kc, _, tile=tile):
                use_scores(tile, kc)
                return 0

            lax.fori_loop(0, chunks, last, 0)
        a = acc[...]
        o = a[:, :DV] / a[:, DV : DV + 1]
        out_ref[:, tile * per * DV : (tile + 1) * per * DV] = jnp.concatenate(
            [o[:rows], o[rows:]], axis=1
        ).astype(BF)
        if tile + 1 < tiles:
            spread(top)


def attention(q, parts):
    heads, rows, _ = q.shape
    counts = tuple(p.shape[0] for p in parts)
    total = sum(counts)
    tokens = total * rows
    vm = pl.BlockSpec(memory_space=pltpu.VMEM)
    return pl.pallas_call(
        functools.partial(attention_kernel, counts),
        out_shape=jax.ShapeDtypeStruct((rows, heads * DV), BF),
        in_specs=[vm] + [pl.BlockSpec(memory_space=pl.ANY)] * len(parts),
        scratch_shapes=[
            pltpu.VMEM((tokens, DK), BF),
            pltpu.VMEM((tokens, 2 * DK), BF),
            pltpu.VMEM((total, rows // 2, DK), BF),
            pltpu.VMEM((2, tokens // 512, 2 * rows, 512), F32),
            pltpu.VMEM((2 * rows, DK), F32),
            pltpu.VMEM((2 * rows, 2 * DK), F32),
            pltpu.SemaphoreType.DMA((total, 3)),
        ],
        compiler_params=pltpu.CompilerParams(vmem_limit_bytes=VMEM_LIMIT),
        name="attention",
    )(q, *parts)


def output_kernel(where_ref, mixed_ref, skip_ref, *rest):
    pieces, (out_ref, buf, sems) = rest[:8], rest[8:]
    copies = weight_copies(where_ref, pieces, buf, sems)
    for c in copies:
        c.start()
    for c in copies:
        c.wait()
    tile = 512
    for n in range(out_ref.shape[1] // tile):
        cols = slice(n * tile, (n + 1) * tile)
        y = jnp.dot(mixed_ref[...], buf[:, cols], preferred_element_type=F32)
        out_ref[:, cols] = (skip_ref[:, cols].astype(F32) + y).astype(BF)


def output(where, mixed, skip, pieces):
    rows, width = skip.shape
    vm = pl.BlockSpec(memory_space=pltpu.VMEM)
    return pl.pallas_call(
        output_kernel,
        out_shape=jax.ShapeDtypeStruct((rows, width), BF),
        in_specs=[pl.BlockSpec(memory_space=pltpu.SMEM), vm, vm]
        + [pl.BlockSpec(memory_space=pl.ANY)] * 8,
        scratch_shapes=[pltpu.VMEM((mixed.shape[1], width), BF), pltpu.SemaphoreType.DMA((16,))],
        compiler_params=pltpu.CompilerParams(vmem_limit_bytes=VMEM_LIMIT),
        name="output",
    )(where, mixed, skip, *pieces)


def gather_kv(own):
    own = own[None]
    pair = jnp.concatenate([own, send(own, OTHER_Y)], 0)
    parts = [pair, send(pair, along_z(1)), send(pair, along_z(-1)), send(pair, along_z(2))]
    return parts + [send(p, OTHER_CORE) for p in parts]


def rotation(seq, rows):
    half = DK // 2
    freqs = jnp.power(10000.0, -jnp.arange(half, dtype=F32) / half)
    positions = seq * rows + jnp.arange(rows, dtype=jnp.int32)
    angle = positions.astype(F32)[:, None] * freqs[None, :]
    c, s = jnp.cos(angle), jnp.sin(angle)
    return jnp.concatenate([c, c], 1), jnp.concatenate([-s, s], 1)


def body(x, conv_gain, conv_weight, conv_bias, attn_gain, q_weight, kv_weight, o_weight):
    rows = x.shape[0] // 2
    seq = lax.axis_index("seq")
    where = jnp.stack([seq // 4, seq % 2]).astype(jnp.int32)
    yh = (seq // 2) % 2
    count = lax.axis_size("seq")
    up = [(i, i + 1) for i in range(count - 1)]
    down = [(j, i) for i, j in up]
    before = lax.ppermute(x[-2:], "seq", up)
    after = lax.ppermute(x[:2], "seq", down)
    qkv_pieces = gather_weight(jnp.concatenate([q_weight, kv_weight], 1), yh)
    o_pieces = gather_weight(o_weight, yh)
    act, raw = activate(x, conv_gain)
    cosine, sine = rotation(seq, rows)
    skip, normed = convolve(
        act, raw, before, after, conv_gain, conv_weight, conv_bias, attn_gain
    )
    q, kv = project(where, normed, cosine, sine, qkv_pieces)
    mixed = attention(q, gather_kv(kv))
    return skip, output(where, mixed, skip, o_pieces)


def solution(mesh):
    rows = P(("dp", "seq"), None)
    in_specs = (rows, P(), P(), P(), P(), P("seq", None), P("seq", None), P("seq", None))
    return jax.shard_map(
        body, mesh=mesh, in_specs=in_specs, out_specs=(rows, rows), check_vma=False
    )
```

time: 177 us -> 164 us (0.927)
  matrix products: 64 us -> 0 us
  Pallas kernels: 0 us -> 60.7 us
  starting transfers between devices: 12 us -> 63.5 us
  other arithmetic: 28.6 us -> 4.38 us
  waiting for transfers between devices: 45.3 us -> 26.4 us
  between operations: 14.3 us -> 1.11 us
  local copies, waits for them, and re-layouts: 11.8 us -> 7.78 us
    dot_general x10 -> x0, matrix products: 64 us -> none  [the longest x5 23.9 us: body(): jnp.dot(padded[kernel_tap:kernel_tap + pos_rows], conv_weight[kernel_tap]...]
    pallas_call x0 -> x5, Pallas kernels: none -> 60.7 us  [the longest x1 22.6 us: attention(): pl.pallas_call(functools.partial(attention_kernel, counts), out_shape=jax...]
    ppermute x2 -> x26, starting transfers between devices: 8.13 us -> 63.5 us  [the longest x24 55.6 us: send(): return lax.ppermute(array, AXES, pairs)]
    all_to_all x1 -> x0, waiting for transfers between devices: 26.6 us -> none  [from_everyone(): lax.all_to_all(jnp.broadcast_to(array[None], (count, *array.shape)), axis...]
    ppermute x2 -> x26, waiting for transfers between devices: 4.49 us -> 26.4 us  [the longest x24 26.4 us: send(): return lax.ppermute(array, AXES, pairs)]
    reduce_sum x3 -> x0, other arithmetic: 16.6 us -> none  [the longest x1 14.3 us: body(): total_new = jnp.sum(weights, axis=-1)]
    all_gather x2 -> x0, waiting for transfers between devices: 13.5 us -> none  [the longest x1 13.5 us: in_one_piece(): lax.all_gather(both, axis, axis=dim, tiled=True)]
    reduce_max x1 -> x0, other arithmetic: 4.3 us -> none  [body(): jnp.max(summed.reshape(tok_rows, 2, width), axis=1).astype(jnp.bfloat16)]
  transfers between devices with their start and end apart: 5 -> 26, of which waited for: 3 -> 7; matrix products, arithmetic and copies ran while one was open for 53% -> 5% of each run, Pallas kernels for 0% -> 33%
where the time goes in v1:
time: 164 us
  starting transfers between devices  63.5 us (39%)
  Pallas kernels  60.7 us (37%)
  waiting for transfers between devices  26.4 us (16%)
  local copies, waits for them, and re-layouts  7.78 us (5%)
  other arithmetic  4.38 us (3%)
    ppermute x24, starting transfers between devices, send(): return lax.ppermute(array, AXES, pairs)  55.6 us
    ppermute x24, waiting for transfers between devices, send(): return lax.ppermute(array, AXES, pairs)  26.4 us
    pallas_call x1, Pallas kernels, attention(): pl.pallas_call(functools.partial(attention_kernel, counts), out_shape=jax...  22.6 us
    pallas_call x1, Pallas kernels, convolve(): pl.pallas_call(functools.partial(conv_kernel, taps), out_shape=(out, out)...  19.3 us
    pallas_call x1, Pallas kernels, project(): pl.pallas_call(project_kernel, out_shape=(jax.ShapeDtypeStruct((HEADS, ro...  6.61 us
    pallas_call x1, Pallas kernels, activate(): pl.pallas_call(activate_kernel, out_shape=(out, out), scratch_shapes=[plt...  6.16 us
    pallas_call x1, Pallas kernels, output(): pl.pallas_call(output_kernel, out_shape=jax.ShapeDtypeStruct((rows, width...  6.09 us
    ppermute x1, starting transfers between devices, body(): before = lax.ppermute(x[-2:], 'seq', up)  5.74 us
  transfers between devices with their start and end apart: 26, of which 7 were waited for; matrix products, arithmetic and copies ran while one was open for 5% of the time, Pallas kernels for 33%

profile of v1, /device:TPU:1, one launch (start us, length us, event | category | flops | bytes accessed | tf_op | source)
XLA Modules:
  0.0 163.9 jit_solution(1660895641696792226)
XLA Ops:
  0.6 0.9 constant_dynamic-update-slice_fusion.1
  1.6 0.9 constant_dynamic-update-slice_fusion
  2.5 3.6 %collective-permute-start.2 = (bf16[96,1344]{1,0:T(8,128)(2,1)S(1)}, bf16[96,1344]{1,0:T(8,128)(2,1)S(1)}, u32[]{:S(2)}, u32[]{:S(2)}) collective-permute-start(bf16[96,1344]{1,0:T(8,128)(2,1)S(1)} %constant_dynamic-update-slice_fusion), channel_id=1, source_target_pairs={{0,18},{1,19},{2,16},{3,17},{4,22},{5,23},{6,20},{7,21},{8,26},{9,... | collective-permute-start | bytes 774152 | tf_op jit(solution)/shard_map/ppermute | solution.py:48
  6.1 6.0 %collective-permute-done.2 = bf16[96,1344]{1,0:T(8,128)(2,1)S(1)} collective-permute-done((bf16[96,1344]{1,0:T(8,128)(2,1)S(1)}, bf16[96,1344]{1,0:T(8,128)(2,1)S(1)}, u32[]{:S(2)}, u32[]{:S(2)}) %collective-permute-start.2) | collective-permute-done | bytes 258080 | tf_op jit(solution)/shard_map/ppermute | solution.py:48
  12.3 1.6 collective-permute-start.3
  13.9 2.2 %collective-permute-start.4 = (bf16[192,1344]{1,0:T(8,128)(2,1)S(1)}, bf16[192,1344]{1,0:T(8,128)(2,1)S(1)}, u32[]{:S(2)}, u32[]{:S(2)}) collective-permute-start(bf16[192,1344]{1,0:T(8,128)(2,1)S(1)} %maximum_select_fusion.1.rest_0_), channel_id=1, source_target_pairs={{0,12},{1,13},{2,14},{3,15},{4,0},{5,1},{6,2},{7,3},{8,4},{9,5},{1... | collective-permute-start | bytes 1548296 | tf_op jit(solution)/shard_map/ppermute | solution.py:48
  16.1 1.2 collective-permute-start.5
  17.3 1.4 fusion.1
  18.7 5.7 %collective-permute-start = (bf16[2,1536]{1,0:T(2,128)(2,1)}, bf16[2,1536]{1,0:T(2,128)(2,1)}, u32[]{:S(2)}, u32[]{:S(2)}) collective-permute-start(bf16[2,1536]{1,0:T(2,128)(2,1)} %get-tuple-element.15), channel_id=1, source_target_pairs={{0,1},{1,2},{2,3},{3,4},{4,5},{5,6},{6,7},{7,8},{8,9},{9,10},{10,1... | collective-permute-start | bytes 18440 | tf_op jit(solution)/shard_map/ppermute | solution.py:412
  24.5 0.6 add_convert_fusion
  25.0 2.1 %collective-permute-done.3.rest_1_ = bf16[192,1344]{1,0:T(8,128)(2,1)S(1)} collective-permute-done((bf16[192,1344]{1,0:T(8,128)(2,1)S(1)}, bf16[192,1344]{1,0:T(8,128)(2,1)S(1)}, u32[]{:S(2)}, u32[]{:S(2)}) %collective-permute-start.3) | collective-permute-done | bytes 516128 | tf_op jit(solution)/shard_map/ppermute | solution.py:48
  27.2 2.9 %collective-permute-start.7 = (bf16[192,1344]{1,0:T(8,128)(2,1)S(1)}, bf16[192,1344]{1,0:T(8,128)(2,1)S(1)}, u32[]{:S(2)}, u32[]{:S(2)}) collective-permute-start(bf16[192,1344]{1,0:T(8,128)(2,1)S(1)} %collective-permute-done.3.rest_1_), channel_id=1, source_target_pairs={{0,1},{1,0},{2,3},{3,2},{4,5},{5,4},{6,7},{7,6},{8,9},{9,8},{10,11... | collective-permute-start | bytes 1548296 | tf_op jit(solution)/shard_map/ppermute | solution.py:48
  30.0 10.2 %collective-permute-start.8 = (bf16[192,1344]{1,0:T(8,128)(2,1)S(1)}, bf16[192,1344]{1,0:T(8,128)(2,1)}, u32[]{:S(2)}, u32[]{:S(2)}) collective-permute-start(bf16[192,1344]{1,0:T(8,128)(2,1)S(1)} %collective-permute-done.4.rest_2_), channel_id=1, source_target_pairs={{0,1},{1,0},{2,3},{3,2},{4,5},{5,4},{6,7},{7,6},{8,9},{9,8},{10,11... | collective-permute-start | bytes 1548296 | tf_op jit(solution)/shard_map/ppermute | solution.py:48
  40.2 1.9 %collective-permute-start.9 = (bf16[192,1344]{1,0:T(8,128)(2,1)S(1)}, bf16[192,1344]{1,0:T(8,128)(2,1)}, u32[]{:S(2)}, u32[]{:S(2)}) collective-permute-start(bf16[192,1344]{1,0:T(8,128)(2,1)S(1)} %collective-permute-done.5.rest_3_), channel_id=1, source_target_pairs={{0,1},{1,0},{2,3},{3,2},{4,5},{5,4},{6,7},{7,6},{8,9},{9,8},{10,11... | collective-permute-start | bytes 1548296 | tf_op jit(solution)/shard_map/ppermute | solution.py:48
  42.1 0.5 multiply_power_fusion
  42.6 2.1 %collective-permute-start.1 = (bf16[2,1536]{1,0:T(2,128)(2,1)}, bf16[2,1536]{1,0:T(2,128)(2,1)S(1)}, u32[]{:S(2)}, u32[]{:S(2)}) collective-permute-start(bf16[2,1536]{1,0:T(2,128)(2,1)} %get-tuple-element.14), channel_id=1, source_target_pairs={{1,0},{2,1},{3,2},{4,3},{5,4},{6,5},{7,6},{8,7},{9,8},{10,9},{11,1... | collective-permute-start | bytes 18440 | tf_op jit(solution)/shard_map/ppermute | solution.py:413
  44.7 0.6 pad_add_fusion.where_ref
  45.3 0.6 broadcast_in_dim.15.gain_ref.cg_ref
  45.9 6.2 %activate.1 = (bf16[2,256,1536]{2,1,0:T(8,128)(2,1)}, bf16[2,256,1536]{2,1,0:T(8,128)(2,1)}) custom-call(bf16[512,1536]{1,0:T(8,128)(2,1)} %x_ref.1, f32[1,1536]{1,0:T(1,128)} %broadcast_in_dim.15.gain_ref.cg_ref), custom_call_target="tpu_custom_call" | custom-call | tf_op jit(solution)/shard_map/activate/pallas_call | solution.py:83
  52.1 0.6 broadcast_in_dim.16.b_ref
  52.6 0.6 broadcast_in_dim.17.ag_ref
  53.3 2.6 %collective-permute-start.18 = (bf16[96,1536]{1,0:T(8,128)(2,1)S(1)}, bf16[96,1536]{1,0:T(8,128)(2,1)}, u32[]{:S(2)}, u32[]{:S(2)}) collective-permute-start(bf16[96,1536]{1,0:T(8,128)(2,1)S(1)} %copy-done.20), channel_id=1, source_target_pairs={{0,18},{1,19},{2,16},{3,17},{4,22},{5,23},{6,20},{7,21},{8,26},{9,... | collective-permute-start | bytes 884744 | tf_op jit(solution)/shard_map/ppermute | solution.py:48
  55.9 0.5 fusion
  56.4 0.9 pad_maximum_fusion.1
  57.3 19.3 %conv.1 = (bf16[256,1536]{1,0:T(8,128)(2,1)}, bf16[256,1536]{1,0:T(8,128)(2,1)}) custom-call(bf16[2,256,1536]{2,1,0:T(8,128)(2,1)} %get-tuple-element.8.act_ref, bf16[2,256,1536]{2,1,0:T(8,128)(2,1)} %get-tuple-element.9.raw_ref, bf16[2,1536]{1,0:T(2,128)(2,1)} %collective-permute-done.before_ref, bf16[2,1536]{1,0:T(2,128)(2,1)} %copy-done.25, ...), custom_call_target="tpu_custom_call" | custom-call | tf_op jit(solution)/shard_map/conv/pallas_call | solution.py:138
  76.7 0.8 copy-done.11
  77.4 0.2 copy-done.12
  77.7 6.6 %project.1 = (bf16[8,256,128]{2,1,0:T(8,128)(2,1)}, bf16[640,128]{1,0:T(8,128)(2,1)}) custom-call(s32[2]{0:T(128)} %pad_add_fusion.where_ref, bf16[256,1536]{1,0:T(8,128)(2,1)} %get-tuple-element.11.norm_ref, f32[256,128]{1,0:T(8,128)} %get-tuple-element.19.cos_ref, f32[256,128]{1,0:T(8,128)} %get-tuple-element.20.sin_ref, bf16[192,1344]{1,0:T(8,128)(2,1)} %copy-done.1, ...), custom_call_target="tpu_custom_call" | custom-call | tf_op jit(solution)/shard_map/project/pallas_call | solution.py:222
  84.4 1.2 maximum_select_fusion.rest_0_
  85.6 0.9 collective-permute-start.19
  86.5 1.8 %collective-permute-start.20 = (bf16[192,1536]{1,0:T(8,128)(2,1)S(1)}, bf16[192,1536]{1,0:T(8,128)(2,1)S(1)}, u32[]{:S(2)}, u32[]{:S(2)}) collective-permute-start(bf16[192,1536]{1,0:T(8,128)(2,1)S(1)} %maximum_select_fusion.rest_0_), channel_id=1, source_target_pairs={{0,12},{1,13},{2,14},{3,15},{4,0},{5,1},{6,2},{7,3},{8,4},{9,5},{1... | collective-permute-start | bytes 1769480 | tf_op jit(solution)/shard_map/ppermute | solution.py:48
  88.3 3.1 %collective-permute-done.10 = bf16[1,640,128]{2,1,0:T(8,128)(2,1)S(1)} collective-permute-done((bf16[1,640,128]{2,1,0:T(8,128)(2,1)}, bf16[1,640,128]{2,1,0:T(8,128)(2,1)S(1)}, u32[]{:S(2)}, u32[]{:S(2)}) %collective-permute-start.10) | collective-permute-done | bytes 163872 | tf_op jit(solution)/shard_map/ppermute | solution.py:48
  91.5 1.0 collective-permute-start.11
  92.5 2.4 %collective-permute-start.21 = (bf16[192,1536]{1,0:T(8,128)(2,1)S(1)}, bf16[192,1536]{1,0:T(8,128)(2,1)S(1)}, u32[]{:S(2)}, u32[]{:S(2)}) collective-permute-start(bf16[192,1536]{1,0:T(8,128)(2,1)S(1)} %maximum_select_fusion.rest_0_), channel_id=1, source_target_pairs={{0,8},{1,9},{2,10},{3,11},{4,12},{5,13},{6,14},{7,15},{8,0},{9,1},... | collective-permute-start | bytes 1769480 | tf_op jit(solution)/shard_map/ppermute | solution.py:48
  95.0 5.6 %collective-permute-done.19.rest_1_ = bf16[192,1536]{1,0:T(8,128)(2,1)S(1)} collective-permute-done((bf16[192,1536]{1,0:T(8,128)(2,1)S(1)}, bf16[192,1536]{1,0:T(8,128)(2,1)S(1)}, u32[]{:S(2)}, u32[]{:S(2)}) %collective-permute-start.19) | collective-permute-done | bytes 589856 | tf_op jit(solution)/shard_map/ppermute | solution.py:48
  100.6 0.8 collective-permute-done.20.rest_2_
  101.4 13.4 %collective-permute-start.14 = (bf16[2,640,128]{2,1,0:T(8,128)(2,1)S(1)}, bf16[2,640,128]{2,1,0:T(8,128)(2,1)S(1)}, u32[]{:S(2)}, u32[]{:S(2)}) collective-permute-start(bf16[2,640,128]{2,1,0:T(8,128)(2,1)S(1)} %pad_maximum_fusion.rest_0_), channel_id=1, source_target_pairs={{0,1},{1,0},{2,3},{3,2},{4,5},{5,4},{6,7},{7,6},{8,9},{9,8},{10,11... | collective-permute-start | bytes 983048 | tf_op jit(solution)/shard_map/ppermute | solution.py:48
  114.9 6.1 %collective-permute-done.12.rest_2_ = bf16[2,640,128]{2,1,0:T(8,128)(2,1)S(1)} collective-permute-done((bf16[2,640,128]{2,1,0:T(8,128)(2,1)S(1)}, bf16[2,640,128]{2,1,0:T(8,128)(2,1)S(1)}, u32[]{:S(2)}, u32[]{:S(2)}) %collective-permute-start.12) | collective-permute-done | bytes 327712 | tf_op jit(solution)/shard_map/ppermute | solution.py:48
  121.0 7.6 %collective-permute-start.16 = (bf16[2,640,128]{2,1,0:T(8,128)(2,1)S(1)}, bf16[2,640,128]{2,1,0:T(8,128)(2,1)S(1)}, u32[]{:S(2)}, u32[]{:S(2)}) collective-permute-start(bf16[2,640,128]{2,1,0:T(8,128)(2,1)S(1)} %collective-permute-done.12.rest_2_), channel_id=1, source_target_pairs={{0,1},{1,0},{2,3},{3,2},{4,5},{5,4},{6,7},{7,6},{8,9},{9,8},{10,11... | collective-permute-start | bytes 983048 | tf_op jit(solution)/shard_map/ppermute | solution.py:48
  128.7 1.1 collective-permute-start.23
  129.9 0.5 collective-permute-start.25
  130.4 0.2 collective-permute-start.17
  130.6 2.6 %collective-permute-done.17.rest_7_ = bf16[2,640,128]{2,1,0:T(8,128)(2,1)S(1)} collective-permute-done((bf16[2,640,128]{2,1,0:T(8,128)(2,1)S(1)}, bf16[2,640,128]{2,1,0:T(8,128)(2,1)S(1)}, u32[]{:S(2)}, u32[]{:S(2)}) %collective-permute-start.17) | collective-permute-done | bytes 327712 | tf_op jit(solution)/shard_map/ppermute | solution.py:48
  133.2 0.7 copy-done.19
  134.0 22.6 %attention.1.mixed_ref = bf16[256,1536]{1,0:T(8,128)(2,1)} custom-call(bf16[8,256,128]{2,1,0:T(8,128)(2,1)} %get-tuple-element.12.q_ref, bf16[2,640,128]{2,1,0:T(8,128)(2,1)} %copy-done.2, bf16[2,640,128]{2,1,0:T(8,128)(2,1)} %copy-done.13, bf16[2,640,128]{2,1,0:T(8,128)(2,1)} %copy-done.14, bf16[2,640,128]{2,1,0:T(8,128)(2,1)} %copy-done.15, ...), custom_call_target="tpu_custom_call" | custom-call | tf_op jit(solution)/shard_map/attention/pallas_call | solution.py:342
  156.7 0.8 copy-done.6
  157.4 0.2 copy-done.7
  157.6 6.1 %output.1 = bf16[256,1536]{1,0:T(8,128)(2,1)} custom-call(s32[2]{0:T(128)} %pad_add_fusion.where_ref, bf16[256,1536]{1,0:T(8,128)(2,1)} %attention.1.mixed_ref, bf16[256,1536]{1,0:T(8,128)(2,1)} %get-tuple-element.6.skip_ref, bf16[192,1536]{1,0:T(8,128)(2,1)} %copy-done, bf16[192,1536]{1,0:T(8,128)(2,1)} %copy-done.3, bf16[192,1536]{1,0:T(8,128)(2,1)} %copy-done.4, ...), custom_call_target="tpu_custom_call" | custom-call | tf_op jit(solution)/shard_map/output/pallas_call | solution.py:377
  (79 shorter events, 0.7 us)
Async XLA Ops:
  0.6 44.7 %copy-start.22 = (f32[1536]{0:T(1024)S(1)}, f32[1536]{0:T(1024)}, u32[]{:S(2)}) copy-start(f32[1536]{0:T(1024)} %param.9) | copy-start | bytes 18436
  2.5 9.7 %collective-permute-start.2 = (bf16[96,1344]{1,0:T(8,128)(2,1)S(1)}, bf16[96,1344]{1,0:T(8,128)(2,1)S(1)}, u32[]{:S(2)}, u32[]{:S(2)}) collective-permute-start(bf16[96,1344]{1,0:T(8,128)(2,1)S(1)} %constant_dynamic-update-slice_fusion), channel_id=1, source_target_pairs={{0,18},{1,19},{2,16},{3,17},{4,22},{5,23},{6,20},{7,21},{8,26},{9,... | collective-permute-start | bytes 774152 | tf_op jit(solution)/shard_map/ppermute | solution.py:48
  6.1 45.9 %copy-start.23 = (f32[1536]{0:T(1024)S(1)}, f32[1536]{0:T(1024)}, u32[]{:S(2)}) copy-start(f32[1536]{0:T(1024)} %param.11) | copy-start | bytes 18436
  6.1 47.1 %copy-start.20 = (bf16[96,1536]{1,0:T(8,128)(2,1)S(1)}, bf16[96,1536]{1,0:T(8,128)(2,1)}, u32[]{:S(2)}) copy-start(bf16[96,1536]{1,0:T(8,128)(2,1)} %param.15) | copy-start | bytes 884740
  12.3 45.0 %copy-start.1 = (bf16[192,1344]{1,0:T(8,128)(2,1)}, bf16[192,1344]{1,0:T(8,128)(2,1)S(1)}, u32[]{:S(2)}) copy-start(bf16[192,1344]{1,0:T(8,128)(2,1)S(1)} %maximum_select_fusion.1.rest_0_) | copy-start | bytes 1548292
  12.3 14.8 %collective-permute-start.3 = (bf16[192,1344]{1,0:T(8,128)(2,1)S(1)}, bf16[192,1344]{1,0:T(8,128)(2,1)S(1)}, u32[]{:S(2)}, u32[]{:S(2)}) collective-permute-start(bf16[192,1344]{1,0:T(8,128)(2,1)S(1)} %maximum_select_fusion.1.rest_0_), channel_id=1, source_target_pairs={{0,4},{1,5},{2,6},{3,7},{4,8},{5,9},{6,10},{7,11},{8,12},{9,13},{1... | collective-permute-start | bytes 1548296 | tf_op jit(solution)/shard_map/ppermute | solution.py:48
  13.9 16.1 %collective-permute-start.4 = (bf16[192,1344]{1,0:T(8,128)(2,1)S(1)}, bf16[192,1344]{1,0:T(8,128)(2,1)S(1)}, u32[]{:S(2)}, u32[]{:S(2)}) collective-permute-start(bf16[192,1344]{1,0:T(8,128)(2,1)S(1)} %maximum_select_fusion.1.rest_0_), channel_id=1, source_target_pairs={{0,12},{1,13},{2,14},{3,15},{4,0},{5,1},{6,2},{7,3},{8,4},{9,5},{1... | collective-permute-start | bytes 1548296 | tf_op jit(solution)/shard_map/ppermute | solution.py:48
  16.1 24.1 %collective-permute-start.5 = (bf16[192,1344]{1,0:T(8,128)(2,1)S(1)}, bf16[192,1344]{1,0:T(8,128)(2,1)S(1)}, u32[]{:S(2)}, u32[]{:S(2)}) collective-permute-start(bf16[192,1344]{1,0:T(8,128)(2,1)S(1)} %maximum_select_fusion.1.rest_0_), channel_id=1, source_target_pairs={{0,8},{1,9},{2,10},{3,11},{4,12},{5,13},{6,14},{7,15},{8,0},{9,1},... | collective-permute-start | bytes 1548296 | tf_op jit(solution)/shard_map/ppermute | solution.py:48
  18.7 23.9 %collective-permute-start = (bf16[2,1536]{1,0:T(2,128)(2,1)}, bf16[2,1536]{1,0:T(2,128)(2,1)}, u32[]{:S(2)}, u32[]{:S(2)}) collective-permute-start(bf16[2,1536]{1,0:T(2,128)(2,1)} %get-tuple-element.15), channel_id=1, source_target_pairs={{0,1},{1,2},{2,3},{3,4},{4,5},{5,6},{6,7},{7,8},{8,9},{9,10},{10,1... | collective-permute-start | bytes 18440 | tf_op jit(solution)/shard_map/ppermute | solution.py:412
  25.0 51.6 %collective-permute-start.6 = (bf16[192,1344]{1,0:T(8,128)(2,1)S(1)}, bf16[192,1344]{1,0:T(8,128)(2,1)S(1)}, u32[]{:S(2)}, u32[]{:S(2)}) collective-permute-start(bf16[192,1344]{1,0:T(8,128)(2,1)S(1)} %maximum_select_fusion.1.rest_0_), channel_id=1, source_target_pairs={{0,1},{1,0},{2,3},{3,2},{4,5},{5,4},{6,7},{7,6},{8,9},{9,8},{10,11... | collective-permute-start | bytes 1548296 | tf_op jit(solution)/shard_map/ppermute | solution.py:48
  27.2 30.1 %copy-start.8 = (bf16[192,1344]{1,0:T(8,128)(2,1)}, bf16[192,1344]{1,0:T(8,128)(2,1)S(1)}, u32[]{:S(2)}) copy-start(bf16[192,1344]{1,0:T(8,128)(2,1)S(1)} %collective-permute-done.3.rest_1_) | copy-start | bytes 1548292
  27.2 49.5 %collective-permute-start.7 = (bf16[192,1344]{1,0:T(8,128)(2,1)S(1)}, bf16[192,1344]{1,0:T(8,128)(2,1)S(1)}, u32[]{:S(2)}, u32[]{:S(2)}) collective-permute-start(bf16[192,1344]{1,0:T(8,128)(2,1)S(1)} %collective-permute-done.3.rest_1_), channel_id=1, source_target_pairs={{0,1},{1,0},{2,3},{3,2},{4,5},{5,4},{6,7},{7,6},{8,9},{9,8},{10,11... | collective-permute-start | bytes 1548296 | tf_op jit(solution)/shard_map/ppermute | solution.py:48
  30.0 27.3 %copy-start.9 = (bf16[192,1344]{1,0:T(8,128)(2,1)}, bf16[192,1344]{1,0:T(8,128)(2,1)S(1)}, u32[]{:S(2)}) copy-start(bf16[192,1344]{1,0:T(8,128)(2,1)S(1)} %collective-permute-done.4.rest_2_) | copy-start | bytes 1548292
  30.0 46.6 %collective-permute-start.8 = (bf16[192,1344]{1,0:T(8,128)(2,1)S(1)}, bf16[192,1344]{1,0:T(8,128)(2,1)}, u32[]{:S(2)}, u32[]{:S(2)}) collective-permute-start(bf16[192,1344]{1,0:T(8,128)(2,1)S(1)} %collective-permute-done.4.rest_2_), channel_id=1, source_target_pairs={{0,1},{1,0},{2,3},{3,2},{4,5},{5,4},{6,7},{7,6},{8,9},{9,8},{10,11... | collective-permute-start | bytes 1548296 | tf_op jit(solution)/shard_map/ppermute | solution.py:48
  40.2 17.1 %copy-start.10 = (bf16[192,1344]{1,0:T(8,128)(2,1)}, bf16[192,1344]{1,0:T(8,128)(2,1)S(1)}, u32[]{:S(2)}) copy-start(bf16[192,1344]{1,0:T(8,128)(2,1)S(1)} %collective-permute-done.5.rest_3_) | copy-start | bytes 1548292
  40.2 36.4 %collective-permute-start.9 = (bf16[192,1344]{1,0:T(8,128)(2,1)S(1)}, bf16[192,1344]{1,0:T(8,128)(2,1)}, u32[]{:S(2)}, u32[]{:S(2)}) collective-permute-start(bf16[192,1344]{1,0:T(8,128)(2,1)S(1)} %collective-permute-done.5.rest_3_), channel_id=1, source_target_pairs={{0,1},{1,0},{2,3},{3,2},{4,5},{5,4},{6,7},{7,6},{8,9},{9,8},{10,11... | collective-permute-start | bytes 1548296 | tf_op jit(solution)/shard_map/ppermute | solution.py:48
  42.6 10.0 %copy-start.24 = (f32[1536]{0:T(1024)S(1)}, f32[1536]{0:T(1024)}, u32[]{:S(2)}) copy-start(f32[1536]{0:T(1024)} %param.12) | copy-start | bytes 18436
  42.6 13.2 %copy-start.26 = (f32[256]{0:T(256)S(1)}, f32[256]{0:T(256)}, u32[]{:S(2)}) copy-start(f32[256]{0:T(256)} %add_convert_fusion) | copy-start | bytes 3076
  42.6 13.2 %copy-start.27 = (f32[64]{0:T(128)S(1)}, f32[64]{0:T(128)}, u32[]{:S(2)}) copy-start(f32[64]{0:T(128)} %multiply_power_fusion) | copy-start | bytes 772
  42.6 10.6 %collective-permute-start.1 = (bf16[2,1536]{1,0:T(2,128)(2,1)}, bf16[2,1536]{1,0:T(2,128)(2,1)S(1)}, u32[]{:S(2)}, u32[]{:S(2)}) collective-permute-start(bf16[2,1536]{1,0:T(2,128)(2,1)} %get-tuple-element.14), channel_id=1, source_target_pairs={{1,0},{2,1},{3,2},{4,3},{5,4},{6,5},{7,6},{8,7},{9,8},{10,9},{11,1... | collective-permute-start | bytes 18440 | tf_op jit(solution)/shard_map/ppermute | solution.py:413
  53.2 4.1 %copy-start.25 = (bf16[2,1536]{1,0:T(2,128)(2,1)}, bf16[2,1536]{1,0:T(2,128)(2,1)S(1)}, u32[]{:S(2)}) copy-start(bf16[2,1536]{1,0:T(2,128)(2,1)S(1)} %collective-permute-done.1.after_ref) | copy-start | bytes 18436
  53.3 31.1 %collective-permute-start.18 = (bf16[96,1536]{1,0:T(8,128)(2,1)S(1)}, bf16[96,1536]{1,0:T(8,128)(2,1)}, u32[]{:S(2)}, u32[]{:S(2)}) collective-permute-start(bf16[96,1536]{1,0:T(8,128)(2,1)S(1)} %copy-done.20), channel_id=1, source_target_pairs={{0,18},{1,19},{2,16},{3,17},{4,22},{5,23},{6,20},{7,21},{8,26},{9,... | collective-permute-start | bytes 884744 | tf_op jit(solution)/shard_map/ppermute | solution.py:48
  84.3 7.1 %copy-start.21 = (bf16[640,128]{1,0:T(8,128)(2,1)S(1)}, bf16[640,128]{1,0:T(8,128)(2,1)}, u32[]{:S(2)}) copy-start(bf16[640,128]{1,0:T(8,128)(2,1)} %get-tuple-element.13) | copy-start | bytes 491524
  84.3 7.1 %collective-permute-start.10 = (bf16[1,640,128]{2,1,0:T(8,128)(2,1)}, bf16[1,640,128]{2,1,0:T(8,128)(2,1)S(1)}, u32[]{:S(2)}, u32[]{:S(2)}) collective-permute-start(bf16[1,640,128]{2,1,0:T(8,128)(2,1)} %bitcast.3), channel_id=1, source_target_pairs={{0,2},{1,3},{2,0},{3,1},{4,6},{5,7},{6,4},{7,5},{8,10},{9,11},{10,... | collective-permute-start | bytes 491528 | tf_op jit(solution)/shard_map/ppermute | solution.py:48
  85.6 71.0 %copy-start = (bf16[192,1536]{1,0:T(8,128)(2,1)}, bf16[192,1536]{1,0:T(8,128)(2,1)S(1)}, u32[]{:S(2)}) copy-start(bf16[192,1536]{1,0:T(8,128)(2,1)S(1)} %maximum_select_fusion.rest_0_) | copy-start | bytes 1769476
  85.6 15.0 %collective-permute-start.19 = (bf16[192,1536]{1,0:T(8,128)(2,1)S(1)}, bf16[192,1536]{1,0:T(8,128)(2,1)S(1)}, u32[]{:S(2)}, u32[]{:S(2)}) collective-permute-start(bf16[192,1536]{1,0:T(8,128)(2,1)S(1)} %maximum_select_fusion.rest_0_), channel_id=1, source_target_pairs={{0,4},{1,5},{2,6},{3,7},{4,8},{5,9},{6,10},{7,11},{8,12},{9,13},{1... | collective-permute-start | bytes 1769480 | tf_op jit(solution)/shard_map/ppermute | solution.py:48
  86.5 14.9 %collective-permute-start.20 = (bf16[192,1536]{1,0:T(8,128)(2,1)S(1)}, bf16[192,1536]{1,0:T(8,128)(2,1)S(1)}, u32[]{:S(2)}, u32[]{:S(2)}) collective-permute-start(bf16[192,1536]{1,0:T(8,128)(2,1)S(1)} %maximum_select_fusion.rest_0_), channel_id=1, source_target_pairs={{0,12},{1,13},{2,14},{3,15},{4,0},{5,1},{6,2},{7,3},{8,4},{9,5},{1... | collective-permute-start | bytes 1769480 | tf_op jit(solution)/shard_map/ppermute | solution.py:48
  91.4 42.5 %copy-start.2 = (bf16[2,640,128]{2,1,0:T(8,128)(2,1)}, bf16[2,640,128]{2,1,0:T(8,128)(2,1)S(1)}, u32[]{:S(2)}) copy-start(bf16[2,640,128]{2,1,0:T(8,128)(2,1)S(1)} %pad_maximum_fusion.rest_0_) | copy-start | bytes 983044
  91.5 23.3 %collective-permute-start.11 = (bf16[2,640,128]{2,1,0:T(8,128)(2,1)S(1)}, bf16[2,640,128]{2,1,0:T(8,128)(2,1)S(1)}, u32[]{:S(2)}, u32[]{:S(2)}) collective-permute-start(bf16[2,640,128]{2,1,0:T(8,128)(2,1)S(1)} %pad_maximum_fusion.rest_0_), channel_id=1, source_target_pairs={{0,4},{1,5},{2,6},{3,7},{4,8},{5,9},{6,10},{7,11},{8,12},{9,13},{1... | collective-permute-start | bytes 983048 | tf_op jit(solution)/shard_map/ppermute | solution.py:48
  92.5 36.1 %collective-permute-start.21 = (bf16[192,1536]{1,0:T(8,128)(2,1)S(1)}, bf16[192,1536]{1,0:T(8,128)(2,1)S(1)}, u32[]{:S(2)}, u32[]{:S(2)}) collective-permute-start(bf16[192,1536]{1,0:T(8,128)(2,1)S(1)} %maximum_select_fusion.rest_0_), channel_id=1, source_target_pairs={{0,8},{1,9},{2,10},{3,11},{4,12},{5,13},{6,14},{7,15},{8,0},{9,1},... | collective-permute-start | bytes 1769480 | tf_op jit(solution)/shard_map/ppermute | solution.py:48
  94.9 26.1 %collective-permute-start.12 = (bf16[2,640,128]{2,1,0:T(8,128)(2,1)S(1)}, bf16[2,640,128]{2,1,0:T(8,128)(2,1)S(1)}, u32[]{:S(2)}, u32[]{:S(2)}) collective-permute-start(bf16[2,640,128]{2,1,0:T(8,128)(2,1)S(1)} %pad_maximum_fusion.rest_0_), channel_id=1, source_target_pairs={{0,12},{1,13},{2,14},{3,15},{4,0},{5,1},{6,2},{7,3},{8,4},{9,5},{1... | collective-permute-start | bytes 983048 | tf_op jit(solution)/shard_map/ppermute | solution.py:48
  100.6 56.0 %copy-start.3 = (bf16[192,1536]{1,0:T(8,128)(2,1)}, bf16[192,1536]{1,0:T(8,128)(2,1)S(1)}, u32[]{:S(2)}) copy-start(bf16[192,1536]{1,0:T(8,128)(2,1)S(1)} %collective-permute-done.19.rest_1_) | copy-start | bytes 1769476
  100.6 28.1 %collective-permute-start.13 = (bf16[2,640,128]{2,1,0:T(8,128)(2,1)S(1)}, bf16[2,640,128]{2,1,0:T(8,128)(2,1)S(1)}, u32[]{:S(2)}, u32[]{:S(2)}) collective-permute-start(bf16[2,640,128]{2,1,0:T(8,128)(2,1)S(1)} %pad_maximum_fusion.rest_0_), channel_id=1, source_target_pairs={{0,8},{1,9},{2,10},{3,11},{4,12},{5,13},{6,14},{7,15},{8,0},{9,1},... | collective-permute-start | bytes 983048 | tf_op jit(solution)/shard_map/ppermute | solution.py:48
  101.4 55.2 %copy-start.4 = (bf16[192,1536]{1,0:T(8,128)(2,1)}, bf16[192,1536]{1,0:T(8,128)(2,1)S(1)}, u32[]{:S(2)}) copy-start(bf16[192,1536]{1,0:T(8,128)(2,1)S(1)} %collective-permute-done.20.rest_2_) | copy-start | bytes 1769476
  101.4 28.4 %collective-permute-start.14 = (bf16[2,640,128]{2,1,0:T(8,128)(2,1)S(1)}, bf16[2,640,128]{2,1,0:T(8,128)(2,1)S(1)}, u32[]{:S(2)}, u32[]{:S(2)}) collective-permute-start(bf16[2,640,128]{2,1,0:T(8,128)(2,1)S(1)} %pad_maximum_fusion.rest_0_), channel_id=1, source_target_pairs={{0,1},{1,0},{2,3},{3,2},{4,5},{5,4},{6,7},{7,6},{8,9},{9,8},{10,11... | collective-permute-start | bytes 983048 | tf_op jit(solution)/shard_map/ppermute | solution.py:48
  114.8 15.1 %copy-start.13 = (bf16[2,640,128]{2,1,0:T(8,128)(2,1)}, bf16[2,640,128]{2,1,0:T(8,128)(2,1)S(1)}, u32[]{:S(2)}) copy-start(bf16[2,640,128]{2,1,0:T(8,128)(2,1)S(1)} %collective-permute-done.11.rest_1_) | copy-start | bytes 983044
  114.8 15.1 %collective-permute-start.15 = (bf16[2,640,128]{2,1,0:T(8,128)(2,1)S(1)}, bf16[2,640,128]{2,1,0:T(8,128)(2,1)S(1)}, u32[]{:S(2)}, u32[]{:S(2)}) collective-permute-start(bf16[2,640,128]{2,1,0:T(8,128)(2,1)S(1)} %collective-permute-done.11.rest_1_), channel_id=1, source_target_pairs={{0,1},{1,0},{2,3},{3,2},{4,5},{5,4},{6,7},{7,6},{8,9},{9,8},{10,11... | collective-permute-start | bytes 983048 | tf_op jit(solution)/shard_map/ppermute | solution.py:48
  121.0 8.9 %copy-start.14 = (bf16[2,640,128]{2,1,0:T(8,128)(2,1)}, bf16[2,640,128]{2,1,0:T(8,128)(2,1)S(1)}, u32[]{:S(2)}) copy-start(bf16[2,640,128]{2,1,0:T(8,128)(2,1)S(1)} %collective-permute-done.12.rest_2_) | copy-start | bytes 983044
  121.0 9.4 %collective-permute-start.16 = (bf16[2,640,128]{2,1,0:T(8,128)(2,1)S(1)}, bf16[2,640,128]{2,1,0:T(8,128)(2,1)S(1)}, u32[]{:S(2)}, u32[]{:S(2)}) collective-permute-start(bf16[2,640,128]{2,1,0:T(8,128)(2,1)S(1)} %collective-permute-done.12.rest_2_), channel_id=1, source_target_pairs={{0,1},{1,0},{2,3},{3,2},{4,5},{5,4},{6,7},{7,6},{8,9},{9,8},{10,11... | collective-permute-start | bytes 983048 | tf_op jit(solution)/shard_map/ppermute | solution.py:48
  128.6 28.0 %copy-start.5 = (bf16[192,1536]{1,0:T(8,128)(2,1)}, bf16[192,1536]{1,0:T(8,128)(2,1)S(1)}, u32[]{:S(2)}) copy-start(bf16[192,1536]{1,0:T(8,128)(2,1)S(1)} %collective-permute-done.21.rest_3_) | copy-start | bytes 1769476
  128.6 28.0 %collective-permute-start.22 = (bf16[192,1536]{1,0:T(8,128)(2,1)S(1)}, bf16[192,1536]{1,0:T(8,128)(2,1)S(1)}, u32[]{:S(2)}, u32[]{:S(2)}) collective-permute-start(bf16[192,1536]{1,0:T(8,128)(2,1)S(1)} %maximum_select_fusion.rest_0_), channel_id=1, source_target_pairs={{0,1},{1,0},{2,3},{3,2},{4,5},{5,4},{6,7},{7,6},{8,9},{9,8},{10,11... | collective-permute-start | bytes 1769480 | tf_op jit(solution)/shard_map/ppermute | solution.py:48
  128.7 27.9 %collective-permute-start.23 = (bf16[192,1536]{1,0:T(8,128)(2,1)S(1)}, bf16[192,1536]{1,0:T(8,128)(2,1)S(1)}, u32[]{:S(2)}, u32[]{:S(2)}) collective-permute-start(bf16[192,1536]{1,0:T(8,128)(2,1)S(1)} %collective-permute-done.19.rest_1_), channel_id=1, source_target_pairs={{0,1},{1,0},{2,3},{3,2},{4,5},{5,4},{6,7},{7,6},{8,9},{9,8},{10,11... | collective-permute-start | bytes 1769480 | tf_op jit(solution)/shard_map/ppermute | solution.py:48
  129.8 3.4 %copy-start.16 = (bf16[2,640,128]{2,1,0:T(8,128)(2,1)}, bf16[2,640,128]{2,1,0:T(8,128)(2,1)S(1)}, u32[]{:S(2)}) copy-start(bf16[2,640,128]{2,1,0:T(8,128)(2,1)S(1)} %collective-permute-done.14.rest_4_) | copy-start | bytes 983044
  129.8 26.8 %collective-permute-start.24 = (bf16[192,1536]{1,0:T(8,128)(2,1)S(1)}, bf16[192,1536]{1,0:T(8,128)(2,1)}, u32[]{:S(2)}, u32[]{:S(2)}) collective-permute-start(bf16[192,1536]{1,0:T(8,128)(2,1)S(1)} %collective-permute-done.20.rest_2_), channel_id=1, source_target_pairs={{0,1},{1,0},{2,3},{3,2},{4,5},{5,4},{6,7},{7,6},{8,9},{9,8},{10,11... | collective-permute-start | bytes 1769480 | tf_op jit(solution)/shard_map/ppermute | solution.py:48
  129.9 3.3 %copy-start.17 = (bf16[2,640,128]{2,1,0:T(8,128)(2,1)}, bf16[2,640,128]{2,1,0:T(8,128)(2,1)S(1)}, u32[]{:S(2)}) copy-start(bf16[2,640,128]{2,1,0:T(8,128)(2,1)S(1)} %collective-permute-done.15.rest_5_) | copy-start | bytes 983044
  129.9 26.7 %collective-permute-start.25 = (bf16[192,1536]{1,0:T(8,128)(2,1)S(1)}, bf16[192,1536]{1,0:T(8,128)(2,1)}, u32[]{:S(2)}, u32[]{:S(2)}) collective-permute-start(bf16[192,1536]{1,0:T(8,128)(2,1)S(1)} %collective-permute-done.21.rest_3_), channel_id=1, source_target_pairs={{0,1},{1,0},{2,3},{3,2},{4,5},{5,4},{6,7},{7,6},{8,9},{9,8},{10,11... | collective-permute-start | bytes 1769480 | tf_op jit(solution)/shard_map/ppermute | solution.py:48
  130.4 2.8 %copy-start.18 = (bf16[2,640,128]{2,1,0:T(8,128)(2,1)}, bf16[2,640,128]{2,1,0:T(8,128)(2,1)S(1)}, u32[]{:S(2)}) copy-start(bf16[2,640,128]{2,1,0:T(8,128)(2,1)S(1)} %collective-permute-done.16.rest_6_) | copy-start | bytes 983044
  130.4 2.8 %collective-permute-start.17 = (bf16[2,640,128]{2,1,0:T(8,128)(2,1)S(1)}, bf16[2,640,128]{2,1,0:T(8,128)(2,1)S(1)}, u32[]{:S(2)}, u32[]{:S(2)}) collective-permute-start(bf16[2,640,128]{2,1,0:T(8,128)(2,1)S(1)} %collective-permute-done.13.rest_3_), channel_id=1, source_target_pairs={{0,1},{1,0},{2,3},{3,2},{4,5},{5,4},{6,7},{7,6},{8,9},{9,8},{10,11... | collective-permute-start | bytes 983048 | tf_op jit(solution)/shard_map/ppermute | solution.py:48
  (6 other events, 6.2 us)

commit v2 on v0

v2 whole, which is shorter than its diff:
```python
import functools
import math

import jax
import jax.numpy as jnp
from jax import lax
from jax.experimental import pallas as pl
from jax.experimental.pallas import tpu as pltpu
from jax.sharding import PartitionSpec as P

HEADS = 8
DK = 128
DV = 192
EPS = 1e-06
BF = jnp.bfloat16
F32 = jnp.float32
AXES = ("dp", "seq")
VMEM_LIMIT = 60 * 1024 * 1024


def place(l):
    dp, s = divmod(l, 16)
    return dp // 2, dp % 2, s // 4, (s // 2) % 2, s % 2


def device(x, yl, z, yh, c):
    return ((x % 4) * 2 + yl) * 16 + (z % 4) * 4 + yh * 2 + c


def moves(f):
    return [(l, device(*f(*place(l)))) for l in range(128)]


def along_x(k):
    return moves(lambda x, yl, z, yh, c: (x + k, yl, z, yh, c))


OTHER_CORE = moves(lambda x, yl, z, yh, c: (x, yl, z, yh, 1 - c))


def send(array, pairs):
    return lax.ppermute(array, AXES, pairs)


def full(shape):
    return pl.BlockSpec(shape, lambda *_: (0,) * len(shape))


ANYWHERE = pl.BlockSpec(memory_space=pl.ANY)
IN_VMEM = pl.BlockSpec(memory_space=pltpu.VMEM)


def conv_kernel(
    x_ref, before_ref, after_ref, cg_ref, bias_ref, ag_ref, w_hbm,
    skip_ref, norm_ref, lhs, raw, wide, act_s, raw_s, w_buf, sems,
):
    n = pl.program_id(0)
    steps = pl.num_programs(0)
    rows, width = skip_ref.shape
    taps, _, tile = w_buf.shape[1:]

    def weights(i):
        cols = pl.ds(pl.multiple_of(i * tile, tile), tile)
        slot = lax.rem(i, 2)
        return pltpu.make_async_copy(w_hbm.at[:, :, cols], w_buf.at[slot], sems.at[slot])

    def activated(v):
        scale = lax.rsqrt(jnp.mean(v * v, axis=-1, keepdims=True) + EPS)
        return jax.nn.gelu(v * scale * cg_ref[...], approximate=True)

    @pl.when(n == 0)
    def _():
        weights(0).start()
        groups, some, lanes = act_s.shape

        def step(i, _):
            at = pl.multiple_of(i * some, some)
            half = pl.ds(pl.multiple_of(i * (some // 2), some // 2), some // 2)
            there = pl.ds(pl.multiple_of(i * (some // 2) + 8, 8), some // 2)
            v = x_ref[pl.ds(at, some), :].astype(F32)
            g = activated(v)
            for k in range(groups):
                cols = slice(k * lanes, (k + 1) * lanes)
                raw_s[k] = v[:, cols]
                act_s[k] = g[:, cols]
                for j in range(2):
                    a = act_s[k, pl.ds(j, some // 2, 2), :]
                    wide[j, there, cols] = a
                    lhs[2 + j, half, cols] = a.astype(BF)
                    raw[j, half, cols] = raw_s[k, pl.ds(j, some // 2, 2), :].astype(BF)
            return 0

        lax.fori_loop(0, x_ref.shape[0] // some, step, 0)
        before = activated(before_ref[...].astype(F32))
        after = activated(after_ref[...].astype(F32))
        for j in range(2):
            wide[j, 7:8, :] = before[j : j + 1]
            wide[j, rows + 8 : rows + 9, :] = after[j : j + 1]
            lhs[j] = wide[j, pl.ds(7, rows), :].astype(BF)
            lhs[4 + j] = wide[j, pl.ds(9, rows), :].astype(BF)

    @pl.when(n + 1 < steps)
    def _():
        weights(n + 1).start()

    weights(n).wait()
    slot = lax.rem(n, 2)
    acc = jnp.zeros((2 * rows, tile), F32)
    for t in range(taps):
        acc = acc + jnp.dot(
            lhs[t : t + 2].reshape(2 * rows, width), w_buf[slot, t], preferred_element_type=F32
        )
    cols = pl.ds(pl.multiple_of(n * tile, tile), tile)
    bias = bias_ref[:, cols]
    even = raw[0, :, cols].astype(F32) + (acc[:rows] + bias)
    odd = raw[1, :, cols].astype(F32) + (acc[rows:] + bias)
    skip_ref[:, cols] = jnp.maximum(even, odd).astype(BF)

    @pl.when(n == steps - 1)
    def _():
        v = skip_ref[...].astype(F32)
        scale = lax.rsqrt(jnp.mean(v * v, axis=-1, keepdims=True) + EPS)
        norm_ref[...] = (v * scale * ag_ref[...]).astype(BF)


def convolve(x, before, after, conv_gain, conv_weight, conv_bias, attn_gain):
    rows, width = x.shape[0] // 2, x.shape[1]
    taps = conv_weight.shape[0]
    tile = 256
    out = jax.ShapeDtypeStruct((rows, width), BF)
    vector = full((1, width))
    return pl.pallas_call(
        conv_kernel,
        out_shape=(out, out),
        grid=(width // tile,),
        in_specs=[full(x.shape), full((2, width)), full((2, width)), vector, vector, vector, ANYWHERE],
        out_specs=(full((rows, width)), full((rows, width))),
        scratch_shapes=[
            pltpu.VMEM((6, rows, width), BF),
            pltpu.VMEM((2, rows, width), BF),
            pltpu.VMEM((2, rows + 16, width), F32),
            pltpu.VMEM((width // 128, 128, 128), F32),
            pltpu.VMEM((width // 128, 128, 128), F32),
            pltpu.VMEM((2, taps, width, tile), BF),
            pltpu.SemaphoreType.DMA((2,)),
        ],
        compiler_params=pltpu.CompilerParams(vmem_limit_bytes=VMEM_LIMIT),
        name="conv",
    )(x, before, after, conv_gain[None], conv_bias[None], attn_gain[None], conv_weight)


def to_same_core(block):
    groups = [[i * 2 + c for i in range(8)] for c in range(2)]
    return lax.all_to_all(block, "seq", 0, 0, tiled=True, axis_index_groups=groups)


def swapped(pieces):
    return [send(p, OTHER_CORE) for p in pieces]


def own_place():
    return lax.axis_index("dp") // 2, lax.rem(lax.axis_index("seq"), 2)


def rows_of_halves(buf, core):
    p = lax.rem(own_place()[0], 2)
    return buf.at[p, :, core], buf.at[1 - p, pl.ds(0, 4), core], buf.at[1 - p, pl.ds(4, 4), core]


def rows_of_quarters(buf, core):
    x = own_place()[0]
    return tuple(buf.at[lax.rem(x + d, 4), :, core] for d in (0, 3, 1, 2))


def fill(rows_of, mine, theirs, buf, sems):
    c = own_place()[1]
    copies = []
    for core, pieces in ((c, mine), (1 - c, theirs)):
        for src, dst in zip(pieces, rows_of(buf, core)):
            copies.append(pltpu.make_async_copy(src, dst, sems.at[len(copies)]))
    for copy in copies:
        copy.start()
    return copies


def pack_kernel(q_hbm, o_hbm, kv_hbm, out_hbm, buf, in_sems, out_sems):
    x, _ = own_place()
    copies, at = [], 0
    for src, index, n in (
        (q_hbm, lax.rem(x, 2), q_hbm.shape[1] // 2),
        (o_hbm, x, o_hbm.shape[1] // 4),
        (kv_hbm, 0, kv_hbm.shape[1]),
    ):
        part = src.at[:, pl.ds(pl.multiple_of(index * n, 128), n)] if src is not kv_hbm else src
        copies.append(
            pltpu.make_async_copy(part, buf.at[:, pl.ds(at, n)], in_sems.at[len(copies)])
        )
        at += n
    for copy in copies:
        copy.start()
    for copy in copies:
        copy.wait()
    copies = [
        pltpu.make_async_copy(buf, out_hbm.at[i], out_sems.at[i]) for i in range(out_hbm.shape[0])
    ]
    for copy in copies:
        copy.start()
    for copy in copies:
        copy.wait()


def pack(q_weight, o_weight, kv_weight):
    rows = q_weight.shape[0]
    n = q_weight.shape[1] // 2 + o_weight.shape[1] // 4 + kv_weight.shape[1]
    return pl.pallas_call(
        pack_kernel,
        out_shape=jax.ShapeDtypeStruct((8, rows, n), BF),
        in_specs=[ANYWHERE] * 3,
        out_specs=ANYWHERE,
        scratch_shapes=[
            pltpu.VMEM((rows, n), BF),
            pltpu.SemaphoreType.DMA((3,)),
            pltpu.SemaphoreType.DMA((8,)),
        ],
        compiler_params=pltpu.CompilerParams(vmem_limit_bytes=VMEM_LIMIT),
        name="pack",
    )(q_weight, o_weight, kv_weight)


def rotated(v, c, s):
    return v * c + pltpu.roll(v, DK // 2, 1) * s


def kv_kernel(norm_ref, cos_ref, sin_ref, own, other, kv_ref, buf, sems):
    _, c = own_place()
    copies = [
        pltpu.make_async_copy(
            own.at[:, :, pl.ds(own.shape[2] - other.shape[2], other.shape[2])],
            buf.at[:, c],
            sems.at[0],
        ),
        pltpu.make_async_copy(other, buf.at[:, 1 - c], sems.at[1]),
    ]
    for copy in copies:
        copy.start()
    for copy in copies:
        copy.wait()
    x = norm_ref[...]
    rows, width = x.shape
    kv = jnp.dot(x, buf[...].reshape(width, buf.shape[-1]), preferred_element_type=F32)
    tail = kv[:, 2 * DK :]
    packed = jnp.concatenate(
        [
            rotated(kv[:, :DK], cos_ref[...], sin_ref[...]),
            kv[:, DK : 2 * DK],
            jnp.concatenate([tail[: rows // 2], tail[rows // 2 :]], axis=1),
        ],
        axis=0,
    ).astype(BF)
    for i in range(kv_ref.shape[0]):
        kv_ref[i] = packed


def key_values(normed, cosine, sine, own, other):
    rows = normed.shape[0]
    return pl.pallas_call(
        kv_kernel,
        out_shape=jax.ShapeDtypeStruct((8, rows * 5 // 2, DK), BF),
        in_specs=[IN_VMEM, IN_VMEM, IN_VMEM, ANYWHERE, ANYWHERE],
        scratch_shapes=[
            pltpu.VMEM((8, 2, *other.shape[1:]), BF),
            pltpu.SemaphoreType.DMA((2,)),
        ],
        compiler_params=pltpu.CompilerParams(vmem_limit_bytes=VMEM_LIMIT),
        name="key_values",
    )(normed, cosine, sine, own, other)


def query_kernel(norm_ref, cos_ref, sin_ref, *rest):
    gathered, *pieces = rest[:6]
    q_ref, buf, sems = rest[6:]
    mine = [gathered.at[:, :, pl.ds(0, buf.shape[-1])], *pieces[:2]]
    for copy in fill(rows_of_halves, mine, pieces[2:], buf, sems):
        copy.wait()
    x = norm_ref[...]
    width = x.shape[1]
    c, s = cos_ref[...], sin_ref[...]
    per = buf.shape[-1] // DK
    for p in range(2):
        y = jnp.dot(x, buf[p].reshape(width, per * DK), preferred_element_type=F32)
        for h in range(per):
            q_ref[p * per + h] = rotated(y[:, h * DK : (h + 1) * DK], c, s).astype(BF)


def queries(normed, cosine, sine, pieces):
    rows, _ = normed.shape
    return pl.pallas_call(
        query_kernel,
        out_shape=jax.ShapeDtypeStruct((HEADS, rows, DK), BF),
        in_specs=[IN_VMEM, IN_VMEM, IN_VMEM] + [ANYWHERE] * 6,
        scratch_shapes=[
            pltpu.VMEM((2, 8, 2, *pieces[1].shape[1:]), BF),
            pltpu.SemaphoreType.DMA((6,)),
        ],
        compiler_params=pltpu.CompilerParams(vmem_limit_bytes=VMEM_LIMIT),
        name="queries",
    )(normed, cosine, sine, *pieces)


def attention_kernel(
    q_ref, own, other, out_ref, kbuf, vbuf, tails, even_s, odd_s, peak, heads_s, sems
):
    heads, rows, _ = q_ref.shape
    slabs = kbuf.shape[0]
    half = rows // 2
    copies = []
    for i, part in enumerate((own, other)):
        to = pl.ds(i * (slabs // 2), slabs // 2)
        for lo, size, dst in (
            (0, rows, kbuf.at[to]),
            (rows, rows, vbuf.at[to, :, pl.ds(0, DK)]),
            (2 * rows, half, tails.at[to]),
        ):
            copies.append(
                pltpu.make_async_copy(part.at[:, pl.ds(lo, size), :], dst, sems.at[len(copies)])
            )
    for copy in copies:
        copy.start()
    for copy in copies:
        copy.wait()
    lane = lax.broadcasted_iota(jnp.int32, (half, DK), 1)
    ones = jnp.where(lane == DK // 2, 1.0, 0.0)
    for i in range(slabs):
        t = tails[i].astype(F32)
        vbuf[i, :half, DK:] = jnp.where(lane < DK // 2, t, ones).astype(BF)
        vbuf[i, half:, DK:] = jnp.where(
            lane < DK // 2, pltpu.roll(t, DK // 2, 1), ones
        ).astype(BF)

    chunks, _, chunk = even_s.shape
    n = chunk // rows
    scale = DK ** (-0.5) * math.log2(math.e)
    lowest = jnp.full((rows, DK), -jnp.inf, F32)

    def make_scores(head, to):
        top = lowest
        for kc in range(chunks):
            k = kbuf[kc * n : (kc + 1) * n].reshape(chunk, DK)
            s = lax.dot_general(
                q_ref[head], k, (((1,), (1,)), ((), ())), preferred_element_type=F32
            )
            to[kc] = s
            for j in range(chunk // DK):
                top = jnp.maximum(top, s[:, j * DK : (j + 1) * DK])
        return jnp.broadcast_to(jnp.max(top, axis=-1, keepdims=True), (rows, DK))

    def use_scores(head, scores, m):
        total = jnp.zeros((rows, 2 * DK), F32)
        for kc in range(chunks):
            s = scores[kc]
            w = jnp.concatenate(
                [jnp.exp2((s[:, j * DK : (j + 1) * DK] - m) * scale) for j in range(chunk // DK)],
                axis=1,
            ).astype(BF)
            v = vbuf[kc * n : (kc + 1) * n].reshape(chunk, 2 * DK)
            total = total + jnp.dot(w, v, preferred_element_type=F32)
        heads_s[head] = total[:, :DV] / total[:, DV : DV + 1]

    peak[...] = make_scores(0, even_s)

    def step(i, _):
        head = 2 * i
        m = peak[...]
        above = make_scores(head + 1, odd_s)
        use_scores(head, even_s, m)
        peak[...] = make_scores(head + 2, even_s)
        use_scores(head + 1, odd_s, above)
        return 0

    lax.fori_loop(0, heads // 2 - 1, step, 0)
    m = peak[...]
    above = make_scores(heads - 1, odd_s)
    use_scores(heads - 2, even_s, m)
    use_scores(heads - 1, odd_s, above)
    for h in range(0, heads, 2):
        out_ref[:, h * DV : (h + 2) * DV] = jnp.concatenate(
            [heads_s[h], heads_s[h + 1]], axis=1
        ).astype(BF)


def attention(q, own, other):
    heads, rows, _ = q.shape
    slabs = 2 * own.shape[0]
    tokens = slabs * rows
    chunk = 2048
    return pl.pallas_call(
        attention_kernel,
        out_shape=jax.ShapeDtypeStruct((rows, heads * DV), BF),
        in_specs=[IN_VMEM, ANYWHERE, ANYWHERE],
        scratch_shapes=[
            pltpu.VMEM((slabs, rows, DK), BF),
            pltpu.VMEM((slabs, rows, 2 * DK), BF),
            pltpu.VMEM((slabs, rows // 2, DK), BF),
            pltpu.VMEM((tokens // chunk, rows, chunk), F32),
            pltpu.VMEM((tokens // chunk, rows, chunk), F32),
            pltpu.VMEM((rows, DK), F32),
            pltpu.VMEM((heads, rows, DV), F32),
            pltpu.SemaphoreType.DMA((6,)),
        ],
        compiler_params=pltpu.CompilerParams(vmem_limit_bytes=VMEM_LIMIT),
        name="attention",
    )(q, own, other)


def output_kernel(mixed_ref, skip_ref, *rest):
    pieces, (out_ref, buf, sems) = rest[:8], rest[8:]
    copies = fill(rows_of_quarters, pieces[:4], pieces[4:], buf, sems)
    x, _ = own_place()
    tile = buf.shape[-1]
    left = mixed_ref[...]
    for i, d in enumerate((0, 3, 1, 2)):
        copies[i].wait()
        copies[4 + i].wait()
        p = lax.rem(x + d, 4)
        cols = pl.ds(pl.multiple_of(p * tile, tile), tile)
        y = jnp.dot(left, buf[p].reshape(left.shape[1], tile), preferred_element_type=F32)
        out_ref[:, cols] = (skip_ref[:, cols].astype(F32) + y).astype(BF)


def output(mixed, skip, pieces):
    rows, width = skip.shape
    return pl.pallas_call(
        output_kernel,
        out_shape=jax.ShapeDtypeStruct((rows, width), BF),
        in_specs=[IN_VMEM, IN_VMEM] + [ANYWHERE] * 8,
        scratch_shapes=[
            pltpu.VMEM((4, 8, 2, *pieces[0].shape[1:]), BF),
            pltpu.SemaphoreType.DMA((8,)),
        ],
        compiler_params=pltpu.CompilerParams(vmem_limit_bytes=VMEM_LIMIT),
        name="output",
    )(mixed, skip, *pieces)


def rotation(seq, rows):
    half = DK // 2
    freqs = jnp.power(10000.0, -jnp.arange(half, dtype=F32) / half)
    positions = seq * rows + jnp.arange(rows, dtype=jnp.int32)
    angle = positions.astype(F32)[:, None] * freqs[None, :]
    c, s = jnp.cos(angle), jnp.sin(angle)
    return jnp.concatenate([c, c], 1), jnp.concatenate([-s, s], 1)


def tied(value, *after):
    return lax.optimization_barrier((value, *after))[0]


def halos(x, seq):
    core = seq % 2
    first, last = x[:2], x[-2:]
    ends = [(l, l + 1) for l in range(128) if l % 2 and l % 16 != 15]
    outer = send(jnp.where(core == 0, first, last), ends + [(j, i) for i, j in ends])
    inner = send(jnp.where(core == 0, last, first), OTHER_CORE)
    return jnp.where(core == 0, outer, inner), jnp.where(core == 0, inner, outer)


def body(x, conv_gain, conv_weight, conv_bias, attn_gain, q_weight, kv_weight, o_weight):
    rows = x.shape[0] // 2
    seq = lax.axis_index("seq")
    qn, on = q_weight.shape[1] // 2, o_weight.shape[1] // 4
    before, after = halos(x, seq)
    block = pack(q_weight, o_weight, kv_weight)
    block, before, after = lax.optimization_barrier((block, before, after))
    block = to_same_core(block)
    skip, normed = convolve(x, before, after, conv_gain, conv_weight, conv_bias, attn_gain)
    cosine, sine = rotation(seq, rows)
    block = tied(block, normed)
    kv = key_values(
        normed, cosine, sine, block, send(block[:, :, qn + on :], OTHER_CORE)
    )
    kv_same = to_same_core(kv)
    q_own = tied(block, kv)[:, :, :qn]
    q_parts = [send(q_own[:4], along_x(1)), send(q_own[4:], along_x(-1))]
    o_own = tied(block, kv)[:, :, qn : qn + on]
    o_parts = [o_own, send(o_own, along_x(1)), send(o_own, along_x(-1))]
    o_parts.append(send(tied(o_own, *q_parts), along_x(2)))
    q = queries(normed, cosine, sine, [block, *q_parts, *swapped([q_own, *q_parts])])
    kv_same = tied(kv_same, q)
    mixed = attention(q, kv_same, send(kv_same, OTHER_CORE))
    *o_parts, mixed = lax.optimization_barrier((*o_parts, mixed))
    return skip, output(mixed, skip, o_parts + swapped(o_parts))


def solution(mesh):
    rows = P(("dp", "seq"), None)
    in_specs = (rows, P(), P(), P(), P(), P("seq", None), P("seq", None), P("seq", None))
    return jax.shard_map(
        body, mesh=mesh, in_specs=in_specs, out_specs=(rows, rows), check_vma=False
    )
```

time: 177 us -> 124 us (0.70)
  matrix products: 64 us -> 0 us
  Pallas kernels: 0 us -> 53 us
  other arithmetic: 28.6 us -> 2.78 us
  starting transfers between devices: 12 us -> 30.3 us
  waiting for transfers between devices: 45.3 us -> 28.5 us
  between operations: 14.3 us -> 1.03 us
  local copies, waits for them, and re-layouts: 11.8 us -> 7.49 us
    dot_general x10 -> x0, matrix products: 64 us -> none  [the longest x5 23.9 us: body(): jnp.dot(padded[kernel_tap:kernel_tap + pos_rows], conv_weight[kernel_tap]...]
    pallas_call x0 -> x6, Pallas kernels: none -> 53 us  [the longest x1 20.5 us: convolve(): pl.pallas_call(conv_kernel, out_shape=(out, out), grid=(width // tile,),...]
    all_to_all x1 -> x2, waiting for transfers between devices: 26.6 us -> 4.59 us  [to_same_core(): lax.all_to_all(block, 'seq', 0, 0, tiled=True, axis_index_groups=groups)]
    ppermute x2 -> x16, waiting for transfers between devices: 4.49 us -> 23.9 us  [send(): return lax.ppermute(array, AXES, pairs)]
    reduce_sum x3 -> x0, other arithmetic: 16.6 us -> none  [the longest x1 14.3 us: body(): total_new = jnp.sum(weights, axis=-1)]
    all_gather x2 -> x0, waiting for transfers between devices: 13.5 us -> none  [the longest x1 13.5 us: in_one_piece(): lax.all_gather(both, axis, axis=dim, tiled=True)]
    ppermute x2 -> x16, starting transfers between devices: 8.13 us -> 19.5 us  [send(): return lax.ppermute(array, AXES, pairs)]
    all_to_all x1 -> x2, starting transfers between devices: 3.77 us -> 10.8 us  [to_same_core(): lax.all_to_all(block, 'seq', 0, 0, tiled=True, axis_index_groups=groups)]
  transfers between devices with their start and end apart: 5 -> 18, of which waited for: 3 -> 10; matrix products, arithmetic and copies ran while one was open for 53% -> 4% of each run, Pallas kernels for 0% -> 34%
where the time goes in v2:
time: 124 us; the launch traced here: 123 us
  Pallas kernels  53 us (43%)
  starting transfers between devices  30.3 us (24%)
  waiting for transfers between devices  28.5 us (23%)
  local copies, waits for them, and re-layouts  7.49 us (6%)
  other arithmetic  2.78 us (2%)
    ppermute x16, waiting for transfers between devices, send(): return lax.ppermute(array, AXES, pairs)  23.9 us
    pallas_call x1, Pallas kernels, convolve(): pl.pallas_call(conv_kernel, out_shape=(out, out), grid=(width // tile,),...  20.5 us
    ppermute x16, starting transfers between devices, send(): return lax.ppermute(array, AXES, pairs)  19.5 us
    pallas_call x1, Pallas kernels, attention(): pl.pallas_call(attention_kernel, out_shape=jax.ShapeDtypeStruct((rows, he...  14.4 us
    all_to_all x2, starting transfers between devices, to_same_core(): lax.all_to_all(block, 'seq', 0, 0, tiled=True, axis_index_groups=groups)  10.8 us
    pallas_call x1, Pallas kernels, output(): pl.pallas_call(output_kernel, out_shape=jax.ShapeDtypeStruct((rows, width...  6.45 us
    pallas_call x1, Pallas kernels, queries(): pl.pallas_call(query_kernel, out_shape=jax.ShapeDtypeStruct((HEADS, rows,...  5.01 us
    all_to_all x2, waiting for transfers between devices, to_same_core(): lax.all_to_all(block, 'seq', 0, 0, tiled=True, axis_index_groups=groups)  4.59 us
  transfers between devices with their start and end apart: 18, of which 10 were waited for; matrix products, arithmetic and copies ran while one was open for 4% of the time, Pallas kernels for 34%

profile of v2, /device:TPU:1, one launch (start us, length us, event | category | flops | bytes accessed | tf_op | source)
XLA Modules:
  0.0 123.1 jit_solution(3994355521992186049)
XLA Ops:
  0.6 0.8 broadcast_select_fusion.2
  1.4 6.2 %collective-permute-start = (bf16[2,1536]{1,0:T(2,128)(2,1)S(1)}, bf16[2,1536]{1,0:T(2,128)(2,1)S(1)}, u32[]{:S(2)}, u32[]{:S(2)}) collective-permute-start(bf16[2,1536]{1,0:T(2,128)(2,1)S(1)} %get-tuple-element.33), channel_id=1, source_target_pairs={{1,2},{3,4},{5,6},{7,8},{9,10},{11,12},{13,14},{17,18},{19,20},{21... | collective-permute-start | bytes 18440 | tf_op jit(solution)/shard_map/ppermute | solution.py:42
  7.6 0.1 collective-permute-start.1
  7.7 2.4 %pack.1 = bf16[8,96,1216]{2,1,0:T(8,128)(2,1)} custom-call(bf16[96,1024]{1,0:T(8,128)(2,1)} %q_hbm.1, bf16[96,1536]{1,0:T(8,128)(2,1)} %o_hbm.1, bf16[96,320]{1,0:T(8,128)(2,1)} %kv_hbm.1), custom_call_target="tpu_custom_call" | custom-call | tf_op jit(solution)/shard_map/pack/pallas_call | solution.py:215
  10.2 0.6 broadcast_select_fusion
  10.8 7.1 %all-to-all-start = ((bf16[8,96,1216]{2,1,0:T(8,128)(2,1)}), bf16[8,96,1216]{2,1,0:T(8,128)(2,1)S(1)}, u32[]{:S(2)}, u32[]{:S(2)}) async-start(bf16[8,96,1216]{2,1,0:T(8,128)(2,1)} %pack.1), calls=%async_computation | async-start | bytes 3932160 | tf_op jit(solution)/shard_map/all_to_all | solution.py:154
  17.9 0.6 broadcast_in_dim.11.cg_ref
  18.5 0.6 broadcast_in_dim.12.bias_ref
  19.1 0.6 broadcast_in_dim.13.ag_ref
  19.7 20.5 %conv.1 = (bf16[256,1536]{1,0:T(8,128)(2,1)}, bf16[256,1536]{1,0:T(8,128)(2,1)}) custom-call(bf16[512,1536]{1,0:T(8,128)(2,1)} %x_ref.1, bf16[2,1536]{1,0:T(2,128)(2,1)} %get-tuple-element.16.before_ref, bf16[2,1536]{1,0:T(2,128)(2,1)} %get-tuple-element.17.after_ref, f32[1,1536]{1,0:T(1,128)} %broadcast_in_dim.11.cg_ref, ...), custom_call_target="tpu_custom_call" | custom-call | tf_op jit(solution)/shard_map/conv/pallas_call | solution.py:132
  40.2 4.6 %all-to-all-done.own.rest_0_ = bf16[8,96,1216]{2,1,0:T(8,128)(2,1)S(1)} async-done(((bf16[8,96,1216]{2,1,0:T(8,128)(2,1)}), bf16[8,96,1216]{2,1,0:T(8,128)(2,1)S(1)}, u32[]{:S(2)}, u32[]{:S(2)}) %all-to-all-start) | async-done | bytes 1867808 | tf_op jit(solution)/shard_map/all_to_all | solution.py:154
  44.8 0.1 slice.25
  44.9 1.1 collective-permute-start.2
  46.1 0.5 fusion
  46.6 0.8 pad_maximum_fusion
  47.4 0.2 collective-permute-done.2.other
  47.7 0.8 copy-done.8
  48.5 4.2 %key_values.1 = bf16[8,640,128]{2,1,0:T(8,128)(2,1)} custom-call(bf16[256,1536]{1,0:T(8,128)(2,1)} %get-tuple-element.20.norm_ref, f32[256,128]{1,0:T(8,128)} %get-tuple-element.39.cos_ref, f32[256,128]{1,0:T(8,128)} %get-tuple-element.40.sin_ref, bf16[8,96,1216]{2,1,0:T(8,128)(2,1)} %copy-done, bf16[8,96,320]{2,1,0:T(8,128)(2,1)} %copy-done.8), custom_call_target="tpu_custom_call" | custom-call | tf_op jit(solution)/shard_map/key_values/pallas_call | solution.py:266
  52.7 3.7 %all-to-all-start.1 = ((bf16[8,640,128]{2,1,0:T(8,128)(2,1)}), bf16[8,640,128]{2,1,0:T(8,128)(2,1)S(1)}, u32[]{:S(2)}, u32[]{:S(2)}) async-start(bf16[8,640,128]{2,1,0:T(8,128)(2,1)} %key_values.1), calls=%async_computation.1 | async-start | bytes 2621440 | tf_op jit(solution)/shard_map/all_to_all | solution.py:154
  56.4 0.1 fusion.1
  56.5 2.5 %collective-permute-start.6 = (bf16[4,96,512]{2,1,0:T(8,128)(2,1)S(1)}, bf16[4,96,512]{2,1,0:T(8,128)(2,1)S(1)}, u32[]{:S(2)}, u32[]{:S(2)}) collective-permute-start(bf16[4,96,512]{2,1,0:T(8,128)(2,1)S(1)} %get-tuple-element.30), channel_id=1, source_target_pairs={{0,96},{1,97},{2,98},{3,99},{4,100},{5,101},{6,102},{7,103},{8,104... | collective-permute-start | bytes 1179656 | tf_op jit(solution)/shard_map/ppermute | solution.py:42
  59.1 0.1 slice.29
  59.1 0.7 collective-permute-start.8
  59.9 7.3 %collective-permute-done.6.rest_2_ = bf16[4,96,512]{2,1,0:T(8,128)(2,1)S(1)} collective-permute-done((bf16[4,96,512]{2,1,0:T(8,128)(2,1)S(1)}, bf16[4,96,512]{2,1,0:T(8,128)(2,1)S(1)}, u32[]{:S(2)}, u32[]{:S(2)}) %collective-permute-start.6) | collective-permute-done | bytes 393248 | tf_op jit(solution)/shard_map/ppermute | solution.py:42
  67.2 1.2 collective-permute-start.10
  68.4 1.9 %collective-permute-done.5.rest_1_ = bf16[4,96,512]{2,1,0:T(8,128)(2,1)S(1)} collective-permute-done((bf16[4,96,512]{2,1,0:T(8,128)(2,1)S(1)}, bf16[4,96,512]{2,1,0:T(8,128)(2,1)S(1)}, u32[]{:S(2)}, u32[]{:S(2)}) %collective-permute-start.5) | collective-permute-done | bytes 393248 | tf_op jit(solution)/shard_map/ppermute | solution.py:42
  70.3 1.5 %collective-permute-start.9 = (bf16[4,96,512]{2,1,0:T(8,128)(2,1)S(1)}, bf16[4,96,512]{2,1,0:T(8,128)(2,1)S(1)}, u32[]{:S(2)}, u32[]{:S(2)}) collective-permute-start(bf16[4,96,512]{2,1,0:T(8,128)(2,1)S(1)} %collective-permute-done.5.rest_1_), channel_id=1, source_target_pairs={{0,1},{1,0},{2,3},{3,2},{4,5},{5,4},{6,7},{7,6},{8,9},{9,8},{10,11... | collective-permute-start | bytes 1179656 | tf_op jit(solution)/shard_map/ppermute | solution.py:42
  71.8 1.3 %collective-permute-done.9.rest_4_ = bf16[4,96,512]{2,1,0:T(8,128)(2,1)S(1)} collective-permute-done((bf16[4,96,512]{2,1,0:T(8,128)(2,1)S(1)}, bf16[4,96,512]{2,1,0:T(8,128)(2,1)S(1)}, u32[]{:S(2)}, u32[]{:S(2)}) %collective-permute-start.9) | collective-permute-done | bytes 393248 | tf_op jit(solution)/shard_map/ppermute | solution.py:42
  73.2 0.7 copy-done.14
  73.9 0.9 copy-done.5
  74.8 5.0 %queries.1.q_ref = bf16[8,256,128]{2,1,0:T(8,128)(2,1)} custom-call(bf16[256,1536]{1,0:T(8,128)(2,1)} %get-tuple-element.20.norm_ref, f32[256,128]{1,0:T(8,128)} %get-tuple-element.39.cos_ref, f32[256,128]{1,0:T(8,128)} %get-tuple-element.40.sin_ref, bf16[8,96,1216]{2,1,0:T(8,128)(2,1)} %copy-done, bf16[4,96,512]{2,1,0:T(8,128)(2,1)} %copy-done.12, ...), custom_call_target="tpu_custom_call" | custom-call | tf_op jit(solution)/shard_map/queries/pallas_call | solution.py:297
  79.8 0.5 collective-permute-start.11
  80.3 1.1 slice.26.rest_0_
  81.4 0.1 collective-permute-start.3
  81.5 2.7 %collective-permute-start.4 = (bf16[8,96,384]{2,1,0:T(8,128)(2,1)S(1)}, bf16[8,96,384]{2,1,0:T(8,128)(2,1)}, u32[]{:S(2)}, u32[]{:S(2)}) collective-permute-start(bf16[8,96,384]{2,1,0:T(8,128)(2,1)S(1)} %slice.26.rest_0_), channel_id=1, source_target_pairs={{0,96},{1,97},{2,98},{3,99},{4,100},{5,101},{6,102},{7,103},{8,104... | collective-permute-start | bytes 1769480 | tf_op jit(solution)/shard_map/ppermute | solution.py:42
  84.2 1.1 copy-done.4
  85.3 14.4 %attention.1.mixed_ref = bf16[256,1536]{1,0:T(8,128)(2,1)} custom-call(bf16[8,256,128]{2,1,0:T(8,128)(2,1)} %queries.1.q_ref, bf16[8,640,128]{2,1,0:T(8,128)(2,1)} %copy-done.2, bf16[8,640,128]{2,1,0:T(8,128)(2,1)} %copy-done.4), custom_call_target="tpu_custom_call" | custom-call | tf_op jit(solution)/shard_map/attention/pallas_call | solution.py:396
  99.8 9.3 %collective-permute-done.7.rest_3_ = bf16[8,96,384]{2,1,0:T(8,128)(2,1)} collective-permute-done((bf16[8,96,384]{2,1,0:T(8,128)(2,1)S(1)}, bf16[8,96,384]{2,1,0:T(8,128)(2,1)}, u32[]{:S(2)}, u32[]{:S(2)}) %collective-permute-start.7) | collective-permute-done | bytes 589856 | tf_op jit(solution)/shard_map/ppermute | solution.py:42
  109.1 2.2 %collective-permute-start.12 = (bf16[8,96,384]{2,1,0:T(8,128)(2,1)S(1)}, bf16[8,96,384]{2,1,0:T(8,128)(2,1)S(1)}, u32[]{:S(2)}, u32[]{:S(2)}) collective-permute-start(bf16[8,96,384]{2,1,0:T(8,128)(2,1)S(1)} %slice.26.rest_0_), channel_id=1, source_target_pairs={{0,1},{1,0},{2,3},{3,2},{4,5},{5,4},{6,7},{7,6},{8,9},{9,8},{10,11... | collective-permute-start | bytes 1769480 | tf_op jit(solution)/shard_map/ppermute | solution.py:42
  111.3 0.1 collective-permute-start.13
  111.4 0.4 collective-permute-start.14
  111.8 0.1 collective-permute-start.15
  111.9 1.0 collective-permute-done.12.rest_4_
  112.9 1.1 collective-permute-done.13.rest_5_
  114.0 0.8 collective-permute-done.14.rest_6_
  114.8 0.8 collective-permute-done.15.rest_7_
  115.7 0.8 copy-done.10
  116.5 6.4 %output.1 = bf16[256,1536]{1,0:T(8,128)(2,1)} custom-call(bf16[256,1536]{1,0:T(8,128)(2,1)} %attention.1.mixed_ref, bf16[256,1536]{1,0:T(8,128)(2,1)} %get-tuple-element.14.skip_ref, bf16[8,96,384]{2,1,0:T(8,128)(2,1)} %copy-done.3, bf16[8,96,384]{2,1,0:T(8,128)(2,1)} %collective-permute-done.3.rest_1_, bf16[8,96,384]{2,1,0:T(8,128)(2,1)} %collective-permute-done.4.rest_2_, ...), custom_call_target="tpu_custom_call" | custom-call | tf_op jit(solution)/shard_map/output/pallas_call | solution.py:432
  (43 shorter events, 0.1 us)
Async XLA Ops:
  1.4 8.7 %collective-permute-start = (bf16[2,1536]{1,0:T(2,128)(2,1)S(1)}, bf16[2,1536]{1,0:T(2,128)(2,1)S(1)}, u32[]{:S(2)}, u32[]{:S(2)}) collective-permute-start(bf16[2,1536]{1,0:T(2,128)(2,1)S(1)} %get-tuple-element.33), channel_id=1, source_target_pairs={{1,2},{3,4},{5,6},{7,8},{9,10},{11,12},{13,14},{17,18},{19,20},{21... | collective-permute-start | bytes 18440 | tf_op jit(solution)/shard_map/ppermute | solution.py:42
  7.6 2.5 %collective-permute-start.1 = (bf16[2,1536]{1,0:T(2,128)(2,1)S(1)}, bf16[2,1536]{1,0:T(2,128)(2,1)S(1)}, u32[]{:S(2)}, u32[]{:S(2)}) collective-permute-start(bf16[2,1536]{1,0:T(2,128)(2,1)S(1)} %get-tuple-element.32), channel_id=1, source_target_pairs={{0,1},{1,0},{2,3},{3,2},{4,5},{5,4},{6,7},{7,6},{8,9},{9,8},{10,11... | collective-permute-start | bytes 18440 | tf_op jit(solution)/shard_map/ppermute | solution.py:42
  10.8 7.1 %copy-start.15 = (f32[1536]{0:T(1024)S(1)}, f32[1536]{0:T(1024)}, u32[]{:S(2)}) copy-start(f32[1536]{0:T(1024)} %param.9) | copy-start | bytes 18436
  10.8 7.7 %copy-start.16 = (f32[1536]{0:T(1024)S(1)}, f32[1536]{0:T(1024)}, u32[]{:S(2)}) copy-start(f32[1536]{0:T(1024)} %param.11) | copy-start | bytes 18436
  10.8 8.3 %copy-start.17 = (f32[1536]{0:T(1024)S(1)}, f32[1536]{0:T(1024)}, u32[]{:S(2)}) copy-start(f32[1536]{0:T(1024)} %param.12) | copy-start | bytes 18436
  10.8 34.1 %all-to-all-start = ((bf16[8,96,1216]{2,1,0:T(8,128)(2,1)}), bf16[8,96,1216]{2,1,0:T(8,128)(2,1)S(1)}, u32[]{:S(2)}, u32[]{:S(2)}) async-start(bf16[8,96,1216]{2,1,0:T(8,128)(2,1)} %pack.1), calls=%async_computation | async-start | bytes 3932160 | tf_op jit(solution)/shard_map/all_to_all | solution.py:154
  44.8 2.8 %copy-start = (bf16[8,96,1216]{2,1,0:T(8,128)(2,1)}, bf16[8,96,1216]{2,1,0:T(8,128)(2,1)S(1)}, u32[]{:S(2)}) copy-start(bf16[8,96,1216]{2,1,0:T(8,128)(2,1)S(1)} %all-to-all-done.own.rest_0_) | copy-start | bytes 5603332
  44.9 2.8 %collective-permute-start.2 = (bf16[8,96,320]{2,1,0:T(8,128)(2,1)S(1)}, bf16[8,96,320]{2,1,0:T(8,128)(2,1)S(1)}, u32[]{:S(2)}, u32[]{:S(2)}) collective-permute-start(bf16[8,96,320]{2,1,0:T(8,128)(2,1)S(1)} %slice.25), channel_id=1, source_target_pairs={{0,1},{1,0},{2,3},{3,2},{4,5},{5,4},{6,7},{7,6},{8,9},{9,8},{10,11... | collective-permute-start | bytes 1474568 | tf_op jit(solution)/shard_map/ppermute | solution.py:42
  47.7 0.8 copy-start.8
  52.7 3.7 %copy-start.1 = (bf16[8,96,1216]{2,1,0:T(8,128)(2,1)S(1)}, bf16[8,96,1216]{2,1,0:T(8,128)(2,1)}, u32[]{:S(2)}) copy-start(bf16[8,96,1216]{2,1,0:T(8,128)(2,1)} %copy-done) | copy-start | bytes 5603332
  52.7 27.1 %all-to-all-start.1 = ((bf16[8,640,128]{2,1,0:T(8,128)(2,1)}), bf16[8,640,128]{2,1,0:T(8,128)(2,1)S(1)}, u32[]{:S(2)}, u32[]{:S(2)}) async-start(bf16[8,640,128]{2,1,0:T(8,128)(2,1)} %key_values.1), calls=%async_computation.1 | async-start | bytes 2621440 | tf_op jit(solution)/shard_map/all_to_all | solution.py:154
  56.5 10.7 %collective-permute-start.6 = (bf16[4,96,512]{2,1,0:T(8,128)(2,1)S(1)}, bf16[4,96,512]{2,1,0:T(8,128)(2,1)S(1)}, u32[]{:S(2)}, u32[]{:S(2)}) collective-permute-start(bf16[4,96,512]{2,1,0:T(8,128)(2,1)S(1)} %get-tuple-element.30), channel_id=1, source_target_pairs={{0,96},{1,97},{2,98},{3,99},{4,100},{5,101},{6,102},{7,103},{8,104... | collective-permute-start | bytes 1179656 | tf_op jit(solution)/shard_map/ppermute | solution.py:42
  59.0 11.2 %collective-permute-start.5 = (bf16[4,96,512]{2,1,0:T(8,128)(2,1)S(1)}, bf16[4,96,512]{2,1,0:T(8,128)(2,1)S(1)}, u32[]{:S(2)}, u32[]{:S(2)}) collective-permute-start(bf16[4,96,512]{2,1,0:T(8,128)(2,1)S(1)} %get-tuple-element.31), channel_id=1, source_target_pairs={{0,32},{1,33},{2,34},{3,35},{4,36},{5,37},{6,38},{7,39},{8,40},{9,... | collective-permute-start | bytes 1179656 | tf_op jit(solution)/shard_map/ppermute | solution.py:42
  59.1 14.0 %collective-permute-start.8 = (bf16[8,96,512]{2,1,0:T(8,128)(2,1)S(1)}, bf16[8,96,512]{2,1,0:T(8,128)(2,1)S(1)}, u32[]{:S(2)}, u32[]{:S(2)}) collective-permute-start(bf16[8,96,512]{2,1,0:T(8,128)(2,1)S(1)} %slice.29), channel_id=1, source_target_pairs={{0,1},{1,0},{2,3},{3,2},{4,5},{5,4},{6,7},{7,6},{8,9},{9,8},{10,11... | collective-permute-start | bytes 2359304 | tf_op jit(solution)/shard_map/ppermute | solution.py:42
  67.2 6.0 %copy-start.11 = (bf16[4,96,512]{2,1,0:T(8,128)(2,1)}, bf16[4,96,512]{2,1,0:T(8,128)(2,1)S(1)}, u32[]{:S(2)}) copy-start(bf16[4,96,512]{2,1,0:T(8,128)(2,1)S(1)} %collective-permute-done.6.rest_2_) | copy-start | bytes 1179652
  67.2 4.6 %collective-permute-start.10 = (bf16[4,96,512]{2,1,0:T(8,128)(2,1)S(1)}, bf16[4,96,512]{2,1,0:T(8,128)(2,1)S(1)}, u32[]{:S(2)}, u32[]{:S(2)}) collective-permute-start(bf16[4,96,512]{2,1,0:T(8,128)(2,1)S(1)} %collective-permute-done.6.rest_2_), channel_id=1, source_target_pairs={{0,1},{1,0},{2,3},{3,2},{4,5},{5,4},{6,7},{7,6},{8,9},{9,8},{10,11... | collective-permute-start | bytes 1179656 | tf_op jit(solution)/shard_map/ppermute | solution.py:42
  70.3 1.5 %copy-start.12 = (bf16[4,96,512]{2,1,0:T(8,128)(2,1)}, bf16[4,96,512]{2,1,0:T(8,128)(2,1)S(1)}, u32[]{:S(2)}) copy-start(bf16[4,96,512]{2,1,0:T(8,128)(2,1)S(1)} %collective-permute-done.5.rest_1_) | copy-start | bytes 1179652
  70.3 2.9 %collective-permute-start.9 = (bf16[4,96,512]{2,1,0:T(8,128)(2,1)S(1)}, bf16[4,96,512]{2,1,0:T(8,128)(2,1)S(1)}, u32[]{:S(2)}, u32[]{:S(2)}) collective-permute-start(bf16[4,96,512]{2,1,0:T(8,128)(2,1)S(1)} %collective-permute-done.5.rest_1_), channel_id=1, source_target_pairs={{0,1},{1,0},{2,3},{3,2},{4,5},{5,4},{6,7},{7,6},{8,9},{9,8},{10,11... | collective-permute-start | bytes 1179656 | tf_op jit(solution)/shard_map/ppermute | solution.py:42
  71.8 1.4 %copy-start.13 = (bf16[4,96,512]{2,1,0:T(8,128)(2,1)}, bf16[4,96,512]{2,1,0:T(8,128)(2,1)S(1)}, u32[]{:S(2)}) copy-start(bf16[4,96,512]{2,1,0:T(8,128)(2,1)S(1)} %collective-permute-done.10.rest_5_) | copy-start | bytes 1179652
  73.1 0.8 copy-start.14
  73.9 0.9 copy-start.5
  79.8 4.4 %copy-start.2 = (bf16[8,640,128]{2,1,0:T(8,128)(2,1)}, bf16[8,640,128]{2,1,0:T(8,128)(2,1)S(1)}, u32[]{:S(2)}) copy-start(bf16[8,640,128]{2,1,0:T(8,128)(2,1)S(1)} %all-to-all-done.1.own) | copy-start | bytes 3932164
  79.8 4.3 %collective-permute-start.11 = (bf16[8,640,128]{2,1,0:T(8,128)(2,1)S(1)}, bf16[8,640,128]{2,1,0:T(8,128)(2,1)S(1)}, u32[]{:S(2)}, u32[]{:S(2)}) collective-permute-start(bf16[8,640,128]{2,1,0:T(8,128)(2,1)S(1)} %all-to-all-done.1.own), channel_id=1, source_target_pairs={{0,1},{1,0},{2,3},{3,2},{4,5},{5,4},{6,7},{7,6},{8,9},{9,8},{10,11... | collective-permute-start | bytes 3932168 | tf_op jit(solution)/shard_map/ppermute | solution.py:42
  81.4 27.7 %copy-start.3 = (bf16[8,96,384]{2,1,0:T(8,128)(2,1)}, bf16[8,96,384]{2,1,0:T(8,128)(2,1)S(1)}, u32[]{:S(2)}) copy-start(bf16[8,96,384]{2,1,0:T(8,128)(2,1)S(1)} %slice.26.rest_0_) | copy-start | bytes 1769476
  81.4 18.3 %collective-permute-start.3 = (bf16[8,96,384]{2,1,0:T(8,128)(2,1)S(1)}, bf16[8,96,384]{2,1,0:T(8,128)(2,1)}, u32[]{:S(2)}, u32[]{:S(2)}) collective-permute-start(bf16[8,96,384]{2,1,0:T(8,128)(2,1)S(1)} %slice.26.rest_0_), channel_id=1, source_target_pairs={{0,32},{1,33},{2,34},{3,35},{4,36},{5,37},{6,38},{7,39},{8,40},{9,... | collective-permute-start | bytes 1769480 | tf_op jit(solution)/shard_map/ppermute | solution.py:42
  81.5 18.2 %collective-permute-start.4 = (bf16[8,96,384]{2,1,0:T(8,128)(2,1)S(1)}, bf16[8,96,384]{2,1,0:T(8,128)(2,1)}, u32[]{:S(2)}, u32[]{:S(2)}) collective-permute-start(bf16[8,96,384]{2,1,0:T(8,128)(2,1)S(1)} %slice.26.rest_0_), channel_id=1, source_target_pairs={{0,96},{1,97},{2,98},{3,99},{4,100},{5,101},{6,102},{7,103},{8,104... | collective-permute-start | bytes 1769480 | tf_op jit(solution)/shard_map/ppermute | solution.py:42
  84.2 24.9 %collective-permute-start.7 = (bf16[8,96,384]{2,1,0:T(8,128)(2,1)S(1)}, bf16[8,96,384]{2,1,0:T(8,128)(2,1)}, u32[]{:S(2)}, u32[]{:S(2)}) collective-permute-start(bf16[8,96,384]{2,1,0:T(8,128)(2,1)S(1)} %slice.26.rest_0_), channel_id=1, source_target_pairs={{0,64},{1,65},{2,66},{3,67},{4,68},{5,69},{6,70},{7,71},{8,72},{9,... | collective-permute-start | bytes 1769480 | tf_op jit(solution)/shard_map/ppermute | solution.py:42
  84.2 1.1 copy-start.4
  109.1 3.8 %collective-permute-start.12 = (bf16[8,96,384]{2,1,0:T(8,128)(2,1)S(1)}, bf16[8,96,384]{2,1,0:T(8,128)(2,1)S(1)}, u32[]{:S(2)}, u32[]{:S(2)}) collective-permute-start(bf16[8,96,384]{2,1,0:T(8,128)(2,1)S(1)} %slice.26.rest_0_), channel_id=1, source_target_pairs={{0,1},{1,0},{2,3},{3,2},{4,5},{5,4},{6,7},{7,6},{8,9},{9,8},{10,11... | collective-permute-start | bytes 1769480 | tf_op jit(solution)/shard_map/ppermute | solution.py:42
  111.3 2.7 %collective-permute-start.13 = (bf16[8,96,384]{2,1,0:T(8,128)(2,1)}, bf16[8,96,384]{2,1,0:T(8,128)(2,1)S(1)}, u32[]{:S(2)}, u32[]{:S(2)}) collective-permute-start(bf16[8,96,384]{2,1,0:T(8,128)(2,1)} %collective-permute-done.3.rest_1_), channel_id=1, source_target_pairs={{0,1},{1,0},{2,3},{3,2},{4,5},{5,4},{6,7},{7,6},{8,9},{9,8},{10,11... | collective-permute-start | bytes 1769480 | tf_op jit(solution)/shard_map/ppermute | solution.py:42
  111.4 3.4 %collective-permute-start.14 = (bf16[8,96,384]{2,1,0:T(8,128)(2,1)}, bf16[8,96,384]{2,1,0:T(8,128)(2,1)S(1)}, u32[]{:S(2)}, u32[]{:S(2)}) collective-permute-start(bf16[8,96,384]{2,1,0:T(8,128)(2,1)} %collective-permute-done.4.rest_2_), channel_id=1, source_target_pairs={{0,1},{1,0},{2,3},{3,2},{4,5},{5,4},{6,7},{7,6},{8,9},{9,8},{10,11... | collective-permute-start | bytes 1769480 | tf_op jit(solution)/shard_map/ppermute | solution.py:42
  111.8 3.9 %collective-permute-start.15 = (bf16[8,96,384]{2,1,0:T(8,128)(2,1)}, bf16[8,96,384]{2,1,0:T(8,128)(2,1)S(1)}, u32[]{:S(2)}, u32[]{:S(2)}) collective-permute-start(bf16[8,96,384]{2,1,0:T(8,128)(2,1)} %collective-permute-done.7.rest_3_), channel_id=1, source_target_pairs={{0,1},{1,0},{2,3},{3,2},{4,5},{5,4},{6,7},{7,6},{8,9},{9,8},{10,11... | collective-permute-start | bytes 1769480 | tf_op jit(solution)/shard_map/ppermute | solution.py:42
  112.9 2.7 %copy-start.6 = (bf16[8,96,384]{2,1,0:T(8,128)(2,1)}, bf16[8,96,384]{2,1,0:T(8,128)(2,1)S(1)}, u32[]{:S(2)}) copy-start(bf16[8,96,384]{2,1,0:T(8,128)(2,1)S(1)} %collective-permute-done.12.rest_4_) | copy-start | bytes 1769476
  114.0 1.7 %copy-start.7 = (bf16[8,96,384]{2,1,0:T(8,128)(2,1)}, bf16[8,96,384]{2,1,0:T(8,128)(2,1)S(1)}, u32[]{:S(2)}) copy-start(bf16[8,96,384]{2,1,0:T(8,128)(2,1)S(1)} %collective-permute-done.13.rest_5_) | copy-start | bytes 1769476
  114.8 0.9 copy-start.9
  115.7 0.8 copy-start.10

commit v3 on v2

--- a/solution.py
+++ b/solution.py
@@ -16,6 +16,7 @@
 F32 = jnp.float32
 AXES = ("dp", "seq")
 VMEM_LIMIT = 60 * 1024 * 1024
+SMALL = pl.CostEstimate(flops=1000, bytes_accessed=1000, transcendentals=0)
 
 
 def place(l):
@@ -66,7 +67,7 @@
 
     def activated(v):
         scale = lax.rsqrt(jnp.mean(v * v, axis=-1, keepdims=True) + EPS)
-        return jax.nn.gelu(v * scale * cg_ref[...], approximate=True)
+        return jax.nn.gelu(v * scale * cg_ref[...].reshape(1, width), approximate=True)
 
     @pl.when(n == 0)
     def _():
@@ -111,7 +112,7 @@
             lhs[t : t + 2].reshape(2 * rows, width), w_buf[slot, t], preferred_element_type=F32
         )
     cols = pl.ds(pl.multiple_of(n * tile, tile), tile)
-    bias = bias_ref[:, cols]
+    bias = bias_ref[cols].reshape(1, tile)
     even = raw[0, :, cols].astype(F32) + (acc[:rows] + bias)
     odd = raw[1, :, cols].astype(F32) + (acc[rows:] + bias)
     skip_ref[:, cols] = jnp.maximum(even, odd).astype(BF)
@@ -120,7 +121,7 @@
     def _():
         v = skip_ref[...].astype(F32)
         scale = lax.rsqrt(jnp.mean(v * v, axis=-1, keepdims=True) + EPS)
-        norm_ref[...] = (v * scale * ag_ref[...]).astype(BF)
+        norm_ref[...] = (v * scale * ag_ref[...].reshape(1, width)).astype(BF)
 
 
 def convolve(x, before, after, conv_gain, conv_weight, conv_bias, attn_gain):
@@ -128,7 +129,7 @@
     taps = conv_weight.shape[0]
     tile = 256
     out = jax.ShapeDtypeStruct((rows, width), BF)
-    vector = full((1, width))
+    vector = full((width,))
     return pl.pallas_call(
         conv_kernel,
         out_shape=(out, out),
@@ -145,8 +146,9 @@
             pltpu.SemaphoreType.DMA((2,)),
         ],
         compiler_params=pltpu.CompilerParams(vmem_limit_bytes=VMEM_LIMIT),
+        cost_estimate=SMALL,
         name="conv",
-    )(x, before, after, conv_gain[None], conv_bias[None], attn_gain[None], conv_weight)
+    )(x, before, after, conv_gain, conv_bias, attn_gain, conv_weight)
 
 
 def to_same_core(block):
@@ -162,14 +164,12 @@
     return lax.axis_index("dp") // 2, lax.rem(lax.axis_index("seq"), 2)
 
 
-def rows_of_halves(buf, core):
-    p = lax.rem(own_place()[0], 2)
-    return buf.at[p, :, core], buf.at[1 - p, pl.ds(0, 4), core], buf.at[1 - p, pl.ds(4, 4), core]
-
-
 def rows_of_quarters(buf, core):
-    x = own_place()[0]
-    return tuple(buf.at[lax.rem(x + d, 4), :, core] for d in (0, 3, 1, 2))
+    x, n = own_place()[0], buf.shape[-1] // 4
+    return tuple(
+        buf.at[:, core, :, pl.ds(pl.multiple_of(lax.rem(x + d, 4) * n, 128), n)]
+        for d in (0, 3, 1, 2)
+    )
 
 
 def fill(rows_of, mine, theirs, buf, sems):
@@ -187,11 +187,11 @@
     x, _ = own_place()
     copies, at = [], 0
     for src, index, n in (
-        (q_hbm, lax.rem(x, 2), q_hbm.shape[1] // 2),
+        (q_hbm, 0, q_hbm.shape[1]),
         (o_hbm, x, o_hbm.shape[1] // 4),
         (kv_hbm, 0, kv_hbm.shape[1]),
     ):
-        part = src.at[:, pl.ds(pl.multiple_of(index * n, 128), n)] if src is not kv_hbm else src
+        part = src if src is not o_hbm else src.at[:, pl.ds(pl.multiple_of(index * n, 128), n)]
         copies.append(
             pltpu.make_async_copy(part, buf.at[:, pl.ds(at, n)], in_sems.at[len(copies)])
         )
@@ -211,7 +211,7 @@
 
 def pack(q_weight, o_weight, kv_weight):
     rows = q_weight.shape[0]
-    n = q_weight.shape[1] // 2 + o_weight.shape[1] // 4 + kv_weight.shape[1]
+    n = q_weight.shape[1] + o_weight.shape[1] // 4 + kv_weight.shape[1]
     return pl.pallas_call(
         pack_kernel,
         out_shape=jax.ShapeDtypeStruct((8, rows, n), BF),
@@ -223,6 +223,7 @@
             pltpu.SemaphoreType.DMA((8,)),
         ],
         compiler_params=pltpu.CompilerParams(vmem_limit_bytes=VMEM_LIMIT),
+        cost_estimate=SMALL,
         name="pack",
     )(q_weight, o_weight, kv_weight)
 
@@ -231,19 +232,18 @@
     return v * c + pltpu.roll(v, DK // 2, 1) * s
 
 
-def kv_kernel(norm_ref, cos_ref, sin_ref, own, other, kv_ref, buf, sems):
+def kv_kernel(norm_ref, cos_ref, sin_ref, own, other, kv_ref, q_ref, o_ref, buf, sems):
     _, c = own_place()
+    qn, on, n = q_ref.shape[2], o_ref.shape[2], other.shape[2]
     copies = [
-        pltpu.make_async_copy(
-            own.at[:, :, pl.ds(own.shape[2] - other.shape[2], other.shape[2])],
-            buf.at[:, c],
-            sems.at[0],
-        ),
+        pltpu.make_async_copy(own.at[:, :, pl.ds(qn + on, n)], buf.at[:, c], sems.at[0]),
         pltpu.make_async_copy(other, buf.at[:, 1 - c], sems.at[1]),
+        pltpu.make_async_copy(own.at[:, :, pl.ds(0, qn)], q_ref, sems.at[2]),
+        pltpu.make_async_copy(own.at[:, :, pl.ds(qn, on)], o_ref, sems.at[3]),
     ]
     for copy in copies:
         copy.start()
-    for copy in copies:
+    for copy in copies[:2]:
         copy.wait()
     x = norm_ref[...]
     rows, width = x.shape
@@ -259,52 +259,62 @@
     ).astype(BF)
     for i in range(kv_ref.shape[0]):
         kv_ref[i] = packed
-
-
-def key_values(normed, cosine, sine, own, other):
+    for copy in copies[2:]:
+        copy.wait()
+
+
+def key_values(normed, cosine, sine, own, other, qn, on):
     rows = normed.shape[0]
     return pl.pallas_call(
         kv_kernel,
-        out_shape=jax.ShapeDtypeStruct((8, rows * 5 // 2, DK), BF),
+        out_shape=(
+            jax.ShapeDtypeStruct((8, rows * 5 // 2, DK), BF),
+            jax.ShapeDtypeStruct((*own.shape[:2], qn), BF),
+            jax.ShapeDtypeStruct((*own.shape[:2], on), BF),
+        ),
+        in_specs=[IN_VMEM, IN_VMEM, IN_VMEM, ANYWHERE, ANYWHERE],
+        out_specs=(IN_VMEM, IN_VMEM, IN_VMEM),
+        scratch_shapes=[
+            pltpu.VMEM((8, 2, *other.shape[1:]), BF),
+            pltpu.SemaphoreType.DMA((4,)),
+        ],
+        compiler_params=pltpu.CompilerParams(vmem_limit_bytes=VMEM_LIMIT),
+        cost_estimate=SMALL,
+        name="key_values",
+    )(normed, cosine, sine, own, other)
+
+
+def query_kernel(norm_ref, cos_ref, sin_ref, own, other, q_ref, buf, sems):
+    _, core = own_place()
+    copies = [
+        pltpu.make_async_copy(own, buf.at[:, core], sems.at[0]),
+        pltpu.make_async_copy(other, buf.at[:, 1 - core], sems.at[1]),
+    ]
+    for copy in copies:
+        copy.start()
+    for copy in copies:
+        copy.wait()
+    x = norm_ref[...]
+    c, s = cos_ref[...], sin_ref[...]
+    y = jnp.dot(x, buf[...].reshape(x.shape[1], buf.shape[-1]), preferred_element_type=F32)
+    for h in range(HEADS):
+        q_ref[h] = rotated(y[:, h * DK : (h + 1) * DK], c, s).astype(BF)
+
+
+def queries(normed, cosine, sine, own, other):
+    rows, _ = normed.shape
+    return pl.pallas_call(
+        query_kernel,
+        out_shape=jax.ShapeDtypeStruct((HEADS, rows, DK), BF),
         in_specs=[IN_VMEM, IN_VMEM, IN_VMEM, ANYWHERE, ANYWHERE],
         scratch_shapes=[
             pltpu.VMEM((8, 2, *other.shape[1:]), BF),
             pltpu.SemaphoreType.DMA((2,)),
         ],
         compiler_params=pltpu.CompilerParams(vmem_limit_bytes=VMEM_LIMIT),
-        name="key_values",
+        cost_estimate=SMALL,
+        name="queries",
     )(normed, cosine, sine, own, other)
-
-
-def query_kernel(norm_ref, cos_ref, sin_ref, *rest):
-    gathered, *pieces = rest[:6]
-    q_ref, buf, sems = rest[6:]
-    mine = [gathered.at[:, :, pl.ds(0, buf.shape[-1])], *pieces[:2]]
-    for copy in fill(rows_of_halves, mine, pieces[2:], buf, sems):
-        copy.wait()
-    x = norm_ref[...]
-    width = x.shape[1]
-    c, s = cos_ref[...], sin_ref[...]
-    per = buf.shape[-1] // DK
-    for p in range(2):
-        y = jnp.dot(x, buf[p].reshape(width, per * DK), preferred_element_type=F32)
-        for h in range(per):
-            q_ref[p * per + h] = rotated(y[:, h * DK : (h + 1) * DK], c, s).astype(BF)
-
-
-def queries(normed, cosine, sine, pieces):
-    rows, _ = normed.shape
-    return pl.pallas_call(
-        query_kernel,
-        out_shape=jax.ShapeDtypeStruct((HEADS, rows, DK), BF),
-        in_specs=[IN_VMEM, IN_VMEM, IN_VMEM] + [ANYWHERE] * 6,
-        scratch_shapes=[
-            pltpu.VMEM((2, 8, 2, *pieces[1].shape[1:]), BF),
-            pltpu.SemaphoreType.DMA((6,)),
-        ],
-        compiler_params=pltpu.CompilerParams(vmem_limit_bytes=VMEM_LIMIT),
-        name="queries",
-    )(normed, cosine, sine, *pieces)
 
 
 def attention_kernel(
@@ -324,19 +334,10 @@
             copies.append(
                 pltpu.make_async_copy(part.at[:, pl.ds(lo, size), :], dst, sems.at[len(copies)])
             )
-    for copy in copies:
-        copy.start()
-    for copy in copies:
-        copy.wait()
-    lane = lax.broadcasted_iota(jnp.int32, (half, DK), 1)
-    ones = jnp.where(lane == DK // 2, 1.0, 0.0)
-    for i in range(slabs):
-        t = tails[i].astype(F32)
-        vbuf[i, :half, DK:] = jnp.where(lane < DK // 2, t, ones).astype(BF)
-        vbuf[i, half:, DK:] = jnp.where(
-            lane < DK // 2, pltpu.roll(t, DK // 2, 1), ones
-        ).astype(BF)
-
+    for i in (0, 3, 1, 2, 4, 5):
+        copies[i].start()
+    copies[0].wait()
+    copies[3].wait()
     chunks, _, chunk = even_s.shape
     n = chunk // rows
     scale = DK ** (-0.5) * math.log2(math.e)
@@ -367,6 +368,16 @@
         heads_s[head] = total[:, :DV] / total[:, DV : DV + 1]
 
     peak[...] = make_scores(0, even_s)
+    for i in (1, 2, 4, 5):
+        copies[i].wait()
+    lane = lax.broadcasted_iota(jnp.int32, (half, DK), 1)
+    ones = jnp.where(lane == DK // 2, 1.0, 0.0)
+    for i in range(slabs):
+        t = tails[i].astype(F32)
+        vbuf[i, :half, DK:] = jnp.where(lane < DK // 2, t, ones).astype(BF)
+        vbuf[i, half:, DK:] = jnp.where(
+            lane < DK // 2, pltpu.roll(t, DK // 2, 1), ones
+        ).astype(BF)
 
     def step(i, _):
         head = 2 * i
@@ -408,23 +419,18 @@
             pltpu.SemaphoreType.DMA((6,)),
         ],
         compiler_params=pltpu.CompilerParams(vmem_limit_bytes=VMEM_LIMIT),
+        cost_estimate=SMALL,
         name="attention",
     )(q, own, other)
 
 
 def output_kernel(mixed_ref, skip_ref, *rest):
     pieces, (out_ref, buf, sems) = rest[:8], rest[8:]
-    copies = fill(rows_of_quarters, pieces[:4], pieces[4:], buf, sems)
-    x, _ = own_place()
-    tile = buf.shape[-1]
+    for copy in fill(rows_of_quarters, pieces[:4], pieces[4:], buf, sems):
+        copy.wait()
     left = mixed_ref[...]
-    for i, d in enumerate((0, 3, 1, 2)):
-        copies[i].wait()
-        copies[4 + i].wait()
-        p = lax.rem(x + d, 4)
-        cols = pl.ds(pl.multiple_of(p * tile, tile), tile)
-        y = jnp.dot(left, buf[p].reshape(left.shape[1], tile), preferred_element_type=F32)
-        out_ref[:, cols] = (skip_ref[:, cols].astype(F32) + y).astype(BF)
+    y = jnp.dot(left, buf[...].reshape(left.shape[1], buf.shape[-1]), preferred_element_type=F32)
+    out_ref[...] = (skip_ref[...].astype(F32) + y).astype(BF)
 
 
 def output(mixed, skip, pieces):
@@ -434,10 +440,11 @@
         out_shape=jax.ShapeDtypeStruct((rows, width), BF),
         in_specs=[IN_VMEM, IN_VMEM] + [ANYWHERE] * 8,
         scratch_shapes=[
-            pltpu.VMEM((4, 8, 2, *pieces[0].shape[1:]), BF),
+            pltpu.VMEM((8, 2, pieces[0].shape[1], width), BF),
             pltpu.SemaphoreType.DMA((8,)),
         ],
         compiler_params=pltpu.CompilerParams(vmem_limit_bytes=VMEM_LIMIT),
+        cost_estimate=SMALL,
         name="output",
     )(mixed, skip, *pieces)
 
@@ -467,7 +474,7 @@
 def body(x, conv_gain, conv_weight, conv_bias, attn_gain, q_weight, kv_weight, o_weight):
     rows = x.shape[0] // 2
     seq = lax.axis_index("seq")
-    qn, on = q_weight.shape[1] // 2, o_weight.shape[1] // 4
+    qn, on = q_weight.shape[1], o_weight.shape[1] // 4
     before, after = halos(x, seq)
     block = pack(q_weight, o_weight, kv_weight)
     block, before, after = lax.optimization_barrier((block, before, after))
@@ -475,20 +482,16 @@
     skip, normed = convolve(x, before, after, conv_gain, conv_weight, conv_bias, attn_gain)
     cosine, sine = rotation(seq, rows)
     block = tied(block, normed)
-    kv = key_values(
-        normed, cosine, sine, block, send(block[:, :, qn + on :], OTHER_CORE)
+    kv, q_own, o_own = key_values(
+        normed, cosine, sine, block, send(block[:, :, qn + on :], OTHER_CORE), qn, on
     )
     kv_same = to_same_core(kv)
-    q_own = tied(block, kv)[:, :, :qn]
-    q_parts = [send(q_own[:4], along_x(1)), send(q_own[4:], along_x(-1))]
-    o_own = tied(block, kv)[:, :, qn : qn + on]
-    o_parts = [o_own, send(o_own, along_x(1)), send(o_own, along_x(-1))]
-    o_parts.append(send(tied(o_own, *q_parts), along_x(2)))
-    q = queries(normed, cosine, sine, [block, *q_parts, *swapped([q_own, *q_parts])])
-    kv_same = tied(kv_same, q)
+    o_parts = [o_own, *(send(o_own, along_x(k)) for k in (1, -1, 2))]
+    q = queries(normed, cosine, sine, q_own, send(q_own, OTHER_CORE))
+    kv_same = tied(kv_same, q, *o_parts[1:3])
     mixed = attention(q, kv_same, send(kv_same, OTHER_CORE))
-    *o_parts, mixed = lax.optimization_barrier((*o_parts, mixed))
-    return skip, output(mixed, skip, o_parts + swapped(o_parts))
+    o_other = swapped(o_parts[:3]) + swapped([tied(o_parts[3], mixed)])
+    return skip, output(mixed, skip, o_parts + o_other)
 
 
 def solution(mesh):

time: 124 us -> 117 us (0.944)
  starting transfers between devices: 30.3 us -> 25.8 us
  local copies, waits for them, and re-layouts: 7.49 us -> 4.86 us
    all_to_all x2, waiting for transfers between devices: 4.59 us -> 19.2 us  [to_same_core(): lax.all_to_all(block, 'seq', 0, 0, tiled=True, axis_index_groups=groups)]
    ppermute x16 -> x12, waiting for transfers between devices: 23.9 us -> 9.6 us  [send(): return lax.ppermute(array, AXES, pairs)]
    ppermute x16 -> x12, starting transfers between devices: 19.5 us -> 14.8 us  [send(): return lax.ppermute(array, AXES, pairs)]
    broadcast_in_dim x3 -> x0, local copies, waits for them, and re-layouts: 1.81 us -> none  [the longest x1 0.61 us: convolve(): conv_gain[None]]
    unnamed x36 -> x14, local copies, waits for them, and re-layouts: 4.38 us -> 3.93 us
  transfers between devices with their start and end apart: 18 -> 14, of which waited for: 10 -> 5; matrix products, arithmetic and copies ran while one was open for 4% -> 1% of each run, Pallas kernels for 34% -> 36%
where the time goes in v3:
time: 117 us
  Pallas kernels  53.4 us (46%)
  waiting for transfers between devices  28.8 us (25%)
  starting transfers between devices  25.8 us (22%)
  local copies, waits for them, and re-layouts  4.86 us (4%)
  other arithmetic  2.79 us (2%)
    pallas_call x1, Pallas kernels, convolve(): pl.pallas_call(conv_kernel, out_shape=(out, out), grid=(width // tile,),...  20.6 us
    all_to_all x2, waiting for transfers between devices, to_same_core(): lax.all_to_all(block, 'seq', 0, 0, tiled=True, axis_index_groups=groups)  19.2 us
    ppermute x12, starting transfers between devices, send(): return lax.ppermute(array, AXES, pairs)  14.8 us
    pallas_call x1, Pallas kernels, attention(): pl.pallas_call(attention_kernel, out_shape=jax.ShapeDtypeStruct((rows, he...  14.2 us
    all_to_all x2, starting transfers between devices, to_same_core(): lax.all_to_all(block, 'seq', 0, 0, tiled=True, axis_index_groups=groups)  11 us
    ppermute x12, waiting for transfers between devices, send(): return lax.ppermute(array, AXES, pairs)  9.6 us
    pallas_call x1, Pallas kernels, output(): pl.pallas_call(output_kernel, out_shape=jax.ShapeDtypeStruct((rows, width...  6.01 us
    pallas_call x1, Pallas kernels, queries(): pl.pallas_call(query_kernel, out_shape=jax.ShapeDtypeStruct((HEADS, rows,...  5.08 us
  transfers between devices with their start and end apart: 14, of which 5 were waited for; matrix products, arithmetic and copies ran while one was open for 1% of the time, Pallas kernels for 36%

profile of v3, /device:TPU:1, one launch (start us, length us, event | category | flops | bytes accessed | tf_op | source)
XLA Modules:
  0.0 116.6 jit_solution(1720131435158884661)
XLA Ops:
  0.6 0.8 broadcast_select_fusion.2
  1.4 1.5 %collective-permute-start.1 = (bf16[2,1536]{1,0:T(2,128)(2,1)S(1)}, bf16[2,1536]{1,0:T(2,128)(2,1)S(1)}, u32[]{:S(2)}, u32[]{:S(2)}) collective-permute-start(bf16[2,1536]{1,0:T(2,128)(2,1)S(1)} %get-tuple-element.24), channel_id=1, source_target_pairs={{0,1},{1,0},{2,3},{3,2},{4,5},{5,4},{6,7},{7,6},{8,9},{9,8},{10,11... | collective-permute-start | bytes 18440 | tf_op jit(solution)/shard_map/ppermute | solution.py:43
  2.9 4.8 %collective-permute-start = (bf16[2,1536]{1,0:T(2,128)(2,1)S(1)}, bf16[2,1536]{1,0:T(2,128)(2,1)S(1)}, u32[]{:S(2)}, u32[]{:S(2)}) collective-permute-start(bf16[2,1536]{1,0:T(2,128)(2,1)S(1)} %get-tuple-element.25), channel_id=1, source_target_pairs={{1,2},{3,4},{5,6},{7,8},{9,10},{11,12},{13,14},{17,18},{19,20},{21... | collective-permute-start | bytes 18440 | tf_op jit(solution)/shard_map/ppermute | solution.py:43
  7.7 2.6 %pack.1 = bf16[8,96,1728]{2,1,0:T(8,128)(2,1)} custom-call(bf16[96,1024]{1,0:T(8,128)(2,1)} %q_hbm.1, bf16[96,1536]{1,0:T(8,128)(2,1)} %o_hbm.1, bf16[96,320]{1,0:T(8,128)(2,1)} %kv_hbm.1), custom_call_target="tpu_custom_call" | custom-call | flops 1000 | bytes 1000 | tf_op jit(solution)/shard_map/pack/pallas_call | solution.py:215
  10.4 0.0 collective-permute-done.1
  10.4 0.0 collective-permute-done
  10.4 0.6 broadcast_select_fusion
  11.0 7.4 %all-to-all-start = ((bf16[8,96,1728]{2,1,0:T(8,128)(2,1)}), bf16[8,96,1728]{2,1,0:T(8,128)(2,1)S(1)}, u32[]{:S(2)}, u32[]{:S(2)}) async-start(bf16[8,96,1728]{2,1,0:T(8,128)(2,1)} %pack.1), calls=%async_computation | async-start | bytes 5505024 | tf_op jit(solution)/shard_map/all_to_all | solution.py:156
  18.5 20.6 %conv.1 = (bf16[256,1536]{1,0:T(8,128)(2,1)}, bf16[256,1536]{1,0:T(8,128)(2,1)}) custom-call(bf16[512,1536]{1,0:T(8,128)(2,1)} %x_ref.1, bf16[2,1536]{1,0:T(2,128)(2,1)} %get-tuple-element.13.before_ref, bf16[2,1536]{1,0:T(2,128)(2,1)} %get-tuple-element.14.after_ref, f32[1536]{0:T(1024)} %cg_ref.1, f32[1536]{0:T(1024)} %bias_ref.1, f32[1536]{0:T(1024)} %ag_ref.1, ...), custom_call_target="tpu_custom_call" | custom-call | flops 1000 | bytes 1000 | tf_op jit(solution)/shard_map/conv/pallas_call | solution.py:133
  39.0 15.4 %all-to-all-done.own = bf16[8,96,1728]{2,1,0:T(8,128)(2,1)S(1)} async-done(((bf16[8,96,1728]{2,1,0:T(8,128)(2,1)}), bf16[8,96,1728]{2,1,0:T(8,128)(2,1)S(1)}, u32[]{:S(2)}, u32[]{:S(2)}) %all-to-all-start) | async-done | bytes 2654240 | tf_op jit(solution)/shard_map/all_to_all | solution.py:156
  54.5 0.0 copy-start
  54.5 0.9 slice.11
  55.4 0.5 collective-permute-start.2
  55.9 0.5 fusion
  56.4 0.8 pad_maximum_fusion
  57.3 0.4 collective-permute-done.2.other
  57.7 0.0 copy-done
  57.7 0.8 copy-done.5
  58.5 4.9 %key_values.1 = (bf16[8,640,128]{2,1,0:T(8,128)(2,1)}, bf16[8,96,1024]{2,1,0:T(8,128)(2,1)}, bf16[8,96,384]{2,1,0:T(8,128)(2,1)}) custom-call(bf16[256,1536]{1,0:T(8,128)(2,1)} %get-tuple-element.16.norm_ref, f32[256,128]{1,0:T(8,128)} %get-tuple-element.31.cos_ref, f32[256,128]{1,0:T(8,128)} %get-tuple-element.32.sin_ref, bf16[8,96,1728]{2,1,0:T(8,128)(2,1)} %copy-done, ...), custom_call_target="tpu_custom_call" | custom-call | flops 1000 | bytes 1000 | tf_op jit(solution)/shard_map/key_values/pallas_call | solution.py:268
  63.5 0.0 copy-start.4
  63.5 0.5 collective-permute-start.3
  63.9 3.6 %all-to-all-start.1 = ((bf16[8,640,128]{2,1,0:T(8,128)(2,1)}), bf16[8,640,128]{2,1,0:T(8,128)(2,1)S(1)}, u32[]{:S(2)}, u32[]{:S(2)}) async-start(bf16[8,640,128]{2,1,0:T(8,128)(2,1)} %get-tuple-element.20), calls=%async_computation.1 | async-start | bytes 2621440 | tf_op jit(solution)/shard_map/all_to_all | solution.py:156
  67.5 0.0 copy-done.4
  67.5 1.3 %collective-permute-start.4 = (bf16[8,96,384]{2,1,0:T(8,128)(2,1)S(1)}, bf16[8,96,384]{2,1,0:T(8,128)(2,1)}, u32[]{:S(2)}, u32[]{:S(2)}) collective-permute-start(bf16[8,96,384]{2,1,0:T(8,128)(2,1)S(1)} %copy-done.4), channel_id=1, source_target_pairs={{0,32},{1,33},{2,34},{3,35},{4,36},{5,37},{6,38},{7,39},{8,40},{9,... | collective-permute-start | bytes 1769480 | tf_op jit(solution)/shard_map/ppermute | solution.py:43
  68.8 1.5 %collective-permute-start.5 = (bf16[8,96,384]{2,1,0:T(8,128)(2,1)S(1)}, bf16[8,96,384]{2,1,0:T(8,128)(2,1)}, u32[]{:S(2)}, u32[]{:S(2)}) collective-permute-start(bf16[8,96,384]{2,1,0:T(8,128)(2,1)S(1)} %copy-done.4), channel_id=1, source_target_pairs={{0,96},{1,97},{2,98},{3,99},{4,100},{5,101},{6,102},{7,103},{8,104... | collective-permute-start | bytes 1769480 | tf_op jit(solution)/shard_map/ppermute | solution.py:43
  70.3 0.0 collective-permute-done.3.other
  70.3 1.2 %copy-done.2 = bf16[8,96,1024]{2,1,0:T(8,128)(2,1)} copy-done((bf16[8,96,1024]{2,1,0:T(8,128)(2,1)}, bf16[8,96,1024]{2,1,0:T(8,128)(2,1)S(1)}, u32[]{:S(2)}) %copy-start.2) | copy-done | bytes 1572888
  71.5 5.1 %queries.1.q_ref = bf16[8,256,128]{2,1,0:T(8,128)(2,1)} custom-call(bf16[256,1536]{1,0:T(8,128)(2,1)} %get-tuple-element.16.norm_ref, f32[256,128]{1,0:T(8,128)} %get-tuple-element.31.cos_ref, f32[256,128]{1,0:T(8,128)} %get-tuple-element.32.sin_ref, bf16[8,96,1024]{2,1,0:T(8,128)(2,1)} %get-tuple-element.19.own, bf16[8,96,1024]{2,1,0:T(8,128)(2,1)} %copy-done.2), custom_call_target="tpu_custom_call" | custom-call | flops 1000 | bytes 1000 | tf_op jit(solution)/shard_map/queries/pallas_call | solution.py:306
  76.5 7.2 %collective-permute-done.4.rest_1_ = bf16[8,96,384]{2,1,0:T(8,128)(2,1)} collective-permute-done((bf16[8,96,384]{2,1,0:T(8,128)(2,1)S(1)}, bf16[8,96,384]{2,1,0:T(8,128)(2,1)}, u32[]{:S(2)}, u32[]{:S(2)}) %collective-permute-start.4) | collective-permute-done | bytes 589856 | tf_op jit(solution)/shard_map/ppermute | solution.py:43
  83.7 0.0 collective-permute-done.5.rest_2_
  83.7 3.8 %all-to-all-done.1.own = bf16[8,640,128]{2,1,0:T(8,128)(2,1)S(1)} async-done(((bf16[8,640,128]{2,1,0:T(8,128)(2,1)}), bf16[8,640,128]{2,1,0:T(8,128)(2,1)S(1)}, u32[]{:S(2)}, u32[]{:S(2)}) %all-to-all-start.1) | async-done | bytes 1310752 | tf_op jit(solution)/shard_map/all_to_all | solution.py:156
  87.5 1.0 collective-permute-start.6
  88.5 2.7 %collective-permute-start.7 = (bf16[8,96,384]{2,1,0:T(8,128)(2,1)S(1)}, bf16[8,96,384]{2,1,0:T(8,128)(2,1)}, u32[]{:S(2)}, u32[]{:S(2)}) collective-permute-start(bf16[8,96,384]{2,1,0:T(8,128)(2,1)S(1)} %copy-done.4), channel_id=1, source_target_pairs={{0,64},{1,65},{2,66},{3,67},{4,68},{5,69},{6,70},{7,71},{8,72},{9,... | collective-permute-start | bytes 1769480 | tf_op jit(solution)/shard_map/ppermute | solution.py:43
  91.2 0.3 collective-permute-start.8
  91.5 0.2 collective-permute-start.9
  91.7 0.3 collective-permute-start.10
  92.0 0.0 collective-permute-done.6.other
  92.0 0.0 copy-done.1
  92.0 1.1 copy-done.3
  93.1 14.2 %attention.1.mixed_ref = bf16[256,1536]{1,0:T(8,128)(2,1)} custom-call(bf16[8,256,128]{2,1,0:T(8,128)(2,1)} %queries.1.q_ref, bf16[8,640,128]{2,1,0:T(8,128)(2,1)} %copy-done.1, bf16[8,640,128]{2,1,0:T(8,128)(2,1)} %copy-done.3), custom_call_target="tpu_custom_call" | custom-call | flops 1000 | bytes 1000 | tf_op jit(solution)/shard_map/attention/pallas_call | solution.py:407
  107.3 0.0 collective-permute-done.7.rest_3_
  107.3 0.3 collective-permute-start.11
  107.6 0.0 collective-permute-done.8.rest_4_
  107.6 0.0 collective-permute-done.9.rest_5_
  107.6 0.0 collective-permute-done.10.rest_6_
  107.6 2.0 %collective-permute-done.11.rest_7_ = bf16[8,96,384]{2,1,0:T(8,128)(2,1)S(1)} collective-permute-done((bf16[8,96,384]{2,1,0:T(8,128)(2,1)}, bf16[8,96,384]{2,1,0:T(8,128)(2,1)S(1)}, u32[]{:S(2)}, u32[]{:S(2)}) %collective-permute-start.11) | collective-permute-done | bytes 589856 | tf_op jit(solution)/shard_map/ppermute | solution.py:43
  109.6 0.8 copy-done.6
  110.4 6.0 %output.1 = bf16[256,1536]{1,0:T(8,128)(2,1)} custom-call(bf16[256,1536]{1,0:T(8,128)(2,1)} %attention.1.mixed_ref, bf16[256,1536]{1,0:T(8,128)(2,1)} %get-tuple-element.11.skip_ref, bf16[8,96,384]{2,1,0:T(8,128)(2,1)} %get-tuple-element.21.rest_0_, bf16[8,96,384]{2,1,0:T(8,128)(2,1)} %collective-permute-done.4.rest_1_, ...), custom_call_target="tpu_custom_call" | custom-call | flops 1000 | bytes 1000 | tf_op jit(solution)/shard_map/output/pallas_call | solution.py:438
  (7 shorter events, 0.0 us)
Async XLA Ops:
  1.4 9.0 %collective-permute-start.1 = (bf16[2,1536]{1,0:T(2,128)(2,1)S(1)}, bf16[2,1536]{1,0:T(2,128)(2,1)S(1)}, u32[]{:S(2)}, u32[]{:S(2)}) collective-permute-start(bf16[2,1536]{1,0:T(2,128)(2,1)S(1)} %get-tuple-element.24), channel_id=1, source_target_pairs={{0,1},{1,0},{2,3},{3,2},{4,5},{5,4},{6,7},{7,6},{8,9},{9,8},{10,11... | collective-permute-start | bytes 18440 | tf_op jit(solution)/shard_map/ppermute | solution.py:43
  2.9 7.5 %collective-permute-start = (bf16[2,1536]{1,0:T(2,128)(2,1)S(1)}, bf16[2,1536]{1,0:T(2,128)(2,1)S(1)}, u32[]{:S(2)}, u32[]{:S(2)}) collective-permute-start(bf16[2,1536]{1,0:T(2,128)(2,1)S(1)} %get-tuple-element.25), channel_id=1, source_target_pairs={{1,2},{3,4},{5,6},{7,8},{9,10},{11,12},{13,14},{17,18},{19,20},{21... | collective-permute-start | bytes 18440 | tf_op jit(solution)/shard_map/ppermute | solution.py:43
  11.0 43.4 %all-to-all-start = ((bf16[8,96,1728]{2,1,0:T(8,128)(2,1)}), bf16[8,96,1728]{2,1,0:T(8,128)(2,1)S(1)}, u32[]{:S(2)}, u32[]{:S(2)}) async-start(bf16[8,96,1728]{2,1,0:T(8,128)(2,1)} %pack.1), calls=%async_computation | async-start | bytes 5505024 | tf_op jit(solution)/shard_map/all_to_all | solution.py:156
  54.5 3.2 %copy-start = (bf16[8,96,1728]{2,1,0:T(8,128)(2,1)}, bf16[8,96,1728]{2,1,0:T(8,128)(2,1)S(1)}, u32[]{:S(2)}) copy-start(bf16[8,96,1728]{2,1,0:T(8,128)(2,1)S(1)} %all-to-all-done.own) | copy-start | bytes 7962628
  55.4 2.3 %collective-permute-start.2 = (bf16[8,96,320]{2,1,0:T(8,128)(2,1)}, bf16[8,96,320]{2,1,0:T(8,128)(2,1)S(1)}, u32[]{:S(2)}, u32[]{:S(2)}) collective-permute-start(bf16[8,96,320]{2,1,0:T(8,128)(2,1)} %slice.11), channel_id=1, source_target_pairs={{0,1},{1,0},{2,3},{3,2},{4,5},{5,4},{6,7},{7,6},{8,9},{9,8},{10,11... | collective-permute-start | bytes 1474568 | tf_op jit(solution)/shard_map/ppermute | solution.py:43
  57.7 0.8 copy-start.5
  63.5 4.0 %copy-start.4 = (bf16[8,96,384]{2,1,0:T(8,128)(2,1)S(1)}, bf16[8,96,384]{2,1,0:T(8,128)(2,1)}, u32[]{:S(2)}) copy-start(bf16[8,96,384]{2,1,0:T(8,128)(2,1)} %get-tuple-element.21.rest_0_) | copy-start | bytes 1769476
  63.5 6.8 %collective-permute-start.3 = (bf16[8,96,1024]{2,1,0:T(8,128)(2,1)}, bf16[8,96,1024]{2,1,0:T(8,128)(2,1)S(1)}, u32[]{:S(2)}, u32[]{:S(2)}) collective-permute-start(bf16[8,96,1024]{2,1,0:T(8,128)(2,1)} %get-tuple-element.19.own), channel_id=1, source_target_pairs={{0,1},{1,0},{2,3},{3,2},{4,5},{5,4},{6,7},{7,6},{8,9},{9,8},{10,11... | collective-permute-start | bytes 4718600 | tf_op jit(solution)/shard_map/ppermute | solution.py:43
  63.9 23.5 %all-to-all-start.1 = ((bf16[8,640,128]{2,1,0:T(8,128)(2,1)}), bf16[8,640,128]{2,1,0:T(8,128)(2,1)S(1)}, u32[]{:S(2)}, u32[]{:S(2)}) async-start(bf16[8,640,128]{2,1,0:T(8,128)(2,1)} %get-tuple-element.20), calls=%async_computation.1 | async-start | bytes 2621440 | tf_op jit(solution)/shard_map/all_to_all | solution.py:156
  67.5 16.2 %collective-permute-start.4 = (bf16[8,96,384]{2,1,0:T(8,128)(2,1)S(1)}, bf16[8,96,384]{2,1,0:T(8,128)(2,1)}, u32[]{:S(2)}, u32[]{:S(2)}) collective-permute-start(bf16[8,96,384]{2,1,0:T(8,128)(2,1)S(1)} %copy-done.4), channel_id=1, source_target_pairs={{0,32},{1,33},{2,34},{3,35},{4,36},{5,37},{6,38},{7,39},{8,40},{9,... | collective-permute-start | bytes 1769480 | tf_op jit(solution)/shard_map/ppermute | solution.py:43
  68.8 14.9 %collective-permute-start.5 = (bf16[8,96,384]{2,1,0:T(8,128)(2,1)S(1)}, bf16[8,96,384]{2,1,0:T(8,128)(2,1)}, u32[]{:S(2)}, u32[]{:S(2)}) collective-permute-start(bf16[8,96,384]{2,1,0:T(8,128)(2,1)S(1)} %copy-done.4), channel_id=1, source_target_pairs={{0,96},{1,97},{2,98},{3,99},{4,100},{5,101},{6,102},{7,103},{8,104... | collective-permute-start | bytes 1769480 | tf_op jit(solution)/shard_map/ppermute | solution.py:43
  70.3 1.2 %copy-start.2 = (bf16[8,96,1024]{2,1,0:T(8,128)(2,1)}, bf16[8,96,1024]{2,1,0:T(8,128)(2,1)S(1)}, u32[]{:S(2)}) copy-start(bf16[8,96,1024]{2,1,0:T(8,128)(2,1)S(1)} %collective-permute-done.3.other) | copy-start | bytes 4718596
  87.5 4.5 %copy-start.1 = (bf16[8,640,128]{2,1,0:T(8,128)(2,1)}, bf16[8,640,128]{2,1,0:T(8,128)(2,1)S(1)}, u32[]{:S(2)}) copy-start(bf16[8,640,128]{2,1,0:T(8,128)(2,1)S(1)} %all-to-all-done.1.own) | copy-start | bytes 3932164
  87.5 4.5 %collective-permute-start.6 = (bf16[8,640,128]{2,1,0:T(8,128)(2,1)S(1)}, bf16[8,640,128]{2,1,0:T(8,128)(2,1)S(1)}, u32[]{:S(2)}, u32[]{:S(2)}) collective-permute-start(bf16[8,640,128]{2,1,0:T(8,128)(2,1)S(1)} %all-to-all-done.1.own), channel_id=1, source_target_pairs={{0,1},{1,0},{2,3},{3,2},{4,5},{5,4},{6,7},{7,6},{8,9},{9,8},{10,11... | collective-permute-start | bytes 3932168 | tf_op jit(solution)/shard_map/ppermute | solution.py:43
  88.5 18.8 %collective-permute-start.7 = (bf16[8,96,384]{2,1,0:T(8,128)(2,1)S(1)}, bf16[8,96,384]{2,1,0:T(8,128)(2,1)}, u32[]{:S(2)}, u32[]{:S(2)}) collective-permute-start(bf16[8,96,384]{2,1,0:T(8,128)(2,1)S(1)} %copy-done.4), channel_id=1, source_target_pairs={{0,64},{1,65},{2,66},{3,67},{4,68},{5,69},{6,70},{7,71},{8,72},{9,... | collective-permute-start | bytes 1769480 | tf_op jit(solution)/shard_map/ppermute | solution.py:43
  91.2 16.4 %collective-permute-start.8 = (bf16[8,96,384]{2,1,0:T(8,128)(2,1)S(1)}, bf16[8,96,384]{2,1,0:T(8,128)(2,1)}, u32[]{:S(2)}, u32[]{:S(2)}) collective-permute-start(bf16[8,96,384]{2,1,0:T(8,128)(2,1)S(1)} %copy-done.4), channel_id=1, source_target_pairs={{0,1},{1,0},{2,3},{3,2},{4,5},{5,4},{6,7},{7,6},{8,9},{9,8},{10,11... | collective-permute-start | bytes 1769480 | tf_op jit(solution)/shard_map/ppermute | solution.py:43
  91.5 16.1 %collective-permute-start.9 = (bf16[8,96,384]{2,1,0:T(8,128)(2,1)}, bf16[8,96,384]{2,1,0:T(8,128)(2,1)}, u32[]{:S(2)}, u32[]{:S(2)}) collective-permute-start(bf16[8,96,384]{2,1,0:T(8,128)(2,1)} %collective-permute-done.4.rest_1_), channel_id=1, source_target_pairs={{0,1},{1,0},{2,3},{3,2},{4,5},{5,4},{6,7},{7,6},{8,9},{9,8},{10,11... | collective-permute-start | bytes 1769480 | tf_op jit(solution)/shard_map/ppermute | solution.py:43
  91.7 15.9 %collective-permute-start.10 = (bf16[8,96,384]{2,1,0:T(8,128)(2,1)}, bf16[8,96,384]{2,1,0:T(8,128)(2,1)}, u32[]{:S(2)}, u32[]{:S(2)}) collective-permute-start(bf16[8,96,384]{2,1,0:T(8,128)(2,1)} %collective-permute-done.5.rest_2_), channel_id=1, source_target_pairs={{0,1},{1,0},{2,3},{3,2},{4,5},{5,4},{6,7},{7,6},{8,9},{9,8},{10,11... | collective-permute-start | bytes 1769480 | tf_op jit(solution)/shard_map/ppermute | solution.py:43
  92.0 1.1 copy-start.3
  107.3 2.3 %collective-permute-start.11 = (bf16[8,96,384]{2,1,0:T(8,128)(2,1)}, bf16[8,96,384]{2,1,0:T(8,128)(2,1)S(1)}, u32[]{:S(2)}, u32[]{:S(2)}) collective-permute-start(bf16[8,96,384]{2,1,0:T(8,128)(2,1)} %collective-permute-done.7.rest_3_), channel_id=1, source_target_pairs={{0,1},{1,0},{2,3},{3,2},{4,5},{5,4},{6,7},{7,6},{8,9},{9,8},{10,11... | collective-permute-start | bytes 1769480 | tf_op jit(solution)/shard_map/ppermute | solution.py:43
  109.6 0.8 copy-start.6

commit v4 on v3

--- a/solution.py
+++ b/solution.py
@@ -15,7 +15,8 @@
 BF = jnp.bfloat16
 F32 = jnp.float32
 AXES = ("dp", "seq")
-VMEM_LIMIT = 60 * 1024 * 1024
+MIB = 1024 * 1024
+VMEM_LIMIT = 60 * MIB
 SMALL = pl.CostEstimate(flops=1000, bytes_accessed=1000, transcendentals=0)
 
 
@@ -145,7 +146,7 @@
             pltpu.VMEM((2, taps, width, tile), BF),
             pltpu.SemaphoreType.DMA((2,)),
         ],
-        compiler_params=pltpu.CompilerParams(vmem_limit_bytes=VMEM_LIMIT),
+        compiler_params=pltpu.CompilerParams(vmem_limit_bytes=36 * MIB),
         cost_estimate=SMALL,
         name="conv",
     )(x, before, after, conv_gain, conv_bias, attn_gain, conv_weight)
@@ -278,7 +279,7 @@
             pltpu.VMEM((8, 2, *other.shape[1:]), BF),
             pltpu.SemaphoreType.DMA((4,)),
         ],
-        compiler_params=pltpu.CompilerParams(vmem_limit_bytes=VMEM_LIMIT),
+        compiler_params=pltpu.CompilerParams(vmem_limit_bytes=16 * MIB),
         cost_estimate=SMALL,
         name="key_values",
     )(normed, cosine, sine, own, other)
@@ -311,7 +312,7 @@
             pltpu.VMEM((8, 2, *other.shape[1:]), BF),
             pltpu.SemaphoreType.DMA((2,)),
         ],
-        compiler_params=pltpu.CompilerParams(vmem_limit_bytes=VMEM_LIMIT),
+        compiler_params=pltpu.CompilerParams(vmem_limit_bytes=16 * MIB),
         cost_estimate=SMALL,
         name="queries",
     )(normed, cosine, sine, own, other)
@@ -418,7 +419,7 @@
             pltpu.VMEM((heads, rows, DV), F32),
             pltpu.SemaphoreType.DMA((6,)),
         ],
-        compiler_params=pltpu.CompilerParams(vmem_limit_bytes=VMEM_LIMIT),
+        compiler_params=pltpu.CompilerParams(vmem_limit_bytes=32 * MIB),
         cost_estimate=SMALL,
         name="attention",
     )(q, own, other)
@@ -443,7 +444,7 @@
             pltpu.VMEM((8, 2, pieces[0].shape[1], width), BF),
             pltpu.SemaphoreType.DMA((8,)),
         ],
-        compiler_params=pltpu.CompilerParams(vmem_limit_bytes=VMEM_LIMIT),
+        compiler_params=pltpu.CompilerParams(vmem_limit_bytes=16 * MIB),
         cost_estimate=SMALL,
         name="output",
     )(mixed, skip, *pieces)

time: 117 us -> 110 us (0.940)
  Pallas kernels: 53.4 us -> 42.3 us
  waiting for transfers between devices: 28.8 us -> 31.4 us
  local copies, waits for them, and re-layouts: 4.86 us -> 7.09 us
  other arithmetic: 2.79 us -> 1.49 us
    ppermute x12, waiting for transfers between devices: 9.6 us -> 14.6 us  [send(): return lax.ppermute(array, AXES, pairs)]
    pallas_call x1, Pallas kernels: 14.2 us -> 11.4 us  [attention(): pl.pallas_call(attention_kernel, out_shape=jax.ShapeDtypeStruct((rows, he...]
    pallas_call x1, Pallas kernels: 6.01 us -> 3.53 us  [output(): pl.pallas_call(output_kernel, out_shape=jax.ShapeDtypeStruct((rows, width...]
    all_to_all x2, waiting for transfers between devices: 19.2 us -> 16.8 us  [to_same_core(): lax.all_to_all(block, 'seq', 0, 0, tiled=True, axis_index_groups=groups)]
    unnamed x14 -> x28, local copies, waits for them, and re-layouts: 3.93 us -> 6.21 us
    pallas_call x1, Pallas kernels: 5.08 us -> 3.03 us  [queries(): pl.pallas_call(query_kernel, out_shape=jax.ShapeDtypeStruct((HEADS, rows,...]
    pallas_call x1, Pallas kernels: 4.94 us -> 3 us  [key_values(): pl.pallas_call(kv_kernel, out_shape=(jax.ShapeDtypeStruct((8, rows * 5 //...]
    pallas_call x1, Pallas kernels: 20.6 us -> 18.8 us  [convolve(): pl.pallas_call(conv_kernel, out_shape=(out, out), grid=(width // tile,),...]
  transfers between devices with their start and end apart: 14 -> 14, of which waited for: 5 -> 6; matrix products, arithmetic and copies ran while one was open for 1% -> 1% of each run, Pallas kernels for 36% -> 33%
where the time goes in v4:
time: 110 us
  Pallas kernels  42.3 us (38%)
  waiting for transfers between devices  31.4 us (29%)
  starting transfers between devices  26.4 us (24%)
  local copies, waits for them, and re-layouts  7.09 us (6%)
  other arithmetic  1.49 us (1%)
    pallas_call x1, Pallas kernels, convolve(): pl.pallas_call(conv_kernel, out_shape=(out, out), grid=(width // tile,),...  18.8 us
    all_to_all x2, waiting for transfers between devices, to_same_core(): lax.all_to_all(block, 'seq', 0, 0, tiled=True, axis_index_groups=groups)  16.8 us
    ppermute x12, starting transfers between devices, send(): return lax.ppermute(array, AXES, pairs)  15.3 us
    ppermute x12, waiting for transfers between devices, send(): return lax.ppermute(array, AXES, pairs)  14.6 us
    pallas_call x1, Pallas kernels, attention(): pl.pallas_call(attention_kernel, out_shape=jax.ShapeDtypeStruct((rows, he...  11.4 us
    all_to_all x2, starting transfers between devices, to_same_core(): lax.all_to_all(block, 'seq', 0, 0, tiled=True, axis_index_groups=groups)  11 us
    unnamed x28, local copies, waits for them, and re-layouts  6.21 us
    pallas_call x1, Pallas kernels, output(): pl.pallas_call(output_kernel, out_shape=jax.ShapeDtypeStruct((rows, width...  3.53 us
  transfers between devices with their start and end apart: 14, of which 6 were waited for; matrix products, arithmetic and copies ran while one was open for 1% of the time, Pallas kernels for 33%

profile of v4, /device:TPU:1, one launch (start us, length us, event | category | flops | bytes accessed | tf_op | source)
XLA Modules:
  0.0 109.6 jit_solution(6342619255155193972)
XLA Ops:
  0.6 0.8 broadcast_select_fusion.2
  1.4 1.5 %collective-permute-start.1 = (bf16[2,1536]{1,0:T(2,128)(2,1)S(1)}, bf16[2,1536]{1,0:T(2,128)(2,1)S(1)}, u32[]{:S(2)}, u32[]{:S(2)}) collective-permute-start(bf16[2,1536]{1,0:T(2,128)(2,1)S(1)} %get-tuple-element.24), channel_id=1, source_target_pairs={{0,1},{1,0},{2,3},{3,2},{4,5},{5,4},{6,7},{7,6},{8,9},{9,8},{10,11... | collective-permute-start | bytes 18440 | tf_op jit(solution)/shard_map/ppermute | solution.py:44
  2.9 4.8 %collective-permute-start = (bf16[2,1536]{1,0:T(2,128)(2,1)S(1)}, bf16[2,1536]{1,0:T(2,128)(2,1)S(1)}, u32[]{:S(2)}, u32[]{:S(2)}) collective-permute-start(bf16[2,1536]{1,0:T(2,128)(2,1)S(1)} %get-tuple-element.25), channel_id=1, source_target_pairs={{1,2},{3,4},{5,6},{7,8},{9,10},{11,12},{13,14},{17,18},{19,20},{21... | collective-permute-start | bytes 18440 | tf_op jit(solution)/shard_map/ppermute | solution.py:44
  7.7 2.6 %pack.1 = bf16[8,96,1728]{2,1,0:T(8,128)(2,1)} custom-call(bf16[96,1024]{1,0:T(8,128)(2,1)} %q_hbm.1, bf16[96,1536]{1,0:T(8,128)(2,1)} %o_hbm.1, bf16[96,320]{1,0:T(8,128)(2,1)} %kv_hbm.1), custom_call_target="tpu_custom_call" | custom-call | flops 1000 | bytes 1000 | tf_op jit(solution)/shard_map/pack/pallas_call | solution.py:216
  10.4 0.0 collective-permute-done.1
  10.4 0.0 collective-permute-done
  10.4 7.5 %all-to-all-start = ((bf16[8,96,1728]{2,1,0:T(8,128)(2,1)}), bf16[8,96,1728]{2,1,0:T(8,128)(2,1)S(1)}, u32[]{:S(2)}, u32[]{:S(2)}) async-start(bf16[8,96,1728]{2,1,0:T(8,128)(2,1)} %pack.1), calls=%async_computation | async-start | bytes 5505024 | tf_op jit(solution)/shard_map/all_to_all | solution.py:157
  17.9 1.4 %copy-done = bf16[512,1536]{1,0:T(8,128)(2,1)S(1)} copy-done((bf16[512,1536]{1,0:T(8,128)(2,1)S(1)}, bf16[512,1536]{1,0:T(8,128)(2,1)}, u32[]{:S(2)}) %copy-start) | copy-done | bytes 1572888
  19.3 0.7 copy-done.11
  20.0 0.7 copy-done.12
  20.7 0.7 copy-done.13
  21.4 18.8 %conv.1 = (bf16[256,1536]{1,0:T(8,128)(2,1)}, bf16[256,1536]{1,0:T(8,128)(2,1)S(1)}) custom-call(bf16[512,1536]{1,0:T(8,128)(2,1)S(1)} %copy-done, bf16[2,1536]{1,0:T(2,128)(2,1)S(1)} %get-tuple-element.13.before_ref, bf16[2,1536]{1,0:T(2,128)(2,1)S(1)} %get-tuple-element.14.after_ref, f32[1536]{0:T(1024)S(1)} %copy-done.11, f32[1536]{0:T(1024)S(1)} %copy-done.12, ...), custom_call_target="tpu_custom_call" | custom-call | flops 1000 | bytes 1000 | tf_op jit(solution)/shard_map/conv/pallas_call | solution.py:134
  40.1 13.7 %all-to-all-done.own = bf16[8,96,1728]{2,1,0:T(8,128)(2,1)S(1)} async-done(((bf16[8,96,1728]{2,1,0:T(8,128)(2,1)}), bf16[8,96,1728]{2,1,0:T(8,128)(2,1)S(1)}, u32[]{:S(2)}, u32[]{:S(2)}) %all-to-all-start) | async-done | bytes 2654240 | tf_op jit(solution)/shard_map/all_to_all | solution.py:157
  53.9 0.9 slice.11
  54.8 0.5 collective-permute-start.2
  55.2 0.5 fusion
  55.8 0.1 pad_maximum_fusion
  55.9 1.2 %collective-permute-done.2.other = bf16[8,96,320]{2,1,0:T(8,128)(2,1)} collective-permute-done((bf16[8,96,320]{2,1,0:T(8,128)(2,1)}, bf16[8,96,320]{2,1,0:T(8,128)(2,1)}, u32[]{:S(2)}, u32[]{:S(2)}) %collective-permute-start.2) | collective-permute-done | bytes 491552 | tf_op jit(solution)/shard_map/ppermute | solution.py:44
  57.2 3.0 %key_values.1 = (bf16[8,640,128]{2,1,0:T(8,128)(2,1)S(1)}, bf16[8,96,1024]{2,1,0:T(8,128)(2,1)}, bf16[8,96,384]{2,1,0:T(8,128)(2,1)S(1)}) custom-call(bf16[256,1536]{1,0:T(8,128)(2,1)S(1)} %get-tuple-element.16.norm_ref, f32[256,128]{1,0:T(8,128)S(1)} %get-tuple-element.31.cos_ref, f32[256,128]{1,0:T(8,128)S(1)} %get-tuple-element.32.sin_ref, ...), custom_call_target="tpu_custom_call" | custom-call | flops 1000 | bytes 1000 | tf_op jit(solution)/shard_map/key_values/pallas_call | solution.py:269
  60.2 1.1 copy-done.1
  61.3 0.8 copy-done.7
  62.1 0.4 collective-permute-start.3
  62.5 3.6 %all-to-all-start.1 = ((bf16[8,640,128]{2,1,0:T(8,128)(2,1)}), bf16[8,640,128]{2,1,0:T(8,128)(2,1)S(1)}, u32[]{:S(2)}, u32[]{:S(2)}) async-start(bf16[8,640,128]{2,1,0:T(8,128)(2,1)} %copy-done.1), calls=%async_computation.1 | async-start | bytes 2621440 | tf_op jit(solution)/shard_map/all_to_all | solution.py:157
  66.1 0.0 copy-done.8
  66.1 1.3 %collective-permute-start.4 = (bf16[8,96,384]{2,1,0:T(8,128)(2,1)S(1)}, bf16[8,96,384]{2,1,0:T(8,128)(2,1)S(1)}, u32[]{:S(2)}, u32[]{:S(2)}) collective-permute-start(bf16[8,96,384]{2,1,0:T(8,128)(2,1)S(1)} %copy-done.8), channel_id=1, source_target_pairs={{0,32},{1,33},{2,34},{3,35},{4,36},{5,37},{6,38},{7,39},{8,40},{9,... | collective-permute-start | bytes 1769480 | tf_op jit(solution)/shard_map/ppermute | solution.py:44
  67.3 1.5 %collective-permute-start.5 = (bf16[8,96,384]{2,1,0:T(8,128)(2,1)S(1)}, bf16[8,96,384]{2,1,0:T(8,128)(2,1)}, u32[]{:S(2)}, u32[]{:S(2)}) collective-permute-start(bf16[8,96,384]{2,1,0:T(8,128)(2,1)S(1)} %copy-done.8), channel_id=1, source_target_pairs={{0,96},{1,97},{2,98},{3,99},{4,100},{5,101},{6,102},{7,103},{8,104... | collective-permute-start | bytes 1769480 | tf_op jit(solution)/shard_map/ppermute | solution.py:44
  68.8 0.0 collective-permute-done.3.other
  68.8 3.0 %queries.1.q_ref = bf16[8,256,128]{2,1,0:T(8,128)(2,1)S(1)} custom-call(bf16[256,1536]{1,0:T(8,128)(2,1)S(1)} %get-tuple-element.16.norm_ref, f32[256,128]{1,0:T(8,128)S(1)} %copy-done.3, f32[256,128]{1,0:T(8,128)S(1)} %copy-done.5, bf16[8,96,1024]{2,1,0:T(8,128)(2,1)} %get-tuple-element.19.own, bf16[8,96,1024]{2,1,0:T(8,128)(2,1)} %collective-permute-done.3.other), custom_call_target="tpu_custom_call" | custom-call | flops 1000 | bytes 1000 | tf_op jit(solution)/shard_map/queries/pallas_call | solution.py:307
  71.9 0.0 copy-start.6
  71.9 10.1 %collective-permute-done.4.rest_1_ = bf16[8,96,384]{2,1,0:T(8,128)(2,1)S(1)} collective-permute-done((bf16[8,96,384]{2,1,0:T(8,128)(2,1)S(1)}, bf16[8,96,384]{2,1,0:T(8,128)(2,1)S(1)}, u32[]{:S(2)}, u32[]{:S(2)}) %collective-permute-start.4) | collective-permute-done | bytes 589856 | tf_op jit(solution)/shard_map/ppermute | solution.py:44
  82.0 0.8 copy-done.9
  82.8 0.0 collective-permute-done.5.rest_2_
  82.8 3.1 %all-to-all-done.1.own = bf16[8,640,128]{2,1,0:T(8,128)(2,1)S(1)} async-done(((bf16[8,640,128]{2,1,0:T(8,128)(2,1)}), bf16[8,640,128]{2,1,0:T(8,128)(2,1)S(1)}, u32[]{:S(2)}, u32[]{:S(2)}) %all-to-all-start.1) | async-done | bytes 1310752 | tf_op jit(solution)/shard_map/all_to_all | solution.py:157
  85.9 1.1 %collective-permute-start.6 = (bf16[8,640,128]{2,1,0:T(8,128)(2,1)S(1)}, bf16[8,640,128]{2,1,0:T(8,128)(2,1)S(1)}, u32[]{:S(2)}, u32[]{:S(2)}) collective-permute-start(bf16[8,640,128]{2,1,0:T(8,128)(2,1)S(1)} %all-to-all-done.1.own), channel_id=1, source_target_pairs={{0,1},{1,0},{2,3},{3,2},{4,5},{5,4},{6,7},{7,6},{8,9},{9,8},{10,11... | collective-permute-start | bytes 3932168 | tf_op jit(solution)/shard_map/ppermute | solution.py:44
  87.0 2.7 %collective-permute-start.7 = (bf16[8,96,384]{2,1,0:T(8,128)(2,1)S(1)}, bf16[8,96,384]{2,1,0:T(8,128)(2,1)S(1)}, u32[]{:S(2)}, u32[]{:S(2)}) collective-permute-start(bf16[8,96,384]{2,1,0:T(8,128)(2,1)S(1)} %copy-done.8), channel_id=1, source_target_pairs={{0,64},{1,65},{2,66},{3,67},{4,68},{5,69},{6,70},{7,71},{8,72},{9,... | collective-permute-start | bytes 1769480 | tf_op jit(solution)/shard_map/ppermute | solution.py:44
  89.8 0.3 collective-permute-start.8
  90.0 0.2 collective-permute-start.9
  90.3 0.3 collective-permute-start.10
  90.5 0.0 collective-permute-done.6.other
  90.6 11.4 %attention.1.mixed_ref = bf16[256,1536]{1,0:T(8,128)(2,1)S(1)} custom-call(bf16[8,256,128]{2,1,0:T(8,128)(2,1)S(1)} %queries.1.q_ref, bf16[8,640,128]{2,1,0:T(8,128)(2,1)S(1)} %all-to-all-done.1.own, bf16[8,640,128]{2,1,0:T(8,128)(2,1)S(1)} %collective-permute-done.6.other), custom_call_target="tpu_custom_call" | custom-call | flops 1000 | bytes 1000 | tf_op jit(solution)/shard_map/attention/pallas_call | solution.py:408
  101.9 1.6 %collective-permute-done.7.rest_3_ = bf16[8,96,384]{2,1,0:T(8,128)(2,1)S(1)} collective-permute-done((bf16[8,96,384]{2,1,0:T(8,128)(2,1)S(1)}, bf16[8,96,384]{2,1,0:T(8,128)(2,1)S(1)}, u32[]{:S(2)}, u32[]{:S(2)}) %collective-permute-start.7) | collective-permute-done | bytes 589856 | tf_op jit(solution)/shard_map/ppermute | solution.py:44
  103.5 0.8 collective-permute-start.11
  104.3 0.0 collective-permute-done.8.rest_4_
  104.3 0.0 collective-permute-done.9.rest_5_
  104.3 0.0 collective-permute-done.10.rest_6_
  104.3 1.6 %collective-permute-done.11.rest_7_ = bf16[8,96,384]{2,1,0:T(8,128)(2,1)S(1)} collective-permute-done((bf16[8,96,384]{2,1,0:T(8,128)(2,1)S(1)}, bf16[8,96,384]{2,1,0:T(8,128)(2,1)S(1)}, u32[]{:S(2)}, u32[]{:S(2)}) %collective-permute-start.11) | collective-permute-done | bytes 589856 | tf_op jit(solution)/shard_map/ppermute | solution.py:44
  105.9 0.0 copy-done.10
  105.9 3.5 %output.1 = bf16[256,1536]{1,0:T(8,128)(2,1)} custom-call(bf16[256,1536]{1,0:T(8,128)(2,1)S(1)} %attention.1.mixed_ref, bf16[256,1536]{1,0:T(8,128)(2,1)S(1)} %copy-done.6, bf16[8,96,384]{2,1,0:T(8,128)(2,1)S(1)} %copy-done.8, bf16[8,96,384]{2,1,0:T(8,128)(2,1)S(1)} %copy-done.10, bf16[8,96,384]{2,1,0:T(8,128)(2,1)} %collective-permute-done.5.rest_2_, ...), custom_call_target="tpu_custom_call" | custom-call | flops 1000 | bytes 1000 | tf_op jit(solution)/shard_map/output/pallas_call | solution.py:439
  (21 shorter events, 0.1 us)
Async XLA Ops:
  1.4 9.0 %collective-permute-start.1 = (bf16[2,1536]{1,0:T(2,128)(2,1)S(1)}, bf16[2,1536]{1,0:T(2,128)(2,1)S(1)}, u32[]{:S(2)}, u32[]{:S(2)}) collective-permute-start(bf16[2,1536]{1,0:T(2,128)(2,1)S(1)} %get-tuple-element.24), channel_id=1, source_target_pairs={{0,1},{1,0},{2,3},{3,2},{4,5},{5,4},{6,7},{7,6},{8,9},{9,8},{10,11... | collective-permute-start | bytes 18440 | tf_op jit(solution)/shard_map/ppermute | solution.py:44
  2.9 7.5 %collective-permute-start = (bf16[2,1536]{1,0:T(2,128)(2,1)S(1)}, bf16[2,1536]{1,0:T(2,128)(2,1)S(1)}, u32[]{:S(2)}, u32[]{:S(2)}) collective-permute-start(bf16[2,1536]{1,0:T(2,128)(2,1)S(1)} %get-tuple-element.25), channel_id=1, source_target_pairs={{1,2},{3,4},{5,6},{7,8},{9,10},{11,12},{13,14},{17,18},{19,20},{21... | collective-permute-start | bytes 18440 | tf_op jit(solution)/shard_map/ppermute | solution.py:44
  10.4 43.5 %all-to-all-start = ((bf16[8,96,1728]{2,1,0:T(8,128)(2,1)}), bf16[8,96,1728]{2,1,0:T(8,128)(2,1)S(1)}, u32[]{:S(2)}, u32[]{:S(2)}) async-start(bf16[8,96,1728]{2,1,0:T(8,128)(2,1)} %pack.1), calls=%async_computation | async-start | bytes 5505024 | tf_op jit(solution)/shard_map/all_to_all | solution.py:157
  17.9 1.4 %copy-start = (bf16[512,1536]{1,0:T(8,128)(2,1)S(1)}, bf16[512,1536]{1,0:T(8,128)(2,1)}, u32[]{:S(2)}) copy-start(bf16[512,1536]{1,0:T(8,128)(2,1)} %x_ref.1) | copy-start | bytes 4718596
  19.3 0.7 copy-start.11
  20.0 0.7 copy-start.12
  20.7 0.7 copy-start.13
  54.8 2.4 %collective-permute-start.2 = (bf16[8,96,320]{2,1,0:T(8,128)(2,1)}, bf16[8,96,320]{2,1,0:T(8,128)(2,1)}, u32[]{:S(2)}, u32[]{:S(2)}) collective-permute-start(bf16[8,96,320]{2,1,0:T(8,128)(2,1)} %slice.11), channel_id=1, source_target_pairs={{0,1},{1,0},{2,3},{3,2},{4,5},{5,4},{6,7},{7,6},{8,9},{9,8},{10,11... | collective-permute-start | bytes 1474568 | tf_op jit(solution)/shard_map/ppermute | solution.py:44
  55.9 4.3 %copy-start.2 = (f32[256,128]{1,0:T(8,128)}, f32[256,128]{1,0:T(8,128)S(1)}, u32[]{:S(2)}) copy-start(f32[256,128]{1,0:T(8,128)S(1)} %get-tuple-element.31.cos_ref) | copy-start | bytes 393220
  55.9 4.3 %copy-start.4 = (f32[256,128]{1,0:T(8,128)}, f32[256,128]{1,0:T(8,128)S(1)}, u32[]{:S(2)}) copy-start(f32[256,128]{1,0:T(8,128)S(1)} %get-tuple-element.32.sin_ref) | copy-start | bytes 393220
  60.2 1.1 copy-start.1
  61.3 0.8 copy-start.7
  62.1 4.0 %copy-start.8 = (bf16[8,96,384]{2,1,0:T(8,128)(2,1)S(1)}, bf16[8,96,384]{2,1,0:T(8,128)(2,1)}, u32[]{:S(2)}) copy-start(bf16[8,96,384]{2,1,0:T(8,128)(2,1)} %copy-done.7) | copy-start | bytes 1769476
  62.1 6.7 %copy-start.3 = (f32[256,128]{1,0:T(8,128)S(1)}, f32[256,128]{1,0:T(8,128)}, u32[]{:S(2)}) copy-start(f32[256,128]{1,0:T(8,128)} %copy-done.2) | copy-start | bytes 393220
  62.1 6.7 %copy-start.5 = (f32[256,128]{1,0:T(8,128)S(1)}, f32[256,128]{1,0:T(8,128)}, u32[]{:S(2)}) copy-start(f32[256,128]{1,0:T(8,128)} %copy-done.4) | copy-start | bytes 393220
  62.1 6.7 %collective-permute-start.3 = (bf16[8,96,1024]{2,1,0:T(8,128)(2,1)}, bf16[8,96,1024]{2,1,0:T(8,128)(2,1)}, u32[]{:S(2)}, u32[]{:S(2)}) collective-permute-start(bf16[8,96,1024]{2,1,0:T(8,128)(2,1)} %get-tuple-element.19.own), channel_id=1, source_target_pairs={{0,1},{1,0},{2,3},{3,2},{4,5},{5,4},{6,7},{7,6},{8,9},{9,8},{10,11... | collective-permute-start | bytes 4718600 | tf_op jit(solution)/shard_map/ppermute | solution.py:44
  62.5 23.4 %all-to-all-start.1 = ((bf16[8,640,128]{2,1,0:T(8,128)(2,1)}), bf16[8,640,128]{2,1,0:T(8,128)(2,1)S(1)}, u32[]{:S(2)}, u32[]{:S(2)}) async-start(bf16[8,640,128]{2,1,0:T(8,128)(2,1)} %copy-done.1), calls=%async_computation.1 | async-start | bytes 2621440 | tf_op jit(solution)/shard_map/all_to_all | solution.py:157
  66.1 15.9 %collective-permute-start.4 = (bf16[8,96,384]{2,1,0:T(8,128)(2,1)S(1)}, bf16[8,96,384]{2,1,0:T(8,128)(2,1)S(1)}, u32[]{:S(2)}, u32[]{:S(2)}) collective-permute-start(bf16[8,96,384]{2,1,0:T(8,128)(2,1)S(1)} %copy-done.8), channel_id=1, source_target_pairs={{0,32},{1,33},{2,34},{3,35},{4,36},{5,37},{6,38},{7,39},{8,40},{9,... | collective-permute-start | bytes 1769480 | tf_op jit(solution)/shard_map/ppermute | solution.py:44
  67.3 15.5 %collective-permute-start.5 = (bf16[8,96,384]{2,1,0:T(8,128)(2,1)S(1)}, bf16[8,96,384]{2,1,0:T(8,128)(2,1)}, u32[]{:S(2)}, u32[]{:S(2)}) collective-permute-start(bf16[8,96,384]{2,1,0:T(8,128)(2,1)S(1)} %copy-done.8), channel_id=1, source_target_pairs={{0,96},{1,97},{2,98},{3,99},{4,100},{5,101},{6,102},{7,103},{8,104... | collective-permute-start | bytes 1769480 | tf_op jit(solution)/shard_map/ppermute | solution.py:44
  71.9 34.0 %copy-start.6 = (bf16[256,1536]{1,0:T(8,128)(2,1)S(1)}, bf16[256,1536]{1,0:T(8,128)(2,1)}, u32[]{:S(2)}) copy-start(bf16[256,1536]{1,0:T(8,128)(2,1)} %get-tuple-element.11.skip_ref) | copy-start | bytes 2359300
  82.0 0.8 copy-start.9
  85.9 20.0 %copy-start.10 = (bf16[8,96,384]{2,1,0:T(8,128)(2,1)S(1)}, bf16[8,96,384]{2,1,0:T(8,128)(2,1)}, u32[]{:S(2)}) copy-start(bf16[8,96,384]{2,1,0:T(8,128)(2,1)} %copy-done.9) | copy-start | bytes 1769476
  85.9 4.7 %collective-permute-start.6 = (bf16[8,640,128]{2,1,0:T(8,128)(2,1)S(1)}, bf16[8,640,128]{2,1,0:T(8,128)(2,1)S(1)}, u32[]{:S(2)}, u32[]{:S(2)}) collective-permute-start(bf16[8,640,128]{2,1,0:T(8,128)(2,1)S(1)} %all-to-all-done.1.own), channel_id=1, source_target_pairs={{0,1},{1,0},{2,3},{3,2},{4,5},{5,4},{6,7},{7,6},{8,9},{9,8},{10,11... | collective-permute-start | bytes 3932168 | tf_op jit(solution)/shard_map/ppermute | solution.py:44
  87.0 16.5 %collective-permute-start.7 = (bf16[8,96,384]{2,1,0:T(8,128)(2,1)S(1)}, bf16[8,96,384]{2,1,0:T(8,128)(2,1)S(1)}, u32[]{:S(2)}, u32[]{:S(2)}) collective-permute-start(bf16[8,96,384]{2,1,0:T(8,128)(2,1)S(1)} %copy-done.8), channel_id=1, source_target_pairs={{0,64},{1,65},{2,66},{3,67},{4,68},{5,69},{6,70},{7,71},{8,72},{9,... | collective-permute-start | bytes 1769480 | tf_op jit(solution)/shard_map/ppermute | solution.py:44
  89.8 14.5 %collective-permute-start.8 = (bf16[8,96,384]{2,1,0:T(8,128)(2,1)S(1)}, bf16[8,96,384]{2,1,0:T(8,128)(2,1)S(1)}, u32[]{:S(2)}, u32[]{:S(2)}) collective-permute-start(bf16[8,96,384]{2,1,0:T(8,128)(2,1)S(1)} %copy-done.8), channel_id=1, source_target_pairs={{0,1},{1,0},{2,3},{3,2},{4,5},{5,4},{6,7},{7,6},{8,9},{9,8},{10,11... | collective-permute-start | bytes 1769480 | tf_op jit(solution)/shard_map/ppermute | solution.py:44
  90.0 14.2 %collective-permute-start.9 = (bf16[8,96,384]{2,1,0:T(8,128)(2,1)}, bf16[8,96,384]{2,1,0:T(8,128)(2,1)S(1)}, u32[]{:S(2)}, u32[]{:S(2)}) collective-permute-start(bf16[8,96,384]{2,1,0:T(8,128)(2,1)} %copy-done.9), channel_id=1, source_target_pairs={{0,1},{1,0},{2,3},{3,2},{4,5},{5,4},{6,7},{7,6},{8,9},{9,8},{10,11... | collective-permute-start | bytes 1769480 | tf_op jit(solution)/shard_map/ppermute | solution.py:44
  90.3 14.0 %collective-permute-start.10 = (bf16[8,96,384]{2,1,0:T(8,128)(2,1)}, bf16[8,96,384]{2,1,0:T(8,128)(2,1)S(1)}, u32[]{:S(2)}, u32[]{:S(2)}) collective-permute-start(bf16[8,96,384]{2,1,0:T(8,128)(2,1)} %collective-permute-done.5.rest_2_), channel_id=1, source_target_pairs={{0,1},{1,0},{2,3},{3,2},{4,5},{5,4},{6,7},{7,6},{8,9},{9,8},{10,11... | collective-permute-start | bytes 1769480 | tf_op jit(solution)/shard_map/ppermute | solution.py:44
  103.5 2.4 %collective-permute-start.11 = (bf16[8,96,384]{2,1,0:T(8,128)(2,1)S(1)}, bf16[8,96,384]{2,1,0:T(8,128)(2,1)S(1)}, u32[]{:S(2)}, u32[]{:S(2)}) collective-permute-start(bf16[8,96,384]{2,1,0:T(8,128)(2,1)S(1)} %collective-permute-done.7.rest_3_), channel_id=1, source_target_pairs={{0,1},{1,0},{2,3},{3,2},{4,5},{5,4},{6,7},{7,6},{8,9},{9,8},{10,11... | collective-permute-start | bytes 1769480 | tf_op jit(solution)/shard_map/ppermute | solution.py:44

commit v5 on v4

--- a/solution.py
+++ b/solution.py
@@ -157,6 +157,16 @@
     return lax.all_to_all(block, "seq", 0, 0, tiled=True, axis_index_groups=groups)
 
 
+def weights_to_same_core(block):
+    groups = [
+        [device(x, y if i % 2 == 0 else 1 - y, i // 2, i % 2, c) for i in range(8)]
+        for x in range(4)
+        for y in range(2)
+        for c in range(2)
+    ]
+    return lax.all_to_all(block, AXES, 0, 0, tiled=True, axis_index_groups=groups)
+
+
 def swapped(pieces):
     return [send(p, OTHER_CORE) for p in pieces]
 
@@ -165,19 +175,15 @@
     return lax.axis_index("dp") // 2, lax.rem(lax.axis_index("seq"), 2)
 
 
-def rows_of_quarters(buf, core):
-    x, n = own_place()[0], buf.shape[-1] // 4
-    return tuple(
-        buf.at[:, core, :, pl.ds(pl.multiple_of(lax.rem(x + d, 4) * n, 128), n)]
-        for d in (0, 3, 1, 2)
-    )
-
-
-def fill(rows_of, mine, theirs, buf, sems):
-    c = own_place()[1]
+def fill(mine, theirs, buf, sems):
+    x, c = own_place()
+    n = buf.shape[-1] // 4
+    low, high = pl.ds(0, 4), pl.ds(4, 4)
     copies = []
     for core, pieces in ((c, mine), (1 - c, theirs)):
-        for src, dst in zip(pieces, rows_of(buf, core)):
+        for d, rows, src in zip((0, 3, 1, 2, 2), (pl.ds(0, 8),) * 3 + (low, high), pieces):
+            cols = pl.ds(pl.multiple_of(lax.rem(x + d, 4) * n, 128), n)
+            dst = buf.at[rows, core, :, cols]
             copies.append(pltpu.make_async_copy(src, dst, sems.at[len(copies)]))
     for copy in copies:
         copy.start()
@@ -279,7 +285,7 @@
             pltpu.VMEM((8, 2, *other.shape[1:]), BF),
             pltpu.SemaphoreType.DMA((4,)),
         ],
-        compiler_params=pltpu.CompilerParams(vmem_limit_bytes=16 * MIB),
+        compiler_params=pltpu.CompilerParams(vmem_limit_bytes=48 * MIB),
         cost_estimate=SMALL,
         name="key_values",
     )(normed, cosine, sine, own, other)
@@ -426,8 +432,8 @@
 
 
 def output_kernel(mixed_ref, skip_ref, *rest):
-    pieces, (out_ref, buf, sems) = rest[:8], rest[8:]
-    for copy in fill(rows_of_quarters, pieces[:4], pieces[4:], buf, sems):
+    pieces, (out_ref, buf, sems) = rest[:10], rest[10:]
+    for copy in fill(pieces[:5], pieces[5:], buf, sems):
         copy.wait()
     left = mixed_ref[...]
     y = jnp.dot(left, buf[...].reshape(left.shape[1], buf.shape[-1]), preferred_element_type=F32)
@@ -439,10 +445,10 @@
     return pl.pallas_call(
         output_kernel,
         out_shape=jax.ShapeDtypeStruct((rows, width), BF),
-        in_specs=[IN_VMEM, IN_VMEM] + [ANYWHERE] * 8,
+        in_specs=[IN_VMEM, IN_VMEM] + [ANYWHERE] * 10,
         scratch_shapes=[
             pltpu.VMEM((8, 2, pieces[0].shape[1], width), BF),
-            pltpu.SemaphoreType.DMA((8,)),
+            pltpu.SemaphoreType.DMA((10,)),
         ],
         compiler_params=pltpu.CompilerParams(vmem_limit_bytes=16 * MIB),
         cost_estimate=SMALL,
@@ -479,7 +485,7 @@
     before, after = halos(x, seq)
     block = pack(q_weight, o_weight, kv_weight)
     block, before, after = lax.optimization_barrier((block, before, after))
-    block = to_same_core(block)
+    block = weights_to_same_core(block)
     skip, normed = convolve(x, before, after, conv_gain, conv_weight, conv_bias, attn_gain)
     cosine, sine = rotation(seq, rows)
     block = tied(block, normed)
@@ -487,12 +493,14 @@
         normed, cosine, sine, block, send(block[:, :, qn + on :], OTHER_CORE), qn, on
     )
     kv_same = to_same_core(kv)
-    o_parts = [o_own, *(send(o_own, along_x(k)) for k in (1, -1, 2))]
+    o_left, o_right = send(o_own, along_x(1)), send(o_own, along_x(-1))
+    o_parts = [o_own, o_left, o_right]
     q = queries(normed, cosine, sine, q_own, send(q_own, OTHER_CORE))
-    kv_same = tied(kv_same, q, *o_parts[1:3])
+    kv_same = tied(kv_same, q, o_left, o_right)
     mixed = attention(q, kv_same, send(kv_same, OTHER_CORE))
-    o_other = swapped(o_parts[:3]) + swapped([tied(o_parts[3], mixed)])
-    return skip, output(mixed, skip, o_parts + o_other)
+    o_last = [send(o_left[:4], along_x(1)), send(o_right[4:], along_x(-1))]
+    o_other = swapped(o_parts) + swapped([tied(p, mixed) for p in o_last])
+    return skip, output(mixed, skip, o_parts + o_last + o_other)
 
 
 def solution(mesh):

time: 110 us -> 108 us (0.982)
  local copies, waits for them, and re-layouts: 7.09 us -> 3.57 us
    all_to_all x0 -> x1, waiting for transfers between devices: none -> 15.6 us  [weights_to_same_core(): lax.all_to_all(block, AXES, 0, 0, tiled=True, axis_index_groups=groups)]
    all_to_all x2 -> x1, waiting for transfers between devices: 16.8 us -> 3.67 us  [to_same_core(): lax.all_to_all(block, 'seq', 0, 0, tiled=True, axis_index_groups=groups)]
    all_to_all x2 -> x1, starting transfers between devices: 11 us -> 3.57 us  [to_same_core(): lax.all_to_all(block, 'seq', 0, 0, tiled=True, axis_index_groups=groups)]
    all_to_all x0 -> x1, starting transfers between devices: none -> 7.37 us  [weights_to_same_core(): lax.all_to_all(block, AXES, 0, 0, tiled=True, axis_index_groups=groups)]
    unnamed x28 -> x10, local copies, waits for them, and re-layouts: 6.21 us -> 1.43 us
    ppermute x12 -> x14, waiting for transfers between devices: 14.6 us -> 13 us  [send(): return lax.ppermute(array, AXES, pairs)]
    ppermute x12 -> x14, starting transfers between devices: 15.3 us -> 15.3 us  [send(): return lax.ppermute(array, AXES, pairs)]
  transfers between devices with their start and end apart: 14 -> 16, of which waited for: 6 -> 6; matrix products, arithmetic and copies ran while one was open for 1% -> 2% of each run, Pallas kernels for 33% -> 33%
where the time goes in v5:
time: 108 us
  Pallas kernels  43 us (40%)
  waiting for transfers between devices  32.3 us (30%)
  starting transfers between devices  26.2 us (24%)
  local copies, waits for them, and re-layouts  3.57 us (3%)
  other arithmetic  1.49 us (1%)
    pallas_call x1, Pallas kernels, convolve(): pl.pallas_call(conv_kernel, out_shape=(out, out), grid=(width // tile,),...  18.8 us
    all_to_all x1, waiting for transfers between devices, weights_to_same_core(): lax.all_to_all(block, AXES, 0, 0, tiled=True, axis_index_groups=groups)  15.6 us
    ppermute x14, starting transfers between devices, send(): return lax.ppermute(array, AXES, pairs)  15.3 us
    ppermute x14, waiting for transfers between devices, send(): return lax.ppermute(array, AXES, pairs)  13 us
    pallas_call x1, Pallas kernels, attention(): pl.pallas_call(attention_kernel, out_shape=jax.ShapeDtypeStruct((rows, he...  11.4 us
    all_to_all x1, starting transfers between devices, weights_to_same_core(): lax.all_to_all(block, AXES, 0, 0, tiled=True, axis_index_groups=groups)  7.37 us
    all_to_all x1, waiting for transfers between devices, to_same_core(): lax.all_to_all(block, 'seq', 0, 0, tiled=True, axis_index_groups=groups)  3.67 us
    pallas_call x1, Pallas kernels, output(): pl.pallas_call(output_kernel, out_shape=jax.ShapeDtypeStruct((rows, width...  3.62 us
  transfers between devices with their start and end apart: 16, of which 6 were waited for; matrix products, arithmetic and copies ran while one was open for 2% of the time, Pallas kernels for 33%

profile of v5, /device:TPU:1, one launch (start us, length us, event | category | flops | bytes accessed | tf_op | source)
XLA Modules:
  0.0 107.6 jit_solution(13737618545077034634)
XLA Ops:
  0.6 0.8 broadcast_select_fusion.2
  1.4 1.5 %collective-permute-start.1 = (bf16[2,1536]{1,0:T(2,128)(2,1)S(1)}, bf16[2,1536]{1,0:T(2,128)(2,1)S(1)}, u32[]{:S(2)}, u32[]{:S(2)}) collective-permute-start(bf16[2,1536]{1,0:T(2,128)(2,1)S(1)} %get-tuple-element.26), channel_id=1, source_target_pairs={{0,1},{1,0},{2,3},{3,2},{4,5},{5,4},{6,7},{7,6},{8,9},{9,8},{10,11... | collective-permute-start | bytes 18440 | tf_op jit(solution)/shard_map/ppermute | solution.py:44
  2.9 4.8 %collective-permute-start = (bf16[2,1536]{1,0:T(2,128)(2,1)S(1)}, bf16[2,1536]{1,0:T(2,128)(2,1)S(1)}, u32[]{:S(2)}, u32[]{:S(2)}) collective-permute-start(bf16[2,1536]{1,0:T(2,128)(2,1)S(1)} %get-tuple-element.27), channel_id=1, source_target_pairs={{1,2},{3,4},{5,6},{7,8},{9,10},{11,12},{13,14},{17,18},{19,20},{21... | collective-permute-start | bytes 18440 | tf_op jit(solution)/shard_map/ppermute | solution.py:44
  7.7 2.7 %pack.1 = bf16[8,96,1728]{2,1,0:T(8,128)(2,1)} custom-call(bf16[96,1024]{1,0:T(8,128)(2,1)} %q_hbm.1, bf16[96,1536]{1,0:T(8,128)(2,1)} %o_hbm.1, bf16[96,320]{1,0:T(8,128)(2,1)} %kv_hbm.1), custom_call_target="tpu_custom_call" | custom-call | flops 1000 | bytes 1000 | tf_op jit(solution)/shard_map/pack/pallas_call | solution.py:222
  10.4 0.0 collective-permute-done.1
  10.4 0.0 collective-permute-done
  10.5 0.0 copy-start.2
  10.5 0.0 copy-start.3
  10.5 0.0 copy-start.4
  10.5 7.4 %all-to-all-start = ((bf16[8,96,1728]{2,1,0:T(8,128)(2,1)}), bf16[8,96,1728]{2,1,0:T(8,128)(2,1)}, u32[]{:S(2)}, u32[]{:S(2)}) async-start(bf16[8,96,1728]{2,1,0:T(8,128)(2,1)} %pack.1), calls=%async_computation | async-start | bytes 5505024 | tf_op jit(solution)/shard_map/all_to_all | solution.py:167
  17.9 0.0 copy-start
  17.9 1.4 %copy-done = bf16[512,1536]{1,0:T(8,128)(2,1)S(1)} copy-done((bf16[512,1536]{1,0:T(8,128)(2,1)S(1)}, bf16[512,1536]{1,0:T(8,128)(2,1)}, u32[]{:S(2)}) %copy-start) | copy-done | bytes 1572888
  19.3 18.8 %conv.1 = (bf16[256,1536]{1,0:T(8,128)(2,1)}, bf16[256,1536]{1,0:T(8,128)(2,1)S(1)}) custom-call(bf16[512,1536]{1,0:T(8,128)(2,1)S(1)} %copy-done, bf16[2,1536]{1,0:T(2,128)(2,1)S(1)} %get-tuple-element.14.before_ref, bf16[2,1536]{1,0:T(2,128)(2,1)S(1)} %get-tuple-element.15.after_ref, f32[1536]{0:T(1024)S(1)} %copy-done.2, f32[1536]{0:T(1024)S(1)} %copy-done.3, ...), custom_call_target="tpu_custom_call" | custom-call | flops 1000 | bytes 1000 | tf_op jit(solution)/shard_map/conv/pallas_call | solution.py:134
  38.1 15.6 %all-to-all-done.own = bf16[8,96,1728]{2,1,0:T(8,128)(2,1)} async-done(((bf16[8,96,1728]{2,1,0:T(8,128)(2,1)}), bf16[8,96,1728]{2,1,0:T(8,128)(2,1)}, u32[]{:S(2)}, u32[]{:S(2)}) %all-to-all-start) | async-done | bytes 2654240 | tf_op jit(solution)/shard_map/all_to_all | solution.py:167
  53.7 1.1 %slice.17 = bf16[8,96,320]{2,1,0:T(8,128)(2,1)S(1)} slice(bf16[8,96,1728]{2,1,0:T(8,128)(2,1)} %all-to-all-done.own), slice={[0:8], [0:96], [1408:1728]} | slice | bytes 983040 | tf_op jit(solution)/shard_map/slice | solution.py:493
  54.8 0.5 collective-permute-start.2
  55.4 0.5 fusion
  55.9 0.1 pad_maximum_fusion
  56.1 0.9 collective-permute-done.2.other
  57.0 3.6 %key_values.1 = (bf16[8,640,128]{2,1,0:T(8,128)(2,1)}, bf16[8,96,1024]{2,1,0:T(8,128)(2,1)}, bf16[8,96,384]{2,1,0:T(8,128)(2,1)}) custom-call(bf16[256,1536]{1,0:T(8,128)(2,1)S(1)} %get-tuple-element.17.norm_ref, f32[256,128]{1,0:T(8,128)S(1)} %get-tuple-element.33.cos_ref, f32[256,128]{1,0:T(8,128)S(1)} %get-tuple-element.34.sin_ref, ...), custom_call_target="tpu_custom_call" | custom-call | flops 1000 | bytes 1000 | tf_op jit(solution)/shard_map/key_values/pallas_call | solution.py:275
  60.5 0.5 collective-permute-start.3
  61.0 3.6 %all-to-all-start.1 = ((bf16[8,640,128]{2,1,0:T(8,128)(2,1)}), bf16[8,640,128]{2,1,0:T(8,128)(2,1)S(1)}, u32[]{:S(2)}, u32[]{:S(2)}) async-start(bf16[8,640,128]{2,1,0:T(8,128)(2,1)} %get-tuple-element.21), calls=%async_computation.1 | async-start | bytes 2621440 | tf_op jit(solution)/shard_map/all_to_all | solution.py:157
  64.6 1.3 %collective-permute-start.4 = (bf16[8,96,384]{2,1,0:T(8,128)(2,1)}, bf16[8,96,384]{2,1,0:T(8,128)(2,1)S(1)}, u32[]{:S(2)}, u32[]{:S(2)}) collective-permute-start(bf16[8,96,384]{2,1,0:T(8,128)(2,1)} %get-tuple-element.22.rest_0_), channel_id=1, source_target_pairs={{0,32},{1,33},{2,34},{3,35},{4,36},{5,37},{6,38},{7,39},{8,40},{9,... | collective-permute-start | bytes 1769480 | tf_op jit(solution)/shard_map/ppermute | solution.py:44
  65.9 1.5 %collective-permute-start.5 = (bf16[8,96,384]{2,1,0:T(8,128)(2,1)}, bf16[8,96,384]{2,1,0:T(8,128)(2,1)}, u32[]{:S(2)}, u32[]{:S(2)}) collective-permute-start(bf16[8,96,384]{2,1,0:T(8,128)(2,1)} %get-tuple-element.22.rest_0_), channel_id=1, source_target_pairs={{0,96},{1,97},{2,98},{3,99},{4,100},{5,101},{6,102},{7,103},{8,104... | collective-permute-start | bytes 1769480 | tf_op jit(solution)/shard_map/ppermute | solution.py:44
  67.3 0.0 collective-permute-done.3.other
  67.3 3.0 %queries.1.q_ref = bf16[8,256,128]{2,1,0:T(8,128)(2,1)S(1)} custom-call(bf16[256,1536]{1,0:T(8,128)(2,1)S(1)} %get-tuple-element.17.norm_ref, f32[256,128]{1,0:T(8,128)S(1)} %get-tuple-element.33.cos_ref, f32[256,128]{1,0:T(8,128)S(1)} %get-tuple-element.34.sin_ref, bf16[8,96,1024]{2,1,0:T(8,128)(2,1)} %get-tuple-element.20.own, ...), custom_call_target="tpu_custom_call" | custom-call | flops 1000 | bytes 1000 | tf_op jit(solution)/shard_map/queries/pallas_call | solution.py:313
  70.3 10.5 %collective-permute-done.4.rest_1_ = bf16[8,96,384]{2,1,0:T(8,128)(2,1)S(1)} collective-permute-done((bf16[8,96,384]{2,1,0:T(8,128)(2,1)}, bf16[8,96,384]{2,1,0:T(8,128)(2,1)S(1)}, u32[]{:S(2)}, u32[]{:S(2)}) %collective-permute-start.4) | collective-permute-done | bytes 589856 | tf_op jit(solution)/shard_map/ppermute | solution.py:44
  80.9 0.0 collective-permute-done.5.rest_2_
  80.9 3.7 %all-to-all-done.1.own = bf16[8,640,128]{2,1,0:T(8,128)(2,1)S(1)} async-done(((bf16[8,640,128]{2,1,0:T(8,128)(2,1)}), bf16[8,640,128]{2,1,0:T(8,128)(2,1)S(1)}, u32[]{:S(2)}, u32[]{:S(2)}) %all-to-all-start.1) | async-done | bytes 1310752 | tf_op jit(solution)/shard_map/all_to_all | solution.py:157
  84.5 1.0 collective-permute-start.6
  85.6 1.3 %collective-permute-start.7 = (bf16[4,96,384]{2,1,0:T(8,128)(2,1)S(1)}, bf16[4,96,384]{2,1,0:T(8,128)(2,1)S(1)}, u32[]{:S(2)}, u32[]{:S(2)}) collective-permute-start(bf16[4,96,384]{2,1,0:T(8,128)(2,1)S(1)} %slice.20), channel_id=1, source_target_pairs={{0,32},{1,33},{2,34},{3,35},{4,36},{5,37},{6,38},{7,39},{8,40},{9,... | collective-permute-start | bytes 884744 | tf_op jit(solution)/shard_map/ppermute | solution.py:44
  86.8 0.3 collective-permute-start.9
  87.1 1.0 slice.21
  88.1 0.0 copy-start.1
  88.1 1.5 %collective-permute-start.8 = (bf16[4,96,384]{2,1,0:T(8,128)(2,1)S(1)}, bf16[4,96,384]{2,1,0:T(8,128)(2,1)S(1)}, u32[]{:S(2)}, u32[]{:S(2)}) collective-permute-start(bf16[4,96,384]{2,1,0:T(8,128)(2,1)S(1)} %slice.21), channel_id=1, source_target_pairs={{0,96},{1,97},{2,98},{3,99},{4,100},{5,101},{6,102},{7,103},{8,104... | collective-permute-start | bytes 884744 | tf_op jit(solution)/shard_map/ppermute | solution.py:44
  89.7 0.5 collective-permute-start.10
  90.2 0.0 collective-permute-done.6.other
  90.2 0.0 collective-permute-start.11
  90.2 11.4 %attention.1.mixed_ref = bf16[256,1536]{1,0:T(8,128)(2,1)S(1)} custom-call(bf16[8,256,128]{2,1,0:T(8,128)(2,1)S(1)} %queries.1.q_ref, bf16[8,640,128]{2,1,0:T(8,128)(2,1)S(1)} %all-to-all-done.1.own, bf16[8,640,128]{2,1,0:T(8,128)(2,1)S(1)} %collective-permute-done.6.other), custom_call_target="tpu_custom_call" | custom-call | flops 1000 | bytes 1000 | tf_op jit(solution)/shard_map/attention/pallas_call | solution.py:414
  101.6 0.0 collective-permute-done.7.rest_3_
  101.6 0.6 collective-permute-start.12
  102.1 0.0 collective-permute-done.8.rest_4_
  102.2 0.1 collective-permute-start.13
  102.3 0.0 collective-permute-done.9.rest_5_
  102.3 0.0 collective-permute-done.11.rest_7_
  102.3 1.1 %collective-permute-done.12.rest_8_ = bf16[4,96,384]{2,1,0:T(8,128)(2,1)S(1)} collective-permute-done((bf16[4,96,384]{2,1,0:T(8,128)(2,1)S(1)}, bf16[4,96,384]{2,1,0:T(8,128)(2,1)S(1)}, u32[]{:S(2)}, u32[]{:S(2)}) %collective-permute-start.12) | collective-permute-done | bytes 294944 | tf_op jit(solution)/shard_map/ppermute | solution.py:44
  103.4 0.4 collective-permute-done.13.rest_9_
  103.8 3.6 %output.1 = bf16[256,1536]{1,0:T(8,128)(2,1)} custom-call(bf16[256,1536]{1,0:T(8,128)(2,1)S(1)} %attention.1.mixed_ref, bf16[256,1536]{1,0:T(8,128)(2,1)S(1)} %copy-done.1, bf16[8,96,384]{2,1,0:T(8,128)(2,1)} %get-tuple-element.22.rest_0_, bf16[8,96,384]{2,1,0:T(8,128)(2,1)S(1)} %collective-permute-done.4.rest_1_, ...), custom_call_target="tpu_custom_call" | custom-call | flops 1000 | bytes 1000 | tf_op jit(solution)/shard_map/output/pallas_call | solution.py:445
  (9 shorter events, 0.1 us)
Async XLA Ops:
  1.4 9.0 %collective-permute-start.1 = (bf16[2,1536]{1,0:T(2,128)(2,1)S(1)}, bf16[2,1536]{1,0:T(2,128)(2,1)S(1)}, u32[]{:S(2)}, u32[]{:S(2)}) collective-permute-start(bf16[2,1536]{1,0:T(2,128)(2,1)S(1)} %get-tuple-element.26), channel_id=1, source_target_pairs={{0,1},{1,0},{2,3},{3,2},{4,5},{5,4},{6,7},{7,6},{8,9},{9,8},{10,11... | collective-permute-start | bytes 18440 | tf_op jit(solution)/shard_map/ppermute | solution.py:44
  2.9 7.5 %collective-permute-start = (bf16[2,1536]{1,0:T(2,128)(2,1)S(1)}, bf16[2,1536]{1,0:T(2,128)(2,1)S(1)}, u32[]{:S(2)}, u32[]{:S(2)}) collective-permute-start(bf16[2,1536]{1,0:T(2,128)(2,1)S(1)} %get-tuple-element.27), channel_id=1, source_target_pairs={{1,2},{3,4},{5,6},{7,8},{9,10},{11,12},{13,14},{17,18},{19,20},{21... | collective-permute-start | bytes 18440 | tf_op jit(solution)/shard_map/ppermute | solution.py:44
  10.5 7.4 %copy-start.2 = (f32[1536]{0:T(1024)S(1)}, f32[1536]{0:T(1024)}, u32[]{:S(2)}) copy-start(f32[1536]{0:T(1024)} %cg_ref.1) | copy-start | bytes 18436
  10.5 7.4 %copy-start.3 = (f32[1536]{0:T(1024)S(1)}, f32[1536]{0:T(1024)}, u32[]{:S(2)}) copy-start(f32[1536]{0:T(1024)} %bias_ref.1) | copy-start | bytes 18436
  10.5 7.4 %copy-start.4 = (f32[1536]{0:T(1024)S(1)}, f32[1536]{0:T(1024)}, u32[]{:S(2)}) copy-start(f32[1536]{0:T(1024)} %ag_ref.1) | copy-start | bytes 18436
  10.5 43.2 %all-to-all-start = ((bf16[8,96,1728]{2,1,0:T(8,128)(2,1)}), bf16[8,96,1728]{2,1,0:T(8,128)(2,1)}, u32[]{:S(2)}, u32[]{:S(2)}) async-start(bf16[8,96,1728]{2,1,0:T(8,128)(2,1)} %pack.1), calls=%async_computation | async-start | bytes 5505024 | tf_op jit(solution)/shard_map/all_to_all | solution.py:167
  17.9 1.4 %copy-start = (bf16[512,1536]{1,0:T(8,128)(2,1)S(1)}, bf16[512,1536]{1,0:T(8,128)(2,1)}, u32[]{:S(2)}) copy-start(bf16[512,1536]{1,0:T(8,128)(2,1)} %x_ref.1) | copy-start | bytes 4718596
  54.8 2.1 %collective-permute-start.2 = (bf16[8,96,320]{2,1,0:T(8,128)(2,1)S(1)}, bf16[8,96,320]{2,1,0:T(8,128)(2,1)S(1)}, u32[]{:S(2)}, u32[]{:S(2)}) collective-permute-start(bf16[8,96,320]{2,1,0:T(8,128)(2,1)S(1)} %slice.17), channel_id=1, source_target_pairs={{0,1},{1,0},{2,3},{3,2},{4,5},{5,4},{6,7},{7,6},{8,9},{9,8},{10,11... | collective-permute-start | bytes 1474568 | tf_op jit(solution)/shard_map/ppermute | solution.py:44
  60.5 6.8 %collective-permute-start.3 = (bf16[8,96,1024]{2,1,0:T(8,128)(2,1)}, bf16[8,96,1024]{2,1,0:T(8,128)(2,1)}, u32[]{:S(2)}, u32[]{:S(2)}) collective-permute-start(bf16[8,96,1024]{2,1,0:T(8,128)(2,1)} %get-tuple-element.20.own), channel_id=1, source_target_pairs={{0,1},{1,0},{2,3},{3,2},{4,5},{5,4},{6,7},{7,6},{8,9},{9,8},{10,11... | collective-permute-start | bytes 4718600 | tf_op jit(solution)/shard_map/ppermute | solution.py:44
  61.0 23.5 %all-to-all-start.1 = ((bf16[8,640,128]{2,1,0:T(8,128)(2,1)}), bf16[8,640,128]{2,1,0:T(8,128)(2,1)S(1)}, u32[]{:S(2)}, u32[]{:S(2)}) async-start(bf16[8,640,128]{2,1,0:T(8,128)(2,1)} %get-tuple-element.21), calls=%async_computation.1 | async-start | bytes 2621440 | tf_op jit(solution)/shard_map/all_to_all | solution.py:157
  64.6 16.3 %collective-permute-start.4 = (bf16[8,96,384]{2,1,0:T(8,128)(2,1)}, bf16[8,96,384]{2,1,0:T(8,128)(2,1)S(1)}, u32[]{:S(2)}, u32[]{:S(2)}) collective-permute-start(bf16[8,96,384]{2,1,0:T(8,128)(2,1)} %get-tuple-element.22.rest_0_), channel_id=1, source_target_pairs={{0,32},{1,33},{2,34},{3,35},{4,36},{5,37},{6,38},{7,39},{8,40},{9,... | collective-permute-start | bytes 1769480 | tf_op jit(solution)/shard_map/ppermute | solution.py:44
  65.9 15.0 %collective-permute-start.5 = (bf16[8,96,384]{2,1,0:T(8,128)(2,1)}, bf16[8,96,384]{2,1,0:T(8,128)(2,1)}, u32[]{:S(2)}, u32[]{:S(2)}) collective-permute-start(bf16[8,96,384]{2,1,0:T(8,128)(2,1)} %get-tuple-element.22.rest_0_), channel_id=1, source_target_pairs={{0,96},{1,97},{2,98},{3,99},{4,100},{5,101},{6,102},{7,103},{8,104... | collective-permute-start | bytes 1769480 | tf_op jit(solution)/shard_map/ppermute | solution.py:44
  84.5 5.7 %collective-permute-start.6 = (bf16[8,640,128]{2,1,0:T(8,128)(2,1)S(1)}, bf16[8,640,128]{2,1,0:T(8,128)(2,1)S(1)}, u32[]{:S(2)}, u32[]{:S(2)}) collective-permute-start(bf16[8,640,128]{2,1,0:T(8,128)(2,1)S(1)} %all-to-all-done.1.own), channel_id=1, source_target_pairs={{0,1},{1,0},{2,3},{3,2},{4,5},{5,4},{6,7},{7,6},{8,9},{9,8},{10,11... | collective-permute-start | bytes 3932168 | tf_op jit(solution)/shard_map/ppermute | solution.py:44
  85.6 16.0 %collective-permute-start.7 = (bf16[4,96,384]{2,1,0:T(8,128)(2,1)S(1)}, bf16[4,96,384]{2,1,0:T(8,128)(2,1)S(1)}, u32[]{:S(2)}, u32[]{:S(2)}) collective-permute-start(bf16[4,96,384]{2,1,0:T(8,128)(2,1)S(1)} %slice.20), channel_id=1, source_target_pairs={{0,32},{1,33},{2,34},{3,35},{4,36},{5,37},{6,38},{7,39},{8,40},{9,... | collective-permute-start | bytes 884744 | tf_op jit(solution)/shard_map/ppermute | solution.py:44
  86.8 15.4 %collective-permute-start.9 = (bf16[8,96,384]{2,1,0:T(8,128)(2,1)}, bf16[8,96,384]{2,1,0:T(8,128)(2,1)S(1)}, u32[]{:S(2)}, u32[]{:S(2)}) collective-permute-start(bf16[8,96,384]{2,1,0:T(8,128)(2,1)} %get-tuple-element.22.rest_0_), channel_id=1, source_target_pairs={{0,1},{1,0},{2,3},{3,2},{4,5},{5,4},{6,7},{7,6},{8,9},{9,8},{10,11... | collective-permute-start | bytes 1769480 | tf_op jit(solution)/shard_map/ppermute | solution.py:44
  88.1 15.7 %copy-start.1 = (bf16[256,1536]{1,0:T(8,128)(2,1)S(1)}, bf16[256,1536]{1,0:T(8,128)(2,1)}, u32[]{:S(2)}) copy-start(bf16[256,1536]{1,0:T(8,128)(2,1)} %get-tuple-element.12.skip_ref) | copy-start | bytes 2359300
  88.1 14.0 %collective-permute-start.8 = (bf16[4,96,384]{2,1,0:T(8,128)(2,1)S(1)}, bf16[4,96,384]{2,1,0:T(8,128)(2,1)S(1)}, u32[]{:S(2)}, u32[]{:S(2)}) collective-permute-start(bf16[4,96,384]{2,1,0:T(8,128)(2,1)S(1)} %slice.21), channel_id=1, source_target_pairs={{0,96},{1,97},{2,98},{3,99},{4,100},{5,101},{6,102},{7,103},{8,104... | collective-permute-start | bytes 884744 | tf_op jit(solution)/shard_map/ppermute | solution.py:44
  89.7 12.6 %collective-permute-start.10 = (bf16[8,96,384]{2,1,0:T(8,128)(2,1)S(1)}, bf16[8,96,384]{2,1,0:T(8,128)(2,1)S(1)}, u32[]{:S(2)}, u32[]{:S(2)}) collective-permute-start(bf16[8,96,384]{2,1,0:T(8,128)(2,1)S(1)} %collective-permute-done.4.rest_1_), channel_id=1, source_target_pairs={{0,1},{1,0},{2,3},{3,2},{4,5},{5,4},{6,7},{7,6},{8,9},{9,8},{10,11... | collective-permute-start | bytes 1769480 | tf_op jit(solution)/shard_map/ppermute | solution.py:44
  90.2 12.1 %collective-permute-start.11 = (bf16[8,96,384]{2,1,0:T(8,128)(2,1)}, bf16[8,96,384]{2,1,0:T(8,128)(2,1)S(1)}, u32[]{:S(2)}, u32[]{:S(2)}) collective-permute-start(bf16[8,96,384]{2,1,0:T(8,128)(2,1)} %collective-permute-done.5.rest_2_), channel_id=1, source_target_pairs={{0,1},{1,0},{2,3},{3,2},{4,5},{5,4},{6,7},{7,6},{8,9},{9,8},{10,11... | collective-permute-start | bytes 1769480 | tf_op jit(solution)/shard_map/ppermute | solution.py:44
  101.6 1.8 %collective-permute-start.12 = (bf16[4,96,384]{2,1,0:T(8,128)(2,1)S(1)}, bf16[4,96,384]{2,1,0:T(8,128)(2,1)S(1)}, u32[]{:S(2)}, u32[]{:S(2)}) collective-permute-start(bf16[4,96,384]{2,1,0:T(8,128)(2,1)S(1)} %collective-permute-done.7.rest_3_), channel_id=1, source_target_pairs={{0,1},{1,0},{2,3},{3,2},{4,5},{5,4},{6,7},{7,6},{8,9},{9,8},{10,11... | collective-permute-start | bytes 884744 | tf_op jit(solution)/shard_map/ppermute | solution.py:44
  102.2 1.6 %collective-permute-start.13 = (bf16[4,96,384]{2,1,0:T(8,128)(2,1)S(1)}, bf16[4,96,384]{2,1,0:T(8,128)(2,1)S(1)}, u32[]{:S(2)}, u32[]{:S(2)}) collective-permute-start(bf16[4,96,384]{2,1,0:T(8,128)(2,1)S(1)} %collective-permute-done.8.rest_4_), channel_id=1, source_target_pairs={{0,1},{1,0},{2,3},{3,2},{4,5},{5,4},{6,7},{7,6},{8,9},{9,8},{10,11... | collective-permute-start | bytes 884744 | tf_op jit(solution)/shard_map/ppermute | solution.py:44

commit v6 on v5

--- a/solution.py
+++ b/solution.py
@@ -146,7 +146,7 @@
             pltpu.VMEM((2, taps, width, tile), BF),
             pltpu.SemaphoreType.DMA((2,)),
         ],
-        compiler_params=pltpu.CompilerParams(vmem_limit_bytes=36 * MIB),
+        compiler_params=pltpu.CompilerParams(vmem_limit_bytes=34 * MIB),
         cost_estimate=SMALL,
         name="conv",
     )(x, before, after, conv_gain, conv_bias, attn_gain, conv_weight)
@@ -425,7 +425,7 @@
             pltpu.VMEM((heads, rows, DV), F32),
             pltpu.SemaphoreType.DMA((6,)),
         ],
-        compiler_params=pltpu.CompilerParams(vmem_limit_bytes=32 * MIB),
+        compiler_params=pltpu.CompilerParams(vmem_limit_bytes=24 * MIB),
         cost_estimate=SMALL,
         name="attention",
     )(q, own, other)

time: 108 us -> 108 us (level)
  no operation moved by 1% of the time
where the time goes in v6:
time: 108 us
  Pallas kernels  43 us (40%)
  waiting for transfers between devices  32.3 us (30%)
  starting transfers between devices  26.2 us (24%)
  local copies, waits for them, and re-layouts  3.57 us (3%)
  other arithmetic  1.49 us (1%)
    pallas_call x1, Pallas kernels, convolve(): pl.pallas_call(conv_kernel, out_shape=(out, out), grid=(width // tile,),...  18.8 us
    all_to_all x1, waiting for transfers between devices, weights_to_same_core(): lax.all_to_all(block, AXES, 0, 0, tiled=True, axis_index_groups=groups)  15.6 us
    ppermute x14, starting transfers between devices, send(): return lax.ppermute(array, AXES, pairs)  15.3 us
    ppermute x14, waiting for transfers between devices, send(): return lax.ppermute(array, AXES, pairs)  13 us
    pallas_call x1, Pallas kernels, attention(): pl.pallas_call(attention_kernel, out_shape=jax.ShapeDtypeStruct((rows, he...  11.4 us
    all_to_all x1, starting transfers between devices, weights_to_same_core(): lax.all_to_all(block, AXES, 0, 0, tiled=True, axis_index_groups=groups)  7.37 us
    all_to_all x1, waiting for transfers between devices, to_same_core(): lax.all_to_all(block, 'seq', 0, 0, tiled=True, axis_index_groups=groups)  3.67 us
    pallas_call x1, Pallas kernels, output(): pl.pallas_call(output_kernel, out_shape=jax.ShapeDtypeStruct((rows, width...  3.62 us
  transfers between devices with their start and end apart: 16, of which 6 were waited for; matrix products, arithmetic and copies ran while one was open for 2% of the time, Pallas kernels for 33%

profile of v6, /device:TPU:1, one launch (start us, length us, event | category | flops | bytes accessed | tf_op | source)
XLA Modules:
  0.0 107.6 jit_solution(13911059214184495693)
XLA Ops:
  0.6 0.8 broadcast_select_fusion.2
  1.4 1.5 %collective-permute-start.1 = (bf16[2,1536]{1,0:T(2,128)(2,1)S(1)}, bf16[2,1536]{1,0:T(2,128)(2,1)S(1)}, u32[]{:S(2)}, u32[]{:S(2)}) collective-permute-start(bf16[2,1536]{1,0:T(2,128)(2,1)S(1)} %get-tuple-element.26), channel_id=1, source_target_pairs={{0,1},{1,0},{2,3},{3,2},{4,5},{5,4},{6,7},{7,6},{8,9},{9,8},{10,11... | collective-permute-start | bytes 18440 | tf_op jit(solution)/shard_map/ppermute | solution.py:44
  2.9 4.8 %collective-permute-start = (bf16[2,1536]{1,0:T(2,128)(2,1)S(1)}, bf16[2,1536]{1,0:T(2,128)(2,1)S(1)}, u32[]{:S(2)}, u32[]{:S(2)}) collective-permute-start(bf16[2,1536]{1,0:T(2,128)(2,1)S(1)} %get-tuple-element.27), channel_id=1, source_target_pairs={{1,2},{3,4},{5,6},{7,8},{9,10},{11,12},{13,14},{17,18},{19,20},{21... | collective-permute-start | bytes 18440 | tf_op jit(solution)/shard_map/ppermute | solution.py:44
  7.7 2.7 %pack.1 = bf16[8,96,1728]{2,1,0:T(8,128)(2,1)} custom-call(bf16[96,1024]{1,0:T(8,128)(2,1)} %q_hbm.1, bf16[96,1536]{1,0:T(8,128)(2,1)} %o_hbm.1, bf16[96,320]{1,0:T(8,128)(2,1)} %kv_hbm.1), custom_call_target="tpu_custom_call" | custom-call | flops 1000 | bytes 1000 | tf_op jit(solution)/shard_map/pack/pallas_call | solution.py:222
  10.4 0.0 collective-permute-done.1
  10.4 0.0 collective-permute-done
  10.5 0.0 copy-start.2
  10.5 0.0 copy-start.3
  10.5 0.0 copy-start.4
  10.5 7.4 %all-to-all-start = ((bf16[8,96,1728]{2,1,0:T(8,128)(2,1)}), bf16[8,96,1728]{2,1,0:T(8,128)(2,1)}, u32[]{:S(2)}, u32[]{:S(2)}) async-start(bf16[8,96,1728]{2,1,0:T(8,128)(2,1)} %pack.1), calls=%async_computation | async-start | bytes 5505024 | tf_op jit(solution)/shard_map/all_to_all | solution.py:167
  17.9 0.0 copy-start
  17.9 1.4 %copy-done = bf16[512,1536]{1,0:T(8,128)(2,1)S(1)} copy-done((bf16[512,1536]{1,0:T(8,128)(2,1)S(1)}, bf16[512,1536]{1,0:T(8,128)(2,1)}, u32[]{:S(2)}) %copy-start) | copy-done | bytes 1572888
  19.3 18.8 %conv.1 = (bf16[256,1536]{1,0:T(8,128)(2,1)}, bf16[256,1536]{1,0:T(8,128)(2,1)S(1)}) custom-call(bf16[512,1536]{1,0:T(8,128)(2,1)S(1)} %copy-done, bf16[2,1536]{1,0:T(2,128)(2,1)S(1)} %get-tuple-element.14.before_ref, bf16[2,1536]{1,0:T(2,128)(2,1)S(1)} %get-tuple-element.15.after_ref, f32[1536]{0:T(1024)S(1)} %copy-done.2, f32[1536]{0:T(1024)S(1)} %copy-done.3, ...), custom_call_target="tpu_custom_call" | custom-call | flops 1000 | bytes 1000 | tf_op jit(solution)/shard_map/conv/pallas_call | solution.py:134
  38.1 15.6 %all-to-all-done.own = bf16[8,96,1728]{2,1,0:T(8,128)(2,1)} async-done(((bf16[8,96,1728]{2,1,0:T(8,128)(2,1)}), bf16[8,96,1728]{2,1,0:T(8,128)(2,1)}, u32[]{:S(2)}, u32[]{:S(2)}) %all-to-all-start) | async-done | bytes 2654240 | tf_op jit(solution)/shard_map/all_to_all | solution.py:167
  53.7 1.1 %slice.17 = bf16[8,96,320]{2,1,0:T(8,128)(2,1)S(1)} slice(bf16[8,96,1728]{2,1,0:T(8,128)(2,1)} %all-to-all-done.own), slice={[0:8], [0:96], [1408:1728]} | slice | bytes 983040 | tf_op jit(solution)/shard_map/slice | solution.py:493
  54.8 0.5 collective-permute-start.2
  55.4 0.5 fusion
  55.9 0.1 pad_maximum_fusion
  56.1 0.9 collective-permute-done.2.other
  57.0 3.6 %key_values.1 = (bf16[8,640,128]{2,1,0:T(8,128)(2,1)}, bf16[8,96,1024]{2,1,0:T(8,128)(2,1)}, bf16[8,96,384]{2,1,0:T(8,128)(2,1)}) custom-call(bf16[256,1536]{1,0:T(8,128)(2,1)S(1)} %get-tuple-element.17.norm_ref, f32[256,128]{1,0:T(8,128)S(1)} %get-tuple-element.33.cos_ref, f32[256,128]{1,0:T(8,128)S(1)} %get-tuple-element.34.sin_ref, ...), custom_call_target="tpu_custom_call" | custom-call | flops 1000 | bytes 1000 | tf_op jit(solution)/shard_map/key_values/pallas_call | solution.py:275
  60.5 0.5 collective-permute-start.3
  61.0 3.6 %all-to-all-start.1 = ((bf16[8,640,128]{2,1,0:T(8,128)(2,1)}), bf16[8,640,128]{2,1,0:T(8,128)(2,1)S(1)}, u32[]{:S(2)}, u32[]{:S(2)}) async-start(bf16[8,640,128]{2,1,0:T(8,128)(2,1)} %get-tuple-element.21), calls=%async_computation.1 | async-start | bytes 2621440 | tf_op jit(solution)/shard_map/all_to_all | solution.py:157
  64.6 1.3 %collective-permute-start.4 = (bf16[8,96,384]{2,1,0:T(8,128)(2,1)}, bf16[8,96,384]{2,1,0:T(8,128)(2,1)S(1)}, u32[]{:S(2)}, u32[]{:S(2)}) collective-permute-start(bf16[8,96,384]{2,1,0:T(8,128)(2,1)} %get-tuple-element.22.rest_0_), channel_id=1, source_target_pairs={{0,32},{1,33},{2,34},{3,35},{4,36},{5,37},{6,38},{7,39},{8,40},{9,... | collective-permute-start | bytes 1769480 | tf_op jit(solution)/shard_map/ppermute | solution.py:44
  65.9 1.5 %collective-permute-start.5 = (bf16[8,96,384]{2,1,0:T(8,128)(2,1)}, bf16[8,96,384]{2,1,0:T(8,128)(2,1)}, u32[]{:S(2)}, u32[]{:S(2)}) collective-permute-start(bf16[8,96,384]{2,1,0:T(8,128)(2,1)} %get-tuple-element.22.rest_0_), channel_id=1, source_target_pairs={{0,96},{1,97},{2,98},{3,99},{4,100},{5,101},{6,102},{7,103},{8,104... | collective-permute-start | bytes 1769480 | tf_op jit(solution)/shard_map/ppermute | solution.py:44
  67.3 0.0 collective-permute-done.3.other
  67.3 3.0 %queries.1.q_ref = bf16[8,256,128]{2,1,0:T(8,128)(2,1)S(1)} custom-call(bf16[256,1536]{1,0:T(8,128)(2,1)S(1)} %get-tuple-element.17.norm_ref, f32[256,128]{1,0:T(8,128)S(1)} %get-tuple-element.33.cos_ref, f32[256,128]{1,0:T(8,128)S(1)} %get-tuple-element.34.sin_ref, bf16[8,96,1024]{2,1,0:T(8,128)(2,1)} %get-tuple-element.20.own, ...), custom_call_target="tpu_custom_call" | custom-call | flops 1000 | bytes 1000 | tf_op jit(solution)/shard_map/queries/pallas_call | solution.py:313
  70.3 10.5 %collective-permute-done.4.rest_1_ = bf16[8,96,384]{2,1,0:T(8,128)(2,1)S(1)} collective-permute-done((bf16[8,96,384]{2,1,0:T(8,128)(2,1)}, bf16[8,96,384]{2,1,0:T(8,128)(2,1)S(1)}, u32[]{:S(2)}, u32[]{:S(2)}) %collective-permute-start.4) | collective-permute-done | bytes 589856 | tf_op jit(solution)/shard_map/ppermute | solution.py:44
  80.9 0.0 collective-permute-done.5.rest_2_
  80.9 3.7 %all-to-all-done.1.own = bf16[8,640,128]{2,1,0:T(8,128)(2,1)S(1)} async-done(((bf16[8,640,128]{2,1,0:T(8,128)(2,1)}), bf16[8,640,128]{2,1,0:T(8,128)(2,1)S(1)}, u32[]{:S(2)}, u32[]{:S(2)}) %all-to-all-start.1) | async-done | bytes 1310752 | tf_op jit(solution)/shard_map/all_to_all | solution.py:157
  84.5 1.0 collective-permute-start.6
  85.6 1.3 %collective-permute-start.7 = (bf16[4,96,384]{2,1,0:T(8,128)(2,1)S(1)}, bf16[4,96,384]{2,1,0:T(8,128)(2,1)S(1)}, u32[]{:S(2)}, u32[]{:S(2)}) collective-permute-start(bf16[4,96,384]{2,1,0:T(8,128)(2,1)S(1)} %slice.20), channel_id=1, source_target_pairs={{0,32},{1,33},{2,34},{3,35},{4,36},{5,37},{6,38},{7,39},{8,40},{9,... | collective-permute-start | bytes 884744 | tf_op jit(solution)/shard_map/ppermute | solution.py:44
  86.8 0.3 collective-permute-start.9
  87.1 1.0 slice.21
  88.1 0.0 copy-start.1
  88.1 1.5 %collective-permute-start.8 = (bf16[4,96,384]{2,1,0:T(8,128)(2,1)S(1)}, bf16[4,96,384]{2,1,0:T(8,128)(2,1)S(1)}, u32[]{:S(2)}, u32[]{:S(2)}) collective-permute-start(bf16[4,96,384]{2,1,0:T(8,128)(2,1)S(1)} %slice.21), channel_id=1, source_target_pairs={{0,96},{1,97},{2,98},{3,99},{4,100},{5,101},{6,102},{7,103},{8,104... | collective-permute-start | bytes 884744 | tf_op jit(solution)/shard_map/ppermute | solution.py:44
  89.7 0.5 collective-permute-start.10
  90.2 0.0 collective-permute-done.6.other
  90.2 0.0 collective-permute-start.11
  90.2 11.4 %attention.1.mixed_ref = bf16[256,1536]{1,0:T(8,128)(2,1)S(1)} custom-call(bf16[8,256,128]{2,1,0:T(8,128)(2,1)S(1)} %queries.1.q_ref, bf16[8,640,128]{2,1,0:T(8,128)(2,1)S(1)} %all-to-all-done.1.own, bf16[8,640,128]{2,1,0:T(8,128)(2,1)S(1)} %collective-permute-done.6.other), custom_call_target="tpu_custom_call" | custom-call | flops 1000 | bytes 1000 | tf_op jit(solution)/shard_map/attention/pallas_call | solution.py:414
  101.6 0.0 collective-permute-done.7.rest_3_
  101.6 0.6 collective-permute-start.12
  102.1 0.0 collective-permute-done.8.rest_4_
  102.2 0.1 collective-permute-start.13
  102.3 0.0 collective-permute-done.9.rest_5_
  102.3 0.0 collective-permute-done.11.rest_7_
  102.3 1.1 %collective-permute-done.12.rest_8_ = bf16[4,96,384]{2,1,0:T(8,128)(2,1)S(1)} collective-permute-done((bf16[4,96,384]{2,1,0:T(8,128)(2,1)S(1)}, bf16[4,96,384]{2,1,0:T(8,128)(2,1)S(1)}, u32[]{:S(2)}, u32[]{:S(2)}) %collective-permute-start.12) | collective-permute-done | bytes 294944 | tf_op jit(solution)/shard_map/ppermute | solution.py:44
  103.4 0.4 collective-permute-done.13.rest_9_
  103.8 3.6 %output.1 = bf16[256,1536]{1,0:T(8,128)(2,1)} custom-call(bf16[256,1536]{1,0:T(8,128)(2,1)S(1)} %attention.1.mixed_ref, bf16[256,1536]{1,0:T(8,128)(2,1)S(1)} %copy-done.1, bf16[8,96,384]{2,1,0:T(8,128)(2,1)} %get-tuple-element.22.rest_0_, bf16[8,96,384]{2,1,0:T(8,128)(2,1)S(1)} %collective-permute-done.4.rest_1_, ...), custom_call_target="tpu_custom_call" | custom-call | flops 1000 | bytes 1000 | tf_op jit(solution)/shard_map/output/pallas_call | solution.py:445
  (9 shorter events, 0.1 us)
Async XLA Ops:
  1.4 9.0 %collective-permute-start.1 = (bf16[2,1536]{1,0:T(2,128)(2,1)S(1)}, bf16[2,1536]{1,0:T(2,128)(2,1)S(1)}, u32[]{:S(2)}, u32[]{:S(2)}) collective-permute-start(bf16[2,1536]{1,0:T(2,128)(2,1)S(1)} %get-tuple-element.26), channel_id=1, source_target_pairs={{0,1},{1,0},{2,3},{3,2},{4,5},{5,4},{6,7},{7,6},{8,9},{9,8},{10,11... | collective-permute-start | bytes 18440 | tf_op jit(solution)/shard_map/ppermute | solution.py:44
  2.9 7.5 %collective-permute-start = (bf16[2,1536]{1,0:T(2,128)(2,1)S(1)}, bf16[2,1536]{1,0:T(2,128)(2,1)S(1)}, u32[]{:S(2)}, u32[]{:S(2)}) collective-permute-start(bf16[2,1536]{1,0:T(2,128)(2,1)S(1)} %get-tuple-element.27), channel_id=1, source_target_pairs={{1,2},{3,4},{5,6},{7,8},{9,10},{11,12},{13,14},{17,18},{19,20},{21... | collective-permute-start | bytes 18440 | tf_op jit(solution)/shard_map/ppermute | solution.py:44
  10.5 7.4 %copy-start.2 = (f32[1536]{0:T(1024)S(1)}, f32[1536]{0:T(1024)}, u32[]{:S(2)}) copy-start(f32[1536]{0:T(1024)} %cg_ref.1) | copy-start | bytes 18436
  10.5 7.4 %copy-start.3 = (f32[1536]{0:T(1024)S(1)}, f32[1536]{0:T(1024)}, u32[]{:S(2)}) copy-start(f32[1536]{0:T(1024)} %bias_ref.1) | copy-start | bytes 18436
  10.5 7.4 %copy-start.4 = (f32[1536]{0:T(1024)S(1)}, f32[1536]{0:T(1024)}, u32[]{:S(2)}) copy-start(f32[1536]{0:T(1024)} %ag_ref.1) | copy-start | bytes 18436
  10.5 43.2 %all-to-all-start = ((bf16[8,96,1728]{2,1,0:T(8,128)(2,1)}), bf16[8,96,1728]{2,1,0:T(8,128)(2,1)}, u32[]{:S(2)}, u32[]{:S(2)}) async-start(bf16[8,96,1728]{2,1,0:T(8,128)(2,1)} %pack.1), calls=%async_computation | async-start | bytes 5505024 | tf_op jit(solution)/shard_map/all_to_all | solution.py:167
  17.9 1.4 %copy-start = (bf16[512,1536]{1,0:T(8,128)(2,1)S(1)}, bf16[512,1536]{1,0:T(8,128)(2,1)}, u32[]{:S(2)}) copy-start(bf16[512,1536]{1,0:T(8,128)(2,1)} %x_ref.1) | copy-start | bytes 4718596
  54.8 2.1 %collective-permute-start.2 = (bf16[8,96,320]{2,1,0:T(8,128)(2,1)S(1)}, bf16[8,96,320]{2,1,0:T(8,128)(2,1)S(1)}, u32[]{:S(2)}, u32[]{:S(2)}) collective-permute-start(bf16[8,96,320]{2,1,0:T(8,128)(2,1)S(1)} %slice.17), channel_id=1, source_target_pairs={{0,1},{1,0},{2,3},{3,2},{4,5},{5,4},{6,7},{7,6},{8,9},{9,8},{10,11... | collective-permute-start | bytes 1474568 | tf_op jit(solution)/shard_map/ppermute | solution.py:44
  60.5 6.8 %collective-permute-start.3 = (bf16[8,96,1024]{2,1,0:T(8,128)(2,1)}, bf16[8,96,1024]{2,1,0:T(8,128)(2,1)}, u32[]{:S(2)}, u32[]{:S(2)}) collective-permute-start(bf16[8,96,1024]{2,1,0:T(8,128)(2,1)} %get-tuple-element.20.own), channel_id=1, source_target_pairs={{0,1},{1,0},{2,3},{3,2},{4,5},{5,4},{6,7},{7,6},{8,9},{9,8},{10,11... | collective-permute-start | bytes 4718600 | tf_op jit(solution)/shard_map/ppermute | solution.py:44
  61.0 23.5 %all-to-all-start.1 = ((bf16[8,640,128]{2,1,0:T(8,128)(2,1)}), bf16[8,640,128]{2,1,0:T(8,128)(2,1)S(1)}, u32[]{:S(2)}, u32[]{:S(2)}) async-start(bf16[8,640,128]{2,1,0:T(8,128)(2,1)} %get-tuple-element.21), calls=%async_computation.1 | async-start | bytes 2621440 | tf_op jit(solution)/shard_map/all_to_all | solution.py:157
  64.6 16.3 %collective-permute-start.4 = (bf16[8,96,384]{2,1,0:T(8,128)(2,1)}, bf16[8,96,384]{2,1,0:T(8,128)(2,1)S(1)}, u32[]{:S(2)}, u32[]{:S(2)}) collective-permute-start(bf16[8,96,384]{2,1,0:T(8,128)(2,1)} %get-tuple-element.22.rest_0_), channel_id=1, source_target_pairs={{0,32},{1,33},{2,34},{3,35},{4,36},{5,37},{6,38},{7,39},{8,40},{9,... | collective-permute-start | bytes 1769480 | tf_op jit(solution)/shard_map/ppermute | solution.py:44
  65.9 15.0 %collective-permute-start.5 = (bf16[8,96,384]{2,1,0:T(8,128)(2,1)}, bf16[8,96,384]{2,1,0:T(8,128)(2,1)}, u32[]{:S(2)}, u32[]{:S(2)}) collective-permute-start(bf16[8,96,384]{2,1,0:T(8,128)(2,1)} %get-tuple-element.22.rest_0_), channel_id=1, source_target_pairs={{0,96},{1,97},{2,98},{3,99},{4,100},{5,101},{6,102},{7,103},{8,104... | collective-permute-start | bytes 1769480 | tf_op jit(solution)/shard_map/ppermute | solution.py:44
  84.5 5.7 %collective-permute-start.6 = (bf16[8,640,128]{2,1,0:T(8,128)(2,1)S(1)}, bf16[8,640,128]{2,1,0:T(8,128)(2,1)S(1)}, u32[]{:S(2)}, u32[]{:S(2)}) collective-permute-start(bf16[8,640,128]{2,1,0:T(8,128)(2,1)S(1)} %all-to-all-done.1.own), channel_id=1, source_target_pairs={{0,1},{1,0},{2,3},{3,2},{4,5},{5,4},{6,7},{7,6},{8,9},{9,8},{10,11... | collective-permute-start | bytes 3932168 | tf_op jit(solution)/shard_map/ppermute | solution.py:44
  85.6 16.0 %collective-permute-start.7 = (bf16[4,96,384]{2,1,0:T(8,128)(2,1)S(1)}, bf16[4,96,384]{2,1,0:T(8,128)(2,1)S(1)}, u32[]{:S(2)}, u32[]{:S(2)}) collective-permute-start(bf16[4,96,384]{2,1,0:T(8,128)(2,1)S(1)} %slice.20), channel_id=1, source_target_pairs={{0,32},{1,33},{2,34},{3,35},{4,36},{5,37},{6,38},{7,39},{8,40},{9,... | collective-permute-start | bytes 884744 | tf_op jit(solution)/shard_map/ppermute | solution.py:44
  86.8 15.4 %collective-permute-start.9 = (bf16[8,96,384]{2,1,0:T(8,128)(2,1)}, bf16[8,96,384]{2,1,0:T(8,128)(2,1)S(1)}, u32[]{:S(2)}, u32[]{:S(2)}) collective-permute-start(bf16[8,96,384]{2,1,0:T(8,128)(2,1)} %get-tuple-element.22.rest_0_), channel_id=1, source_target_pairs={{0,1},{1,0},{2,3},{3,2},{4,5},{5,4},{6,7},{7,6},{8,9},{9,8},{10,11... | collective-permute-start | bytes 1769480 | tf_op jit(solution)/shard_map/ppermute | solution.py:44
  88.1 15.7 %copy-start.1 = (bf16[256,1536]{1,0:T(8,128)(2,1)S(1)}, bf16[256,1536]{1,0:T(8,128)(2,1)}, u32[]{:S(2)}) copy-start(bf16[256,1536]{1,0:T(8,128)(2,1)} %get-tuple-element.12.skip_ref) | copy-start | bytes 2359300
  88.1 14.0 %collective-permute-start.8 = (bf16[4,96,384]{2,1,0:T(8,128)(2,1)S(1)}, bf16[4,96,384]{2,1,0:T(8,128)(2,1)S(1)}, u32[]{:S(2)}, u32[]{:S(2)}) collective-permute-start(bf16[4,96,384]{2,1,0:T(8,128)(2,1)S(1)} %slice.21), channel_id=1, source_target_pairs={{0,96},{1,97},{2,98},{3,99},{4,100},{5,101},{6,102},{7,103},{8,104... | collective-permute-start | bytes 884744 | tf_op jit(solution)/shard_map/ppermute | solution.py:44
  89.7 12.6 %collective-permute-start.10 = (bf16[8,96,384]{2,1,0:T(8,128)(2,1)S(1)}, bf16[8,96,384]{2,1,0:T(8,128)(2,1)S(1)}, u32[]{:S(2)}, u32[]{:S(2)}) collective-permute-start(bf16[8,96,384]{2,1,0:T(8,128)(2,1)S(1)} %collective-permute-done.4.rest_1_), channel_id=1, source_target_pairs={{0,1},{1,0},{2,3},{3,2},{4,5},{5,4},{6,7},{7,6},{8,9},{9,8},{10,11... | collective-permute-start | bytes 1769480 | tf_op jit(solution)/shard_map/ppermute | solution.py:44
  90.2 12.1 %collective-permute-start.11 = (bf16[8,96,384]{2,1,0:T(8,128)(2,1)}, bf16[8,96,384]{2,1,0:T(8,128)(2,1)S(1)}, u32[]{:S(2)}, u32[]{:S(2)}) collective-permute-start(bf16[8,96,384]{2,1,0:T(8,128)(2,1)} %collective-permute-done.5.rest_2_), channel_id=1, source_target_pairs={{0,1},{1,0},{2,3},{3,2},{4,5},{5,4},{6,7},{7,6},{8,9},{9,8},{10,11... | collective-permute-start | bytes 1769480 | tf_op jit(solution)/shard_map/ppermute | solution.py:44
  101.6 1.8 %collective-permute-start.12 = (bf16[4,96,384]{2,1,0:T(8,128)(2,1)S(1)}, bf16[4,96,384]{2,1,0:T(8,128)(2,1)S(1)}, u32[]{:S(2)}, u32[]{:S(2)}) collective-permute-start(bf16[4,96,384]{2,1,0:T(8,128)(2,1)S(1)} %collective-permute-done.7.rest_3_), channel_id=1, source_target_pairs={{0,1},{1,0},{2,3},{3,2},{4,5},{5,4},{6,7},{7,6},{8,9},{9,8},{10,11... | collective-permute-start | bytes 884744 | tf_op jit(solution)/shard_map/ppermute | solution.py:44
  102.2 1.6 %collective-permute-start.13 = (bf16[4,96,384]{2,1,0:T(8,128)(2,1)S(1)}, bf16[4,96,384]{2,1,0:T(8,128)(2,1)S(1)}, u32[]{:S(2)}, u32[]{:S(2)}) collective-permute-start(bf16[4,96,384]{2,1,0:T(8,128)(2,1)S(1)} %collective-permute-done.8.rest_4_), channel_id=1, source_target_pairs={{0,1},{1,0},{2,3},{3,2},{4,5},{5,4},{6,7},{7,6},{8,9},{9,8},{10,11... | collective-permute-start | bytes 884744 | tf_op jit(solution)/shard_map/ppermute | solution.py:44
